TPU v7x, 32 devices: a whole 2x2x4 slice. The times are simulated.
32 devices in a mesh: node: 4 (over z), cuts: 8 (over y, x, core).
Axes of the slice: x: 2, y: 2, z: 4, core: 2. Of those that a mesh axis runs over, the one named last changes fastest.
Arguments:
- core_x: bfloat16 [8, 256, 256, 256], P('node', 'cuts'), may hold values from -6 to 6
- core_y: bfloat16 [8, 256, 256, 256], P('node', 'cuts'), may hold values from -0.0234375 to 0.0234375
- left_intersection: bfloat16 [8, 256, 256], P('node', 'cuts'), may hold values from -0.375 to 0.375
- right_intersection: bfloat16 [8, 256, 256], P('node', 'cuts'), may hold values from -0.375 to 0.375
Outputs:
- parent_intersection: float32 [8, 256, 256], P('node', 'cuts')
All inputs are finite; a program needn't handle non-finite values.
Results may differ from a plain program's by a relative error of at most 0.004.
Values may be sent and summed in bfloat16 or wider, within the bound.
No kernel may reach another device: no remote copies, remote signals or barrier semaphores. Data moves between devices by JAX's collectives and lax.ppermute only.
A program may use at most 64 MiB of HBM per device.

v0:
```python
import jax
import jax.numpy as jnp
from jax import lax
from jax.sharding import PartitionSpec as P


def shards(core_x, core_y, left_intersection, right_intersection):
    left_full = lax.all_gather(left_intersection, "cuts", axis=1, tiled=True)
    first = jnp.einsum(
        "pik,paij->pakj", left_full, core_x, preferred_element_type=jnp.float32
    ).astype(jnp.bfloat16)
    right_full = lax.all_gather(right_intersection, "cuts", axis=1, tiled=True)
    moved = lax.all_to_all(
        jnp.einsum("pakj,pjl->pakl", first, right_full, preferred_element_type=jnp.float32).astype(
            jnp.bfloat16
        ),
        "cuts",
        split_axis=2,
        concat_axis=1,
        tiled=True,
    )
    mine = lax.psum_scatter(
        jnp.einsum("pakl,pklb->apb", moved, core_y, preferred_element_type=jnp.float32),
        "cuts",
        scatter_dimension=0,
        tiled=True,
    )
    return jnp.transpose(mine, (1, 0, 2))


def solution(mesh):
    return jax.shard_map(
        shards,
        mesh=mesh,
        in_specs=(
            P("node", "cuts", None, None),
            P("node", "cuts", None, None),
            P("node", "cuts", None),
            P("node", "cuts", None),
        ),
        out_specs=P("node", "cuts", None),
        check_vma=False,
    )
```

profile of v0, /device:TPU:0, one launch (start us, length us, event | category | flops | bytes accessed | tf_op | source)
XLA Modules:
  0.0 204.2 jit_solution(5130480853384822507)
XLA Ops:
  6.5 0.0 reduce-scatter.2.cloned.1.call-start
  6.5 11.0 %all_gather.6 = bf16[2,256,256]{2,1,0:T(8,128)(2,1)S(1)} all-gather(bf16[2,32,256]{2,1,0:T(8,128)(2,1)} %param.6), channel_id=1, replica_groups=mesh['node'=4,'cuts'=8] {'cuts'}, dimensions={1}, use_global_device_ids=true | all-gather | bytes 294912 | tf_op jit(solution)/shard_map/all_gather | solution.py:8
  17.5 9.1 %all_gather.7 = bf16[2,256,256]{2,1,0:T(8,128)(2,1)S(1)} all-gather(bf16[2,32,256]{2,1,0:T(8,128)(2,1)} %param.7), channel_id=1, replica_groups=mesh['node'=4,'cuts'=8] {'cuts'}, dimensions={1}, use_global_device_ids=true | all-gather | bytes 294912 | tf_op jit(solution)/shard_map/all_gather | solution.py:12
  26.6 8.9 %fusion.5 = bf16[2,32,256,256]{3,2,1,0:T(8,128)(2,1)} fusion(bf16[2,32,256,256]{3,2,1,0:T(8,128)(2,1)} %param.4, bf16[2,256,256]{2,1,0:T(8,128)(2,1)S(1)} %all_gather.7, bf16[2,256,256]{2,1,0:T(8,128)(2,1)S(1)} %all_gather.6), kind=kOutput, calls=%fused_computation.4 | convolution fusion | flops 4303355904 | bytes 17301504 | tf_op jit(solution)/shard_map/pakj,pjl->pakl/dot_general | solution.py:14
  35.5 11.4 %copy.6 = bf16[2,32,256,256]{3,1,0,2:T(8,128)(2,1)} copy(bf16[2,32,256,256]{3,2,1,0:T(8,128)(2,1)} %fusion.5) | data formatting | bytes 16777216 | tf_op jit(solution)/shard_map/convert_element_type | solution.py:14
  46.9 99.8 %all_to_all.18 = bf16[2,32,256,256]{3,1,0,2:T(8,128)(2,1)} all-to-all(bf16[2,32,256,256]{3,1,0,2:T(8,128)(2,1)} %copy.6), channel_id=1, replica_groups=mesh['node'=4,'cuts'=8] {'cuts'}, dimensions={2} | all-to-all | bytes 16777216 | tf_op jit(solution)/shard_map/all_to_all | solution.py:13
  146.7 8.0 %copy.7 = bf16[2,32,8,32,256]{4,1,2,3,0:T(8,128)(2,1)} copy(bf16[2,32,8,32,256]{4,1,0,3,2:T(8,128)(2,1)} %bitcast.29) | data formatting | bytes 16777216 | tf_op jit(solution)/shard_map/all_to_all | solution.py:13
  154.7 8.9 %convolution_bitcast_fusion = f32[256,2,256]{2,0,1:T(8,128)} fusion(bf16[2,256,32,256]{3,1,2,0:T(8,128)(2,1)} %bitcast.30, bf16[2,32,256,256]{3,2,1,0:T(8,128)(2,1)} %param.5), kind=kOutput, calls=%fused_computation.5 | convolution fusion | flops 2147483648 | bytes 17301504 | tf_op jit(solution)/shard_map/pakl,pklb->apb/dot_general | solution.py:23
  163.6 0.0 reduce-scatter.2.cloned.1.call-update
  163.7 33.7 %reduce-scatter.2.cloned.1.call-done = f32[32,2,256]{2,0,1:T(8,128)} async-done(((f32[256,2,256]{2,0,1:T(8,128)}), f32[32,2,256]{2,0,1:T(8,128)}) %reduce-scatter.2.cloned.1.call-update) | async-done | bytes 65552 | tf_op jit(solution)/shard_map/reduce_scatter | solution.py:22
Async XLA Ops:
  6.5 190.8 %reduce-scatter.2.cloned.1.call-start = ((), (), s32[]{:S(2)}) async-start(), calls=%async_computation.2 | async-start | bytes 589824 | tf_op jit(solution)/shard_map/reduce_scatter | solution.py:22
Sparse Core Ops, SparseCore 0:
  163.8 33.4 reduce-scatter.1
where the time goes:
time: 205 us; the launch traced here: 204 us
  blocking collectives  120 us (59%)
  waiting for transfers between devices  33.7 us (16%)
  local copies, waits for them, and re-layouts  19.4 us (9%)
  matrix products  17.9 us (9%)
  between operations  13.4 us (7%)
    all_to_all x1, blocking collectives, shards(): lax.all_to_all(jnp.einsum('pakj,pjl->pakl', first, right_full, preferred_...  99.8 us
    reduce_scatter x1, waiting for transfers between devices, shards(): lax.psum_scatter(jnp.einsum('pakl,pklb->apb', moved, core_y, preferred_el...  33.7 us
    convert_element_type x1, local copies, waits for them, and re-layouts, shards(): jnp.einsum('pakj,pjl->pakl', first, right_full, preferred_element_type=jn...  11.4 us
    all_gather x1, blocking collectives, shards(): left_full = lax.all_gather(left_intersection, 'cuts', axis=1, tiled=True)  11 us
    all_gather x1, blocking collectives, shards(): right_full = lax.all_gather(right_intersection, 'cuts', axis=1, tiled=True)  9.07 us
    dot_general x1, matrix products, shards(): jnp.einsum('pakj,pjl->pakl', first, right_full, preferred_element_type=jn...  8.95 us
    dot_general x1, matrix products, shards(): jnp.einsum('pakl,pklb->apb', moved, core_y, preferred_element_type=jnp.fl...  8.94 us
    all_to_all x1, local copies, waits for them, and re-layouts, shards(): lax.all_to_all(jnp.einsum('pakj,pjl->pakl', first, right_full, preferred_...  8.05 us
  transfers between devices with their start and end apart: 1, of which 1 were waited for; matrix products, arithmetic and copies ran while one was open for 0% of the time, Pallas kernels for 0%

commit v1 on v0

v1 whole, which is shorter than its diff:
```python
import functools

import jax
import jax.numpy as jnp
from jax import lax
from jax.experimental import pallas as pl
from jax.experimental.pallas import tpu as pltpu
from jax.sharding import PartitionSpec as P

AXIS = "cuts"
LIMIT = 48 * 1024 * 1024
LANES = 128


def plain(core_x, core_y, left_intersection, right_intersection):
    left_full = lax.all_gather(left_intersection, AXIS, axis=1, tiled=True)
    first = jnp.einsum(
        "pik,paij->pakj", left_full, core_x, preferred_element_type=jnp.float32
    ).astype(jnp.bfloat16)
    right_full = lax.all_gather(right_intersection, AXIS, axis=1, tiled=True)
    moved = lax.all_to_all(
        jnp.einsum("pakj,pjl->pakl", first, right_full, preferred_element_type=jnp.float32).astype(
            jnp.bfloat16
        ),
        AXIS,
        split_axis=2,
        concat_axis=1,
        tiled=True,
    )
    mine = lax.psum_scatter(
        jnp.einsum("pakl,pklb->apb", moved, core_y, preferred_element_type=jnp.float32),
        AXIS,
        scatter_dimension=0,
        tiled=True,
    )
    return jnp.transpose(mine, (1, 0, 2))


def swap(value, mask, n):
    return lax.ppermute(value, AXIS, [(i, i ^ mask) for i in range(n)])


def gather_rows(value, n):
    rows = [None] * n
    rows[0] = value
    for mask in range(n - 2, 0, -2):
        rows[mask] = swap(value, mask, n)
    for mask in range(0, n, 2):
        rows[mask + 1] = swap(rows[mask], 1, n)
    return rows


def first_kernel(n, masks, me_ref, *refs):
    pieces, x_ref = refs[:n], refs[n]
    outs, (full, turned, chosen) = refs[n + 1 : n + 1 + len(masks)], refs[n + 1 + len(masks) :]
    rows = pieces[0].shape[1]
    me = me_ref[0]

    @pl.when(pl.program_id(1) == 0)
    def _():
        for m in range(n):
            full[pl.ds(pl.multiple_of((me ^ m) * rows, rows), rows), :] = pieces[m][0]
        turned[...] = full[...].T
        for slot, m in enumerate(masks):
            chosen[slot * rows : (slot + 1) * rows, :] = turned[
                pl.ds(pl.multiple_of((me ^ m) * rows, rows), rows), :
            ]

    for a in range(x_ref.shape[1]):
        product = jnp.dot(chosen[...], x_ref[0, a], preferred_element_type=jnp.float32).astype(jnp.bfloat16)
        for slot, out in enumerate(outs):
            out[0, a] = product[slot * rows : (slot + 1) * rows, :]


def first_for(me, pieces, core_x, masks):
    n = len(pieces)
    parents, mine, left, right = core_x.shape
    rows = pieces[0].shape[1]
    step = min(8, mine)
    spec = pl.BlockSpec((1, rows, left), lambda p, c: (p, 0, 0))
    return pl.pallas_call(
        functools.partial(first_kernel, n, masks),
        grid=(parents, mine // step),
        in_specs=[pl.BlockSpec(memory_space=pltpu.SMEM)]
        + [spec] * n
        + [pl.BlockSpec((1, step, left, right), lambda p, c: (p, c, 0, 0))],
        out_specs=[pl.BlockSpec((1, step, rows, right), lambda p, c: (p, c, 0, 0))] * len(masks),
        out_shape=[jax.ShapeDtypeStruct((parents, mine, rows, right), jnp.bfloat16)] * len(masks),
        scratch_shapes=[
            pltpu.VMEM((left, left), jnp.bfloat16),
            pltpu.VMEM((left, left), jnp.bfloat16),
            pltpu.VMEM((rows * len(masks), left), jnp.bfloat16),
        ],
        compiler_params=pltpu.CompilerParams(vmem_limit_bytes=LIMIT),
        cost_estimate=pl.CostEstimate(
            flops=2 * parents * mine * rows * len(masks) * left * right,
            bytes_accessed=2 * parents * mine * right * (left + rows * len(masks)),
            transcendentals=0,
        ),
        name="first",
    )(me, *pieces, core_x)


def join_kernel(n, me_ref, *refs):
    pieces, out = refs[:n], refs[n]
    rows = pieces[0].shape[1]
    for m in range(n):
        at = pl.ds(pl.multiple_of((me_ref[0] ^ m) * rows, rows), rows)
        out[:, at, :] = pieces[m][...]


def join(me, pieces):
    n = len(pieces)
    parents, rows, width = pieces[0].shape
    return pl.pallas_call(
        functools.partial(join_kernel, n),
        in_specs=[pl.BlockSpec(memory_space=pltpu.SMEM)] + [pl.BlockSpec(memory_space=pltpu.VMEM)] * n,
        out_specs=pl.BlockSpec(memory_space=pltpu.VMEM),
        out_shape=jax.ShapeDtypeStruct((parents, n * rows, width), pieces[0].dtype),
        cost_estimate=pl.CostEstimate(flops=0, bytes_accessed=4 * parents * n * rows * width, transcendentals=0),
        name="join",
    )(me, *pieces)


def last_kernel(held, first_ref, right_ref, y_ref, *refs):
    out_ref, second, flat = refs[-3:]
    count, rows = first_ref.shape[1], first_ref.shape[2]
    width = right_ref.shape[2]
    c = pl.program_id(1)

    @pl.when(c == 0)
    def _():
        whole = jnp.dot(
            first_ref[0].reshape(count * rows, first_ref.shape[3]),
            right_ref[0],
            preferred_element_type=jnp.float32,
        )
        for h in range(width // LANES):
            second[h] = whole[:, h * LANES : (h + 1) * LANES]
        for k in range(rows):
            for h in range(width // LANES):
                flat[:, k * width + h * LANES : k * width + (h + 1) * LANES] = second[
                    h, pl.ds(k, count, stride=rows), :
                ].astype(jnp.bfloat16)
        if held:
            out_ref[...] = refs[0][...]
        else:
            out_ref[...] = jnp.zeros_like(out_ref)

    depth = y_ref.shape[1] * width
    out_ref[0] += jnp.dot(
        flat[:, pl.ds(pl.multiple_of(c * depth, depth), depth)],
        y_ref[0].reshape(depth, y_ref.shape[3]),
        preferred_element_type=jnp.float32,
    )


def last_for(first, right_full, core_y, begin=None):
    parents, count, rows, depth = first.shape
    width, out_width = right_full.shape[2], core_y.shape[3]
    step = min(8, rows)
    spec = pl.BlockSpec((1, count, out_width), lambda p, c: (p, 0, 0))
    return pl.pallas_call(
        functools.partial(last_kernel, begin is not None),
        grid=(parents, rows // step),
        in_specs=[
            pl.BlockSpec((1, count, rows, depth), lambda p, c: (p, 0, 0, 0)),
            pl.BlockSpec((1, depth, width), lambda p, c: (p, 0, 0)),
            pl.BlockSpec((1, step, width, out_width), lambda p, c: (p, c, 0, 0)),
        ]
        + [spec] * (begin is not None),
        out_specs=spec,
        out_shape=jax.ShapeDtypeStruct((parents, count, out_width), jnp.float32),
        scratch_shapes=[
            pltpu.VMEM((width // LANES, count * rows, LANES), jnp.float32),
            pltpu.VMEM((count, rows * width), jnp.bfloat16),
        ],
        compiler_params=pltpu.CompilerParams(vmem_limit_bytes=LIMIT),
        cost_estimate=pl.CostEstimate(
            flops=2 * parents * count * rows * width * (depth + out_width),
            bytes_accessed=2 * parents * rows * width * (count + out_width),
            transcendentals=0,
        ),
        name="last",
    )(first, right_full, core_y, *([] if begin is None else [begin]))


def exchanged(core_x, core_y, left_intersection, right_intersection, n):
    me = lax.axis_index(AXIS).astype(jnp.int32).reshape(1)
    pairs = list(range(2, n, 2))
    left = gather_rows(left_intersection, n)
    early = [mask + 1 for mask in pairs[:2]]
    late = [mask for mask in range(n) if mask not in early]
    sent = dict(zip(early, first_for(me, left, core_x, early)))
    came = {mask: swap(sent[mask], mask, n) for mask in early}
    sent.update(zip(late, first_for(me, left, core_x, late)))
    for mask in [m for m in pairs[:2]] + [m + 1 for m in pairs[2:]] + pairs[2:] + [1]:
        came[mask] = swap(sent[mask], mask, n)
    came[0] = sent[0]
    right = join(me, gather_rows(right_intersection, n))
    total = []
    for mask in pairs + [0]:
        odd = last_for(came[mask + 1], right, core_y)
        part = last_for(came[mask], right, core_y, swap(odd, 1, n))
        total.append(swap(part, mask, n) if mask else part)
    return sum(total[1:], total[0])


def solution(mesh):
    n = mesh.shape[AXIS]

    def shards(core_x, core_y, left_intersection, right_intersection):
        rows = left_intersection.shape[1]
        fits = n >= 4 and n & (n - 1) == 0 and rows % 16 == 0 and core_x.shape[1] % 8 == 0 and core_x.shape[3] % LANES == 0
        if not fits:
            return plain(core_x, core_y, left_intersection, right_intersection)
        return exchanged(core_x, core_y, left_intersection, right_intersection, n)

    return jax.shard_map(
        shards,
        mesh=mesh,
        in_specs=(
            P("node", AXIS, None, None),
            P("node", AXIS, None, None),
            P("node", AXIS, None),
            P("node", AXIS, None),
        ),
        out_specs=P("node", AXIS, None),
        check_vma=False,
    )
```

time: 205 us -> 150 us (0.73)
  blocking collectives: 120 us -> 0 us
  Pallas kernels: 0 us -> 89.7 us
  matrix products: 17.9 us -> 0 us
  starting transfers between devices: 0.01 us -> 17.9 us
  local copies, waits for them, and re-layouts: 19.4 us -> 1.74 us
  between operations: 13.4 us -> 0.21 us
  waiting for transfers between devices: 33.7 us -> 38.1 us
    all_to_all x1 -> x0, blocking collectives: 99.8 us -> none  [shards(): lax.all_to_all(jnp.einsum('pakj,pjl->pakl', first, right_full, preferred_...]
    pallas_call x0 -> x11, Pallas kernels: none -> 89.7 us  [the longest x8 71.1 us: last_for(): pl.pallas_call(functools.partial(last_kernel, begin is not None), grid=(p...]
    ppermute x0 -> x28, waiting for transfers between devices: none -> 38.1 us  [swap(): return lax.ppermute(value, AXIS, [(i, i ^ mask) for i in range(n)])]
    reduce_scatter x1 -> x0, waiting for transfers between devices: 33.7 us -> none  [shards(): lax.psum_scatter(jnp.einsum('pakl,pklb->apb', moved, core_y, preferred_el...]
    all_gather x2 -> x0, blocking collectives: 20 us -> none  [the longest x1 11 us: shards(): left_full = lax.all_gather(left_intersection, 'cuts', axis=1, tiled=True)]
    dot_general x2 -> x0, matrix products: 17.9 us -> none  [the longest x1 8.95 us: shards(): jnp.einsum('pakj,pjl->pakl', first, right_full, preferred_element_type=jn...]
    ppermute x0 -> x28, starting transfers between devices: none -> 17.9 us  [swap(): return lax.ppermute(value, AXIS, [(i, i ^ mask) for i in range(n)])]
    convert_element_type x1 -> x0, local copies, waits for them, and re-layouts: 11.4 us -> none  [shards(): jnp.einsum('pakj,pjl->pakl', first, right_full, preferred_element_type=jn...]
  transfers between devices with their start and end apart: 1 -> 28, of which waited for: 1 -> 12; matrix products, arithmetic and copies ran while one was open for 0% -> 0% of each run, Pallas kernels for 0% -> 55%
where the time goes in v1:
time: 150 us; the launch traced here: 148 us
  Pallas kernels  89.7 us (60%)
  waiting for transfers between devices  38.1 us (25%)
  starting transfers between devices  17.9 us (12%)
  local copies, waits for them, and re-layouts  1.74 us (1%)
    pallas_call x8, Pallas kernels, last_for(): pl.pallas_call(functools.partial(last_kernel, begin is not None), grid=(p...  71.1 us
    ppermute x28, waiting for transfers between devices, swap(): return lax.ppermute(value, AXIS, [(i, i ^ mask) for i in range(n)])  38.1 us
    ppermute x28, starting transfers between devices, swap(): return lax.ppermute(value, AXIS, [(i, i ^ mask) for i in range(n)])  17.9 us
    pallas_call x2, Pallas kernels, first_for(): pl.pallas_call(functools.partial(first_kernel, n, masks), grid=(parents,...  17 us
  transfers between devices with their start and end apart: 28, of which 12 were waited for; matrix products, arithmetic and copies ran while one was open for 0% of the time, Pallas kernels for 55%

profile of v1, /device:TPU:0, one launch (start us, length us, event | category | flops | bytes accessed | tf_op | source)
XLA Modules:
  0.0 148.3 jit_solution(8324961415374988792)
XLA Ops:
  0.0 2.9 %collective-permute-start.1 = (bf16[2,32,256]{2,1,0:T(8,128)(2,1)}, bf16[2,32,256]{2,1,0:T(8,128)(2,1)S(1)}, u32[]{:S(2)}, u32[]{:S(2)}) collective-permute-start(bf16[2,32,256]{2,1,0:T(8,128)(2,1)} %refs_0_.5), channel_id=1, source_target_pairs={{0,2},{1,3},{2,0},{3,1},{4,6},{5,7},{6,4},{7,5},{8,10},{9,11},{10,... | collective-permute-start | bytes 98312 | tf_op jit(solution)/shard_map/ppermute | solution.py:40
  2.9 1.5 %collective-permute-start.3 = (bf16[2,32,256]{2,1,0:T(8,128)(2,1)}, bf16[2,32,256]{2,1,0:T(8,128)(2,1)S(1)}, u32[]{:S(2)}, u32[]{:S(2)}) collective-permute-start(bf16[2,32,256]{2,1,0:T(8,128)(2,1)} %refs_0_.5), channel_id=1, source_target_pairs={{0,4},{1,5},{2,6},{3,7},{4,0},{5,1},{6,2},{7,3},{8,12},{9,13},{10,... | collective-permute-start | bytes 98312 | tf_op jit(solution)/shard_map/ppermute | solution.py:40
  4.5 0.6 collective-permute-done.1.refs_2_
  5.0 0.0 collective-permute-start.2
  5.0 2.0 %collective-permute-done.3.refs_4_ = bf16[2,32,256]{2,1,0:T(8,128)(2,1)S(1)} collective-permute-done((bf16[2,32,256]{2,1,0:T(8,128)(2,1)}, bf16[2,32,256]{2,1,0:T(8,128)(2,1)S(1)}, u32[]{:S(2)}, u32[]{:S(2)}) %collective-permute-start.3) | collective-permute-done | bytes 32800 | tf_op jit(solution)/shard_map/ppermute | solution.py:40
  7.1 0.0 collective-permute-start.4
  7.1 2.4 %collective-permute-done.5.refs_6_ = bf16[2,32,256]{2,1,0:T(8,128)(2,1)S(1)} collective-permute-done((bf16[2,32,256]{2,1,0:T(8,128)(2,1)}, bf16[2,32,256]{2,1,0:T(8,128)(2,1)S(1)}, u32[]{:S(2)}, u32[]{:S(2)}) %collective-permute-start.5) | collective-permute-done | bytes 32800 | tf_op jit(solution)/shard_map/ppermute | solution.py:40
  9.5 1.2 collective-permute-done.6.refs_7_
  10.7 0.8 copy-done.2
  11.5 8.8 %first.2 = (bf16[2,32,32,256]{3,2,1,0:T(8,128)(2,1)S(1)}, bf16[2,32,32,256]{3,2,1,0:T(8,128)(2,1)S(1)}, bf16[2,32,32,256]{3,2,1,0:T(8,128)(2,1)}, bf16[2,32,32,2...) custom-call(s32[1]{0:T(128)} %bitcast.me_ref, ...), custom_call_target="tpu_custom_call" | custom-call | flops 1610612736 | bytes 14680064 | tf_op jit(solution)/shard_map/first/pallas_call | solution.py:81
  20.3 0.2 collective-permute-start.26
  20.5 1.9 %collective-permute-start.9 = (bf16[2,32,256]{2,1,0:T(8,128)(2,1)S(1)}, bf16[2,32,256]{2,1,0:T(8,128)(2,1)S(1)}, u32[]{:S(2)}, u32[]{:S(2)}) collective-permute-start(bf16[2,32,256]{2,1,0:T(8,128)(2,1)S(1)} %copy-done.3), channel_id=1, source_target_pairs={{0,2},{1,3},{2,0},{3,1},{4,6},{5,7},{6,4},{7,5},{8,10},{9,11},{10,... | collective-permute-start | bytes 98312 | tf_op jit(solution)/shard_map/ppermute | solution.py:40
  22.4 1.5 %collective-permute-start.11 = (bf16[2,32,256]{2,1,0:T(8,128)(2,1)S(1)}, bf16[2,32,256]{2,1,0:T(8,128)(2,1)S(1)}, u32[]{:S(2)}, u32[]{:S(2)}) collective-permute-start(bf16[2,32,256]{2,1,0:T(8,128)(2,1)S(1)} %copy-done.3), channel_id=1, source_target_pairs={{0,4},{1,5},{2,6},{3,7},{4,0},{5,1},{6,2},{7,3},{8,12},{9,13},{10,... | collective-permute-start | bytes 98312 | tf_op jit(solution)/shard_map/ppermute | solution.py:40
  23.9 0.1 collective-permute-start.13
  24.0 8.2 %first.3 = (bf16[2,32,32,256]{3,2,1,0:T(8,128)(2,1)}, bf16[2,32,32,256]{3,2,1,0:T(8,128)(2,1)}) custom-call(s32[1]{0:T(128)} %bitcast.me_ref, bf16[2,32,256]{2,1,0:T(8,128)(2,1)S(1)} %copy-done.2, bf16[2,32,256]{2,1,0:T(8,128)(2,1)S(1)} %collective-permute-done.refs_1_, bf16[2,32,256]{2,1,0:T(8,128)(2,1)S(1)} %collective-permute-done.1.refs_2_, ...), custom_call_target="tpu_custom_call" | custom-call | flops 536870912 | bytes 10485760 | tf_op jit(solution)/shard_map/first/pallas_call | solution.py:81
  32.2 14.7 %collective-permute-done.9.refs_2_ = bf16[2,32,256]{2,1,0:T(8,128)(2,1)S(1)} collective-permute-done((bf16[2,32,256]{2,1,0:T(8,128)(2,1)S(1)}, bf16[2,32,256]{2,1,0:T(8,128)(2,1)S(1)}, u32[]{:S(2)}, u32[]{:S(2)}) %collective-permute-start.9) | collective-permute-done | bytes 32800 | tf_op jit(solution)/shard_map/ppermute | solution.py:40
  46.9 0.9 collective-permute-done.11.refs_4_
  47.8 0.5 collective-permute-done.13.refs_6_
  48.3 0.7 collective-permute-done.8.refs_1_
  49.0 0.2 collective-permute-start.12
  49.2 0.4 collective-permute-done.10.refs_3_
  49.5 0.6 collective-permute-start.19
  50.2 0.0 collective-permute-done.12.refs_5_
  50.2 0.3 collective-permute-start.14
  50.5 0.9 collective-permute-done.14.refs_7_
  51.4 1.9 %collective-permute-start.22 = (bf16[2,32,32,256]{3,2,1,0:T(8,128)(2,1)}, bf16[2,32,32,256]{3,2,1,0:T(8,128)(2,1)}, u32[]{:S(2)}, u32[]{:S(2)}) collective-permute-start(bf16[2,32,32,256]{3,2,1,0:T(8,128)(2,1)} %get-tuple-element.17), channel_id=1, source_target_pairs={{0,6},{1,7},{2,4},{3,5},{4,2},{5,3},{6,0},{7,1},{8,14},{9,15},{10,... | collective-permute-start | bytes 3145736 | tf_op jit(solution)/shard_map/ppermute | solution.py:40
  53.3 0.7 collective-permute-start.7
  54.0 0.9 collective-permute-start.18
  55.0 1.6 %join.1.right_ref = bf16[2,256,256]{2,1,0:T(8,128)(2,1)} custom-call(s32[1]{0:T(128)} %bitcast.me_ref, bf16[2,32,256]{2,1,0:T(8,128)(2,1)} %refs_0_.4, bf16[2,32,256]{2,1,0:T(8,128)(2,1)} %copy-done.7, bf16[2,32,256]{2,1,0:T(8,128)(2,1)} %copy-done.4, bf16[2,32,256]{2,1,0:T(8,128)(2,1)} %copy-done.8, bf16[2,32,256]{2,1,0:T(8,128)(2,1)} %copy-done.5, ...), custom_call_target="tpu_custom_call" | custom-call | bytes 524288 | tf_op jit(solution)/shard_map/join/pallas_call | solution.py:115
  56.6 0.9 copy-done
  57.5 8.7 %last.12 = f32[2,32,256]{2,1,0:T(8,128)S(1)} custom-call(bf16[2,32,32,256]{3,2,1,0:T(8,128)(2,1)S(1)} %collective-permute-done.23.first_ref, bf16[2,256,256]{2,1,0:T(8,128)(2,1)S(1)} %copy-done, bf16[2,32,256,256]{3,2,1,0:T(8,128)(2,1)} %y_ref.15), custom_call_target="tpu_custom_call" | custom-call | flops 536870912 | bytes 9437184 | tf_op jit(solution)/shard_map/last/pallas_call | solution.py:163
  66.2 8.7 %last.14 = f32[2,32,256]{2,1,0:T(8,128)S(1)} custom-call(bf16[2,32,32,256]{3,2,1,0:T(8,128)(2,1)S(1)} %collective-permute-done.26.first_ref, bf16[2,256,256]{2,1,0:T(8,128)(2,1)S(1)} %copy-done, bf16[2,32,256,256]{3,2,1,0:T(8,128)(2,1)} %y_ref.15), custom_call_target="tpu_custom_call" | custom-call | flops 536870912 | bytes 9437184 | tf_op jit(solution)/shard_map/last/pallas_call | solution.py:163
  74.9 0.1 collective-permute-start.24
  75.0 9.0 %last.8 = f32[2,32,256]{2,1,0:T(8,128)S(1)} custom-call(bf16[2,32,32,256]{3,2,1,0:T(8,128)(2,1)} %collective-permute-done.15.first_ref, bf16[2,256,256]{2,1,0:T(8,128)(2,1)S(1)} %copy-done, bf16[2,32,256,256]{3,2,1,0:T(8,128)(2,1)} %y_ref.15), custom_call_target="tpu_custom_call" | custom-call | flops 536870912 | bytes 9437184 | tf_op jit(solution)/shard_map/last/pallas_call | solution.py:163
  84.0 13.4 %collective-permute-done.19.first_ref = bf16[2,32,32,256]{3,2,1,0:T(8,128)(2,1)} collective-permute-done((bf16[2,32,32,256]{3,2,1,0:T(8,128)(2,1)}, bf16[2,32,32,256]{3,2,1,0:T(8,128)(2,1)}, u32[]{:S(2)}, u32[]{:S(2)}) %collective-permute-start.19) | collective-permute-done | bytes 1048608 | tf_op jit(solution)/shard_map/ppermute | solution.py:40
  97.4 0.8 collective-permute-start.16
  98.2 9.0 %last.10 = f32[2,32,256]{2,1,0:T(8,128)S(1)} custom-call(bf16[2,32,32,256]{3,2,1,0:T(8,128)(2,1)} %collective-permute-done.19.first_ref, bf16[2,256,256]{2,1,0:T(8,128)(2,1)S(1)} %copy-done, bf16[2,32,256,256]{3,2,1,0:T(8,128)(2,1)} %y_ref.15), custom_call_target="tpu_custom_call" | custom-call | flops 536870912 | bytes 9437184 | tf_op jit(solution)/shard_map/last/pallas_call | solution.py:163
  107.3 0.1 collective-permute-start.27
  107.3 0.5 collective-permute-start.20
  107.8 9.0 %last.13 = f32[2,32,256]{2,1,0:T(8,128)S(1)} custom-call(bf16[2,32,32,256]{3,2,1,0:T(8,128)(2,1)} %collective-permute-done.22.first_ref, bf16[2,256,256]{2,1,0:T(8,128)(2,1)S(1)} %copy-done, bf16[2,32,256,256]{3,2,1,0:T(8,128)(2,1)} %y_ref.15, f32[2,32,256]{2,1,0:T(8,128)S(1)} %collective-permute-done.24.refs_0_), custom_call_target="tpu_custom_call" | custom-call | flops 536870912 | bytes 9437184 | tf_op jit(solution)/shard_map/last/pallas_call | solution.py:163
  116.9 0.4 collective-permute-done.7.first_ref
  117.2 1.9 %collective-permute-start.25 = (f32[2,32,256]{2,1,0:T(8,128)S(1)}, f32[2,32,256]{2,1,0:T(8,128)S(1)}, u32[]{:S(2)}, u32[]{:S(2)}) collective-permute-start(f32[2,32,256]{2,1,0:T(8,128)S(1)} %last.13), channel_id=1, source_target_pairs={{0,6},{1,7},{2,4},{3,5},{4,2},{5,3},{6,0},{7,1},{8,14},{9,15},{10,... | collective-permute-start | bytes 196616 | tf_op jit(solution)/shard_map/ppermute | solution.py:40
  119.2 9.0 %last.9 = f32[2,32,256]{2,1,0:T(8,128)S(1)} custom-call(bf16[2,32,32,256]{3,2,1,0:T(8,128)(2,1)} %collective-permute-done.7.first_ref, bf16[2,256,256]{2,1,0:T(8,128)(2,1)S(1)} %copy-done, bf16[2,32,256,256]{3,2,1,0:T(8,128)(2,1)} %y_ref.15, f32[2,32,256]{2,1,0:T(8,128)S(1)} %collective-permute-done.16.refs_0_), custom_call_target="tpu_custom_call" | custom-call | flops 536870912 | bytes 9437184 | tf_op jit(solution)/shard_map/last/pallas_call | solution.py:163
  128.2 1.1 collective-permute-start.17
  129.3 9.0 %last.11 = f32[2,32,256]{2,1,0:T(8,128)S(1)} custom-call(bf16[2,32,32,256]{3,2,1,0:T(8,128)(2,1)} %collective-permute-done.18.first_ref, bf16[2,256,256]{2,1,0:T(8,128)(2,1)S(1)} %copy-done, bf16[2,32,256,256]{3,2,1,0:T(8,128)(2,1)} %y_ref.15, f32[2,32,256]{2,1,0:T(8,128)S(1)} %collective-permute-done.20.refs_0_), custom_call_target="tpu_custom_call" | custom-call | flops 536870912 | bytes 9437184 | tf_op jit(solution)/shard_map/last/pallas_call | solution.py:163
  138.3 0.6 collective-permute-start.21
  138.9 8.7 %last.15 = f32[2,32,256]{2,1,0:T(8,128)S(1)} custom-call(bf16[2,32,32,256]{3,2,1,0:T(8,128)(2,1)S(1)} %get-tuple-element.19.first_ref, bf16[2,256,256]{2,1,0:T(8,128)(2,1)S(1)} %copy-done.1, bf16[2,32,256,256]{3,2,1,0:T(8,128)(2,1)} %y_ref.15, f32[2,32,256]{2,1,0:T(8,128)S(1)} %collective-permute-done.27.refs_0_), custom_call_target="tpu_custom_call" | custom-call | flops 536870912 | bytes 9437184 | tf_op jit(solution)/shard_map/last/pallas_call | solution.py:163
  147.6 0.6 add_add_fusion
  (42 shorter events, 0.1 us)
Async XLA Ops:
  0.0 5.0 %collective-permute-start.1 = (bf16[2,32,256]{2,1,0:T(8,128)(2,1)}, bf16[2,32,256]{2,1,0:T(8,128)(2,1)S(1)}, u32[]{:S(2)}, u32[]{:S(2)}) collective-permute-start(bf16[2,32,256]{2,1,0:T(8,128)(2,1)} %refs_0_.5), channel_id=1, source_target_pairs={{0,2},{1,3},{2,0},{3,1},{4,6},{5,7},{6,4},{7,5},{8,10},{9,11},{10,... | collective-permute-start | bytes 98312 | tf_op jit(solution)/shard_map/ppermute | solution.py:40
  2.9 4.1 %collective-permute-start.3 = (bf16[2,32,256]{2,1,0:T(8,128)(2,1)}, bf16[2,32,256]{2,1,0:T(8,128)(2,1)S(1)}, u32[]{:S(2)}, u32[]{:S(2)}) collective-permute-start(bf16[2,32,256]{2,1,0:T(8,128)(2,1)} %refs_0_.5), channel_id=1, source_target_pairs={{0,4},{1,5},{2,6},{3,7},{4,0},{5,1},{6,2},{7,3},{8,12},{9,13},{10,... | collective-permute-start | bytes 98312 | tf_op jit(solution)/shard_map/ppermute | solution.py:40
  4.5 5.0 %collective-permute-start.5 = (bf16[2,32,256]{2,1,0:T(8,128)(2,1)}, bf16[2,32,256]{2,1,0:T(8,128)(2,1)S(1)}, u32[]{:S(2)}, u32[]{:S(2)}) collective-permute-start(bf16[2,32,256]{2,1,0:T(8,128)(2,1)} %refs_0_.5), channel_id=1, source_target_pairs={{0,6},{1,7},{2,4},{3,5},{4,2},{5,3},{6,0},{7,1},{8,14},{9,15},{10,... | collective-permute-start | bytes 98312 | tf_op jit(solution)/shard_map/ppermute | solution.py:40
  4.5 5.0 %collective-permute-start = (bf16[2,32,256]{2,1,0:T(8,128)(2,1)}, bf16[2,32,256]{2,1,0:T(8,128)(2,1)S(1)}, u32[]{:S(2)}, u32[]{:S(2)}) collective-permute-start(bf16[2,32,256]{2,1,0:T(8,128)(2,1)} %refs_0_.5), channel_id=1, source_target_pairs={{0,1},{1,0},{2,3},{3,2},{4,5},{5,4},{6,7},{7,6},{8,9},{9,8},{10,11... | collective-permute-start | bytes 98312 | tf_op jit(solution)/shard_map/ppermute | solution.py:40
  5.0 4.5 %collective-permute-start.2 = (bf16[2,32,256]{2,1,0:T(8,128)(2,1)S(1)}, bf16[2,32,256]{2,1,0:T(8,128)(2,1)S(1)}, u32[]{:S(2)}, u32[]{:S(2)}) collective-permute-start(bf16[2,32,256]{2,1,0:T(8,128)(2,1)S(1)} %collective-permute-done.1.refs_2_), channel_id=1, source_target_pairs={{0,1},{1,0},{2,3},{3,2},{4,5},{5,4},{6,7},{7,6},{8,9},{9,8},{10,11... | collective-permute-start | bytes 98312 | tf_op jit(solution)/shard_map/ppermute | solution.py:40
  7.1 2.4 %collective-permute-start.4 = (bf16[2,32,256]{2,1,0:T(8,128)(2,1)S(1)}, bf16[2,32,256]{2,1,0:T(8,128)(2,1)S(1)}, u32[]{:S(2)}, u32[]{:S(2)}) collective-permute-start(bf16[2,32,256]{2,1,0:T(8,128)(2,1)S(1)} %collective-permute-done.3.refs_4_), channel_id=1, source_target_pairs={{0,1},{1,0},{2,3},{3,2},{4,5},{5,4},{6,7},{7,6},{8,9},{9,8},{10,11... | collective-permute-start | bytes 98312 | tf_op jit(solution)/shard_map/ppermute | solution.py:40
  9.5 1.2 collective-permute-start.6
  10.7 0.8 copy-start.2
  11.5 9.1 %copy-start.3 = (bf16[2,32,256]{2,1,0:T(8,128)(2,1)S(1)}, bf16[2,32,256]{2,1,0:T(8,128)(2,1)}, u32[]{:S(2)}) copy-start(bf16[2,32,256]{2,1,0:T(8,128)(2,1)} %refs_0_.4) | copy-start | bytes 98308
  20.3 33.0 %collective-permute-start.23 = (bf16[2,32,32,256]{3,2,1,0:T(8,128)(2,1)}, bf16[2,32,32,256]{3,2,1,0:T(8,128)(2,1)S(1)}, u32[]{:S(2)}, u32[]{:S(2)}) collective-permute-start(bf16[2,32,32,256]{3,2,1,0:T(8,128)(2,1)} %get-tuple-element.18), channel_id=1, source_target_pairs={{0,7},{1,6},{2,5},{3,4},{4,3},{5,2},{6,1},{7,0},{8,15},{9,14},{10,... | collective-permute-start | bytes 3145736 | tf_op jit(solution)/shard_map/ppermute | solution.py:40
  20.3 33.7 %collective-permute-start.26 = (bf16[2,32,32,256]{3,2,1,0:T(8,128)(2,1)S(1)}, bf16[2,32,32,256]{3,2,1,0:T(8,128)(2,1)S(1)}, u32[]{:S(2)}, u32[]{:S(2)}) collective-permute-start(bf16[2,32,32,256]{3,2,1,0:T(8,128)(2,1)S(1)} %get-tuple-element.20), channel_id=1, source_target_pairs={{0,1},{1,0},{2,3},{3,2},{4,5},{5,4},{6,7},{7,6},{8,9},{9,8},{10,11... | collective-permute-start | bytes 3145736 | tf_op jit(solution)/shard_map/ppermute | solution.py:40
  20.5 26.4 %collective-permute-start.9 = (bf16[2,32,256]{2,1,0:T(8,128)(2,1)S(1)}, bf16[2,32,256]{2,1,0:T(8,128)(2,1)S(1)}, u32[]{:S(2)}, u32[]{:S(2)}) collective-permute-start(bf16[2,32,256]{2,1,0:T(8,128)(2,1)S(1)} %copy-done.3), channel_id=1, source_target_pairs={{0,2},{1,3},{2,0},{3,1},{4,6},{5,7},{6,4},{7,5},{8,10},{9,11},{10,... | collective-permute-start | bytes 98312 | tf_op jit(solution)/shard_map/ppermute | solution.py:40
  22.4 25.4 %collective-permute-start.11 = (bf16[2,32,256]{2,1,0:T(8,128)(2,1)S(1)}, bf16[2,32,256]{2,1,0:T(8,128)(2,1)S(1)}, u32[]{:S(2)}, u32[]{:S(2)}) collective-permute-start(bf16[2,32,256]{2,1,0:T(8,128)(2,1)S(1)} %copy-done.3), channel_id=1, source_target_pairs={{0,4},{1,5},{2,6},{3,7},{4,0},{5,1},{6,2},{7,3},{8,12},{9,13},{10,... | collective-permute-start | bytes 98312 | tf_op jit(solution)/shard_map/ppermute | solution.py:40
  23.9 24.4 %collective-permute-start.13 = (bf16[2,32,256]{2,1,0:T(8,128)(2,1)S(1)}, bf16[2,32,256]{2,1,0:T(8,128)(2,1)S(1)}, u32[]{:S(2)}, u32[]{:S(2)}) collective-permute-start(bf16[2,32,256]{2,1,0:T(8,128)(2,1)S(1)} %copy-done.3), channel_id=1, source_target_pairs={{0,6},{1,7},{2,4},{3,5},{4,2},{5,3},{6,0},{7,1},{8,14},{9,15},{10,... | collective-permute-start | bytes 98312 | tf_op jit(solution)/shard_map/ppermute | solution.py:40
  46.9 8.0 %copy-start.4 = (bf16[2,32,256]{2,1,0:T(8,128)(2,1)}, bf16[2,32,256]{2,1,0:T(8,128)(2,1)S(1)}, u32[]{:S(2)}) copy-start(bf16[2,32,256]{2,1,0:T(8,128)(2,1)S(1)} %collective-permute-done.9.refs_2_) | copy-start | bytes 98308
  46.9 28.0 %collective-permute-start.15 = (bf16[2,32,32,256]{3,2,1,0:T(8,128)(2,1)}, bf16[2,32,32,256]{3,2,1,0:T(8,128)(2,1)}, u32[]{:S(2)}, u32[]{:S(2)}) collective-permute-start(bf16[2,32,32,256]{3,2,1,0:T(8,128)(2,1)} %get-tuple-element.14), channel_id=1, source_target_pairs={{0,3},{1,2},{2,1},{3,0},{4,7},{5,6},{6,5},{7,4},{8,11},{9,10},{10,... | collective-permute-start | bytes 3145736 | tf_op jit(solution)/shard_map/ppermute | solution.py:40
  47.8 7.1 %copy-start.5 = (bf16[2,32,256]{2,1,0:T(8,128)(2,1)}, bf16[2,32,256]{2,1,0:T(8,128)(2,1)S(1)}, u32[]{:S(2)}) copy-start(bf16[2,32,256]{2,1,0:T(8,128)(2,1)S(1)} %collective-permute-done.11.refs_4_) | copy-start | bytes 98308
  47.8 1.2 collective-permute-start.8
  48.3 6.6 %copy-start.6 = (bf16[2,32,256]{2,1,0:T(8,128)(2,1)}, bf16[2,32,256]{2,1,0:T(8,128)(2,1)S(1)}, u32[]{:S(2)}) copy-start(bf16[2,32,256]{2,1,0:T(8,128)(2,1)S(1)} %collective-permute-done.13.refs_6_) | copy-start | bytes 98308
  48.3 1.2 collective-permute-start.10
  49.0 5.9 %copy-start.7 = (bf16[2,32,256]{2,1,0:T(8,128)(2,1)}, bf16[2,32,256]{2,1,0:T(8,128)(2,1)S(1)}, u32[]{:S(2)}) copy-start(bf16[2,32,256]{2,1,0:T(8,128)(2,1)S(1)} %collective-permute-done.8.refs_1_) | copy-start | bytes 98308
  49.0 1.2 collective-permute-start.12
  49.5 5.4 %copy-start.8 = (bf16[2,32,256]{2,1,0:T(8,128)(2,1)}, bf16[2,32,256]{2,1,0:T(8,128)(2,1)S(1)}, u32[]{:S(2)}) copy-start(bf16[2,32,256]{2,1,0:T(8,128)(2,1)S(1)} %collective-permute-done.10.refs_3_) | copy-start | bytes 98308
  49.5 47.9 %collective-permute-start.19 = (bf16[2,32,32,256]{3,2,1,0:T(8,128)(2,1)}, bf16[2,32,32,256]{3,2,1,0:T(8,128)(2,1)}, u32[]{:S(2)}, u32[]{:S(2)}) collective-permute-start(bf16[2,32,32,256]{3,2,1,0:T(8,128)(2,1)} %get-tuple-element.16), channel_id=1, source_target_pairs={{0,5},{1,4},{2,7},{3,6},{4,1},{5,0},{6,3},{7,2},{8,13},{9,12},{10,... | collective-permute-start | bytes 3145736 | tf_op jit(solution)/shard_map/ppermute | solution.py:40
  50.2 4.7 %copy-start.9 = (bf16[2,32,256]{2,1,0:T(8,128)(2,1)}, bf16[2,32,256]{2,1,0:T(8,128)(2,1)S(1)}, u32[]{:S(2)}) copy-start(bf16[2,32,256]{2,1,0:T(8,128)(2,1)S(1)} %collective-permute-done.12.refs_5_) | copy-start | bytes 98308
  50.2 1.2 collective-permute-start.14
  51.4 3.5 %copy-start.10 = (bf16[2,32,256]{2,1,0:T(8,128)(2,1)}, bf16[2,32,256]{2,1,0:T(8,128)(2,1)S(1)}, u32[]{:S(2)}) copy-start(bf16[2,32,256]{2,1,0:T(8,128)(2,1)S(1)} %collective-permute-done.14.refs_7_) | copy-start | bytes 98308
  51.4 55.8 %collective-permute-start.22 = (bf16[2,32,32,256]{3,2,1,0:T(8,128)(2,1)}, bf16[2,32,32,256]{3,2,1,0:T(8,128)(2,1)}, u32[]{:S(2)}, u32[]{:S(2)}) collective-permute-start(bf16[2,32,32,256]{3,2,1,0:T(8,128)(2,1)} %get-tuple-element.17), channel_id=1, source_target_pairs={{0,6},{1,7},{2,4},{3,5},{4,2},{5,3},{6,0},{7,1},{8,14},{9,15},{10,... | collective-permute-start | bytes 3145736 | tf_op jit(solution)/shard_map/ppermute | solution.py:40
  53.3 63.9 %collective-permute-start.7 = (bf16[2,32,32,256]{3,2,1,0:T(8,128)(2,1)}, bf16[2,32,32,256]{3,2,1,0:T(8,128)(2,1)}, u32[]{:S(2)}, u32[]{:S(2)}) collective-permute-start(bf16[2,32,32,256]{3,2,1,0:T(8,128)(2,1)} %get-tuple-element.13), channel_id=1, source_target_pairs={{0,2},{1,3},{2,0},{3,1},{4,6},{5,7},{6,4},{7,5},{8,10},{9,11},{10,... | collective-permute-start | bytes 3145736 | tf_op jit(solution)/shard_map/ppermute | solution.py:40
  54.0 75.3 %collective-permute-start.18 = (bf16[2,32,32,256]{3,2,1,0:T(8,128)(2,1)}, bf16[2,32,32,256]{3,2,1,0:T(8,128)(2,1)}, u32[]{:S(2)}, u32[]{:S(2)}) collective-permute-start(bf16[2,32,32,256]{3,2,1,0:T(8,128)(2,1)} %get-tuple-element.15), channel_id=1, source_target_pairs={{0,4},{1,5},{2,6},{3,7},{4,0},{5,1},{6,2},{7,3},{8,12},{9,13},{10,... | collective-permute-start | bytes 3145736 | tf_op jit(solution)/shard_map/ppermute | solution.py:40
  56.6 0.9 copy-start
  74.9 32.4 %collective-permute-start.24 = (f32[2,32,256]{2,1,0:T(8,128)S(1)}, f32[2,32,256]{2,1,0:T(8,128)S(1)}, u32[]{:S(2)}, u32[]{:S(2)}) collective-permute-start(f32[2,32,256]{2,1,0:T(8,128)S(1)} %last.12), channel_id=1, source_target_pairs={{0,1},{1,0},{2,3},{3,2},{4,5},{5,4},{6,7},{7,6},{8,9},{9,8},{10,11... | collective-permute-start | bytes 196616 | tf_op jit(solution)/shard_map/ppermute | solution.py:40
  97.4 21.7 %collective-permute-start.16 = (f32[2,32,256]{2,1,0:T(8,128)S(1)}, f32[2,32,256]{2,1,0:T(8,128)S(1)}, u32[]{:S(2)}, u32[]{:S(2)}) collective-permute-start(f32[2,32,256]{2,1,0:T(8,128)S(1)} %last.8), channel_id=1, source_target_pairs={{0,1},{1,0},{2,3},{3,2},{4,5},{5,4},{6,7},{7,6},{8,9},{9,8},{10,11... | collective-permute-start | bytes 196616 | tf_op jit(solution)/shard_map/ppermute | solution.py:40
  107.3 31.7 %collective-permute-start.27 = (f32[2,32,256]{2,1,0:T(8,128)S(1)}, f32[2,32,256]{2,1,0:T(8,128)S(1)}, u32[]{:S(2)}, u32[]{:S(2)}) collective-permute-start(f32[2,32,256]{2,1,0:T(8,128)S(1)} %last.14), channel_id=1, source_target_pairs={{0,1},{1,0},{2,3},{3,2},{4,5},{5,4},{6,7},{7,6},{8,9},{9,8},{10,11... | collective-permute-start | bytes 196616 | tf_op jit(solution)/shard_map/ppermute | solution.py:40
  107.3 22.0 %collective-permute-start.20 = (f32[2,32,256]{2,1,0:T(8,128)S(1)}, f32[2,32,256]{2,1,0:T(8,128)S(1)}, u32[]{:S(2)}, u32[]{:S(2)}) collective-permute-start(f32[2,32,256]{2,1,0:T(8,128)S(1)} %last.10), channel_id=1, source_target_pairs={{0,1},{1,0},{2,3},{3,2},{4,5},{5,4},{6,7},{7,6},{8,9},{9,8},{10,11... | collective-permute-start | bytes 196616 | tf_op jit(solution)/shard_map/ppermute | solution.py:40
  116.8 22.1 %copy-start.1 = (bf16[2,256,256]{2,1,0:T(8,128)(2,1)S(1)}, bf16[2,256,256]{2,1,0:T(8,128)(2,1)}, u32[]{:S(2)}) copy-start(bf16[2,256,256]{2,1,0:T(8,128)(2,1)} %join.1.right_ref) | copy-start | bytes 786436
  117.2 30.4 %collective-permute-start.25 = (f32[2,32,256]{2,1,0:T(8,128)S(1)}, f32[2,32,256]{2,1,0:T(8,128)S(1)}, u32[]{:S(2)}, u32[]{:S(2)}) collective-permute-start(f32[2,32,256]{2,1,0:T(8,128)S(1)} %last.13), channel_id=1, source_target_pairs={{0,6},{1,7},{2,4},{3,5},{4,2},{5,3},{6,0},{7,1},{8,14},{9,15},{10,... | collective-permute-start | bytes 196616 | tf_op jit(solution)/shard_map/ppermute | solution.py:40
  128.2 19.4 %collective-permute-start.17 = (f32[2,32,256]{2,1,0:T(8,128)S(1)}, f32[2,32,256]{2,1,0:T(8,128)S(1)}, u32[]{:S(2)}, u32[]{:S(2)}) collective-permute-start(f32[2,32,256]{2,1,0:T(8,128)S(1)} %last.9), channel_id=1, source_target_pairs={{0,2},{1,3},{2,0},{3,1},{4,6},{5,7},{6,4},{7,5},{8,10},{9,11},{10,... | collective-permute-start | bytes 196616 | tf_op jit(solution)/shard_map/ppermute | solution.py:40
  138.3 9.3 %collective-permute-start.21 = (f32[2,32,256]{2,1,0:T(8,128)S(1)}, f32[2,32,256]{2,1,0:T(8,128)S(1)}, u32[]{:S(2)}, u32[]{:S(2)}) collective-permute-start(f32[2,32,256]{2,1,0:T(8,128)S(1)} %last.11), channel_id=1, source_target_pairs={{0,4},{1,5},{2,6},{3,7},{4,0},{5,1},{6,2},{7,3},{8,12},{9,13},{10,... | collective-permute-start | bytes 196616 | tf_op jit(solution)/shard_map/ppermute | solution.py:40

commit v2 on v1

--- a/solution.py
+++ b/solution.py
@@ -8,7 +8,7 @@
 from jax.sharding import PartitionSpec as P
 
 AXIS = "cuts"
-LIMIT = 48 * 1024 * 1024
+LIMIT = 20 * 1024 * 1024
 LANES = 128
 
 
@@ -40,23 +40,25 @@
     return lax.ppermute(value, AXIS, [(i, i ^ mask) for i in range(n)])
 
 
-def gather_rows(value, n):
+def off_chip_rows(value, n):
+    return {mask: swap(value, mask, n) if mask else value for mask in range(n - 2, -2, -2)}
+
+
+def both_cores(even, n):
     rows = [None] * n
-    rows[0] = value
-    for mask in range(n - 2, 0, -2):
-        rows[mask] = swap(value, mask, n)
-    for mask in range(0, n, 2):
-        rows[mask + 1] = swap(rows[mask], 1, n)
+    for mask, value in even.items():
+        rows[mask], rows[mask + 1] = value, swap(value, 1, n)
     return rows
 
 
 def first_kernel(n, masks, me_ref, *refs):
     pieces, x_ref = refs[:n], refs[n]
-    outs, (full, turned, chosen) = refs[n + 1 : n + 1 + len(masks)], refs[n + 1 + len(masks) :]
+    outs, (full, turned, chosen) = refs[-3 - len(masks) : -3], refs[-3:]
     rows = pieces[0].shape[1]
+    parent, chunk, step = pl.program_id(0), pl.program_id(1), outs[0].shape[1]
     me = me_ref[0]
 
-    @pl.when(pl.program_id(1) == 0)
+    @pl.when(chunk == 0)
     def _():
         for m in range(n):
             full[pl.ds(pl.multiple_of((me ^ m) * rows, rows), rows), :] = pieces[m][0]
@@ -66,13 +68,15 @@
                 pl.ds(pl.multiple_of((me ^ m) * rows, rows), rows), :
             ]
 
-    for a in range(x_ref.shape[1]):
-        product = jnp.dot(chosen[...], x_ref[0, a], preferred_element_type=jnp.float32).astype(jnp.bfloat16)
+    for a in range(step):
+        product = jnp.dot(
+            chosen[...], x_ref[parent, chunk * step + a], preferred_element_type=jnp.float32
+        ).astype(jnp.bfloat16)
         for slot, out in enumerate(outs):
             out[0, a] = product[slot * rows : (slot + 1) * rows, :]
 
 
-def first_for(me, pieces, core_x, masks):
+def first_for(me, pieces, core_x, masks, after=()):
     n = len(pieces)
     parents, mine, left, right = core_x.shape
     rows = pieces[0].shape[1]
@@ -83,7 +87,8 @@
         grid=(parents, mine // step),
         in_specs=[pl.BlockSpec(memory_space=pltpu.SMEM)]
         + [spec] * n
-        + [pl.BlockSpec((1, step, left, right), lambda p, c: (p, c, 0, 0))],
+        + [pl.BlockSpec(memory_space=pltpu.VMEM)]
+        + [pl.BlockSpec(memory_space=pl.ANY)] * len(after),
         out_specs=[pl.BlockSpec((1, step, rows, right), lambda p, c: (p, c, 0, 0))] * len(masks),
         out_shape=[jax.ShapeDtypeStruct((parents, mine, rows, right), jnp.bfloat16)] * len(masks),
         scratch_shapes=[
@@ -98,7 +103,7 @@
             transcendentals=0,
         ),
         name="first",
-    )(me, *pieces, core_x)
+    )(me, *pieces, core_x, *after)
 
 
 def join_kernel(n, me_ref, *refs):
@@ -126,47 +131,37 @@
     out_ref, second, flat = refs[-3:]
     count, rows = first_ref.shape[1], first_ref.shape[2]
     width = right_ref.shape[2]
-    c = pl.program_id(1)
-
-    @pl.when(c == 0)
-    def _():
-        whole = jnp.dot(
-            first_ref[0].reshape(count * rows, first_ref.shape[3]),
-            right_ref[0],
-            preferred_element_type=jnp.float32,
-        )
+    whole = jnp.dot(
+        first_ref[0].reshape(count * rows, first_ref.shape[3]),
+        right_ref[0],
+        preferred_element_type=jnp.float32,
+    )
+    for h in range(width // LANES):
+        second[h] = whole[:, h * LANES : (h + 1) * LANES]
+    for k in range(rows):
         for h in range(width // LANES):
-            second[h] = whole[:, h * LANES : (h + 1) * LANES]
-        for k in range(rows):
-            for h in range(width // LANES):
-                flat[:, k * width + h * LANES : k * width + (h + 1) * LANES] = second[
-                    h, pl.ds(k, count, stride=rows), :
-                ].astype(jnp.bfloat16)
-        if held:
-            out_ref[...] = refs[0][...]
-        else:
-            out_ref[...] = jnp.zeros_like(out_ref)
-
-    depth = y_ref.shape[1] * width
-    out_ref[0] += jnp.dot(
-        flat[:, pl.ds(pl.multiple_of(c * depth, depth), depth)],
-        y_ref[0].reshape(depth, y_ref.shape[3]),
+            flat[:, k * width + h * LANES : k * width + (h + 1) * LANES] = second[
+                h, pl.ds(k, count, stride=rows), :
+            ].astype(jnp.bfloat16)
+    total = jnp.dot(
+        flat[...],
+        y_ref[pl.program_id(0)].reshape(rows * width, y_ref.shape[3]),
         preferred_element_type=jnp.float32,
     )
+    out_ref[0] = total + refs[0][0] if held else total
 
 
 def last_for(first, right_full, core_y, begin=None):
     parents, count, rows, depth = first.shape
     width, out_width = right_full.shape[2], core_y.shape[3]
-    step = min(8, rows)
-    spec = pl.BlockSpec((1, count, out_width), lambda p, c: (p, 0, 0))
+    spec = pl.BlockSpec((1, count, out_width), lambda p: (p, 0, 0))
     return pl.pallas_call(
         functools.partial(last_kernel, begin is not None),
-        grid=(parents, rows // step),
+        grid=(parents,),
         in_specs=[
-            pl.BlockSpec((1, count, rows, depth), lambda p, c: (p, 0, 0, 0)),
-            pl.BlockSpec((1, depth, width), lambda p, c: (p, 0, 0)),
-            pl.BlockSpec((1, step, width, out_width), lambda p, c: (p, c, 0, 0)),
+            pl.BlockSpec((1, count, rows, depth), lambda p: (p, 0, 0, 0)),
+            pl.BlockSpec((1, depth, width), lambda p: (p, 0, 0)),
+            pl.BlockSpec(memory_space=pltpu.VMEM),
         ]
         + [spec] * (begin is not None),
         out_specs=spec,
@@ -188,16 +183,18 @@
 def exchanged(core_x, core_y, left_intersection, right_intersection, n):
     me = lax.axis_index(AXIS).astype(jnp.int32).reshape(1)
     pairs = list(range(2, n, 2))
-    left = gather_rows(left_intersection, n)
+    left = off_chip_rows(left_intersection, n)
+    right = off_chip_rows(right_intersection, n)
+    left = both_cores(left, n)
     early = [mask + 1 for mask in pairs[:2]]
     late = [mask for mask in range(n) if mask not in early]
-    sent = dict(zip(early, first_for(me, left, core_x, early)))
+    sent = dict(zip(early, first_for(me, left, core_x, early, list(right.values()))))
     came = {mask: swap(sent[mask], mask, n) for mask in early}
     sent.update(zip(late, first_for(me, left, core_x, late)))
     for mask in [m for m in pairs[:2]] + [m + 1 for m in pairs[2:]] + pairs[2:] + [1]:
         came[mask] = swap(sent[mask], mask, n)
     came[0] = sent[0]
-    right = join(me, gather_rows(right_intersection, n))
+    right = join(me, both_cores(right, n))
     total = []
     for mask in pairs + [0]:
         odd = last_for(came[mask + 1], right, core_y)

time: 150 us -> 132 us (0.88)
  Pallas kernels: 89.7 us -> 46.4 us
  waiting for transfers between devices: 38.1 us -> 52.4 us
  local copies, waits for them, and re-layouts: 1.74 us -> 9.27 us
  starting transfers between devices: 17.9 us -> 22.3 us
    pallas_call x8, Pallas kernels: 71.1 us -> 36.6 us  [last_for(): pl.pallas_call(functools.partial(last_kernel, begin is not None), grid=(p...]
    ppermute x28, waiting for transfers between devices: 38.1 us -> 52.4 us  [swap(): return lax.ppermute(value, AXIS, [(i, i ^ mask) for i in range(n)])]
    pallas_call x2, Pallas kernels: 17 us -> 8.2 us  [first_for(): pl.pallas_call(functools.partial(first_kernel, n, masks), grid=(parents,...]
    unnamed x22 -> x30, local copies, waits for them, and re-layouts: 1.74 us -> 9.27 us
    ppermute x28, starting transfers between devices: 17.9 us -> 22.3 us  [swap(): return lax.ppermute(value, AXIS, [(i, i ^ mask) for i in range(n)])]
  transfers between devices with their start and end apart: 28 -> 28, of which waited for: 12 -> 8; matrix products, arithmetic and copies ran while one was open for 0% -> 0% of each run, Pallas kernels for 55% -> 33%
where the time goes in v2:
time: 132 us; the launch traced here: 131 us
  waiting for transfers between devices  52.4 us (40%)
  Pallas kernels  46.4 us (35%)
  starting transfers between devices  22.3 us (17%)
  local copies, waits for them, and re-layouts  9.27 us (7%)
    ppermute x28, waiting for transfers between devices, swap(): return lax.ppermute(value, AXIS, [(i, i ^ mask) for i in range(n)])  52.4 us
    pallas_call x8, Pallas kernels, last_for(): pl.pallas_call(functools.partial(last_kernel, begin is not None), grid=(p...  36.6 us
    ppermute x28, starting transfers between devices, swap(): return lax.ppermute(value, AXIS, [(i, i ^ mask) for i in range(n)])  22.3 us
    unnamed x30, local copies, waits for them, and re-layouts  9.27 us
    pallas_call x2, Pallas kernels, first_for(): pl.pallas_call(functools.partial(first_kernel, n, masks), grid=(parents,...  8.2 us
  transfers between devices with their start and end apart: 28, of which 8 were waited for; matrix products, arithmetic and copies ran while one was open for 0% of the time, Pallas kernels for 33%

profile of v2, /device:TPU:0, one launch (start us, length us, event | category | flops | bytes accessed | tf_op | source)
XLA Modules:
  0.0 131.2 jit_solution(7603230705112037219)
XLA Ops:
  0.0 3.9 %collective-permute-start.5 = (bf16[2,32,256]{2,1,0:T(8,128)(2,1)}, bf16[2,32,256]{2,1,0:T(8,128)(2,1)S(1)}, u32[]{:S(2)}, u32[]{:S(2)}) collective-permute-start(bf16[2,32,256]{2,1,0:T(8,128)(2,1)} %refs_0_.5), channel_id=1, source_target_pairs={{0,6},{1,7},{2,4},{3,5},{4,2},{5,3},{6,0},{7,1},{8,14},{9,15},{10,... | collective-permute-start | bytes 98312 | tf_op jit(solution)/shard_map/ppermute | solution.py:40
  3.9 0.5 collective-permute-start.3
  4.4 0.1 collective-permute-start.1
  4.5 2.9 %collective-permute-start.13 = (bf16[2,32,256]{2,1,0:T(8,128)(2,1)}, bf16[2,32,256]{2,1,0:T(8,128)(2,1)S(1)}, u32[]{:S(2)}, u32[]{:S(2)}) collective-permute-start(bf16[2,32,256]{2,1,0:T(8,128)(2,1)} %refs_12_.1), channel_id=1, source_target_pairs={{0,6},{1,7},{2,4},{3,5},{4,2},{5,3},{6,0},{7,1},{8,14},{9,15},{10,... | collective-permute-start | bytes 98312 | tf_op jit(solution)/shard_map/ppermute | solution.py:40
  7.4 0.6 collective-permute-start.11
  8.0 1.4 %collective-permute-start.9 = (bf16[2,32,256]{2,1,0:T(8,128)(2,1)}, bf16[2,32,256]{2,1,0:T(8,128)(2,1)S(1)}, u32[]{:S(2)}, u32[]{:S(2)}) collective-permute-start(bf16[2,32,256]{2,1,0:T(8,128)(2,1)} %refs_12_.1), channel_id=1, source_target_pairs={{0,2},{1,3},{2,0},{3,1},{4,6},{5,7},{6,4},{7,5},{8,10},{9,11},{10,... | collective-permute-start | bytes 98312 | tf_op jit(solution)/shard_map/ppermute | solution.py:40
  9.5 0.5 collective-permute-start.4
  10.0 0.1 collective-permute-start.2
  10.1 1.4 %collective-permute-done.11.refs_4_.refs_10_ = bf16[2,32,256]{2,1,0:T(8,128)(2,1)S(1)} collective-permute-done((bf16[2,32,256]{2,1,0:T(8,128)(2,1)}, bf16[2,32,256]{2,1,0:T(8,128)(2,1)S(1)}, u32[]{:S(2)}, u32[]{:S(2)}) %collective-permute-start.11) | collective-permute-done | bytes 32800 | tf_op jit(solution)/shard_map/ppermute | solution.py:40
  11.5 0.6 collective-permute-done.9.refs_2_.refs_11_
  12.2 3.4 %copy-done.1 = bf16[2,32,256,256]{3,2,1,0:T(8,128)(2,1)S(1)} copy-done((bf16[2,32,256,256]{3,2,1,0:T(8,128)(2,1)S(1)}, bf16[2,32,256,256]{3,2,1,0:T(8,128)(2,1)}, u32[]{:S(2)}) %copy-start.1) | copy-done | bytes 8388632
  15.6 0.8 copy-done.4
  16.3 0.8 copy-done.5
  17.1 2.8 %first.3 = (bf16[2,32,32,256]{3,2,1,0:T(8,128)(2,1)S(1)}, bf16[2,32,32,256]{3,2,1,0:T(8,128)(2,1)S(1)}) custom-call(s32[1]{0:T(128)} %bitcast.me_ref, bf16[2,32,256]{2,1,0:T(8,128)(2,1)S(1)} %copy-done.4, bf16[2,32,256]{2,1,0:T(8,128)(2,1)S(1)} %collective-permute-done.refs_1_, bf16[2,32,256]{2,1,0:T(8,128)(2,1)S(1)} %collective-permute-done.1.refs_2_, ...), custom_call_target="tpu_custom_call" | custom-call | flops 536870912 | bytes 10485760 | tf_op jit(solution)/shard_map/first/pallas_call | solution.py:85
  19.9 0.3 collective-permute-start.15
  20.3 1.7 %collective-permute-start.19 = (bf16[2,32,32,256]{3,2,1,0:T(8,128)(2,1)S(1)}, bf16[2,32,32,256]{3,2,1,0:T(8,128)(2,1)S(1)}, u32[]{:S(2)}, u32[]{:S(2)}) collective-permute-start(bf16[2,32,32,256]{3,2,1,0:T(8,128)(2,1)S(1)} %get-tuple-element.16), channel_id=1, source_target_pairs={{0,5},{1,4},{2,7},{3,6},{4,1},{5,0},{6,3},{7,2},{8,13},{9,12},{10,... | collective-permute-start | bytes 3145736 | tf_op jit(solution)/shard_map/ppermute | solution.py:40
  21.9 5.4 %first.2 = (bf16[2,32,32,256]{3,2,1,0:T(8,128)(2,1)S(1)}, bf16[2,32,32,256]{3,2,1,0:T(8,128)(2,1)}, bf16[2,32,32,256]{3,2,1,0:T(8,128)(2,1)}, bf16[2,32,32,256]{...) custom-call(s32[1]{0:T(128)} %bitcast.me_ref, ...), custom_call_target="tpu_custom_call" | custom-call | flops 1610612736 | bytes 14680064 | tf_op jit(solution)/shard_map/first/pallas_call | solution.py:85
  27.3 0.8 collective-permute-start.23
  28.1 0.6 collective-permute-start.8
  28.7 0.9 collective-permute-done.8.refs_1_
  29.6 0.3 collective-permute-start.12
  29.9 0.2 collective-permute-start.26
  30.1 0.7 collective-permute-done.12.refs_5_
  30.8 0.3 collective-permute-start.10
  31.1 1.5 %collective-permute-done.10.refs_3_ = bf16[2,32,256]{2,1,0:T(8,128)(2,1)S(1)} collective-permute-done((bf16[2,32,256]{2,1,0:T(8,128)(2,1)S(1)}, bf16[2,32,256]{2,1,0:T(8,128)(2,1)S(1)}, u32[]{:S(2)}, u32[]{:S(2)}) %collective-permute-start.10) | collective-permute-done | bytes 32800 | tf_op jit(solution)/shard_map/ppermute | solution.py:40
  32.6 1.4 %collective-permute-start.7 = (bf16[2,32,32,256]{3,2,1,0:T(8,128)(2,1)}, bf16[2,32,32,256]{3,2,1,0:T(8,128)(2,1)}, u32[]{:S(2)}, u32[]{:S(2)}) collective-permute-start(bf16[2,32,32,256]{3,2,1,0:T(8,128)(2,1)} %get-tuple-element.13), channel_id=1, source_target_pairs={{0,2},{1,3},{2,0},{3,1},{4,6},{5,7},{6,4},{7,5},{8,10},{9,11},{10,... | collective-permute-start | bytes 3145736 | tf_op jit(solution)/shard_map/ppermute | solution.py:40
  34.1 11.4 %collective-permute-done.15.first_ref = bf16[2,32,32,256]{3,2,1,0:T(8,128)(2,1)S(1)} collective-permute-done((bf16[2,32,32,256]{3,2,1,0:T(8,128)(2,1)S(1)}, bf16[2,32,32,256]{3,2,1,0:T(8,128)(2,1)S(1)}, u32[]{:S(2)}, u32[]{:S(2)}) %collective-permute-start.15) | collective-permute-done | bytes 1048608 | tf_op jit(solution)/shard_map/ppermute | solution.py:40
  45.4 1.3 %collective-permute-start.18 = (bf16[2,32,32,256]{3,2,1,0:T(8,128)(2,1)}, bf16[2,32,32,256]{3,2,1,0:T(8,128)(2,1)}, u32[]{:S(2)}, u32[]{:S(2)}) collective-permute-start(bf16[2,32,32,256]{3,2,1,0:T(8,128)(2,1)} %get-tuple-element.15), channel_id=1, source_target_pairs={{0,4},{1,5},{2,6},{3,7},{4,0},{5,1},{6,2},{7,3},{8,12},{9,13},{10,... | collective-permute-start | bytes 3145736 | tf_op jit(solution)/shard_map/ppermute | solution.py:40
  46.7 21.1 %collective-permute-done.19.first_ref = bf16[2,32,32,256]{3,2,1,0:T(8,128)(2,1)S(1)} collective-permute-done((bf16[2,32,32,256]{3,2,1,0:T(8,128)(2,1)S(1)}, bf16[2,32,32,256]{3,2,1,0:T(8,128)(2,1)S(1)}, u32[]{:S(2)}, u32[]{:S(2)}) %collective-permute-start.19) | collective-permute-done | bytes 1048608 | tf_op jit(solution)/shard_map/ppermute | solution.py:40
  67.8 1.6 %join.1.right_ref = bf16[2,256,256]{2,1,0:T(8,128)(2,1)} custom-call(s32[1]{0:T(128)} %bitcast.me_ref, bf16[2,32,256]{2,1,0:T(8,128)(2,1)} %refs_12_.1, bf16[2,32,256]{2,1,0:T(8,128)(2,1)} %copy-done.9, bf16[2,32,256]{2,1,0:T(8,128)(2,1)} %copy-done.8, bf16[2,32,256]{2,1,0:T(8,128)(2,1)} %copy-done.12, bf16[2,32,256]{2,1,0:T(8,128)(2,1)} %copy-done.7, ...), custom_call_target="tpu_custom_call" | custom-call | bytes 524288 | tf_op jit(solution)/shard_map/join/pallas_call | solution.py:120
  69.4 3.4 %copy-done = bf16[2,32,256,256]{3,2,1,0:T(8,128)(2,1)S(1)} copy-done((bf16[2,32,256,256]{3,2,1,0:T(8,128)(2,1)S(1)}, bf16[2,32,256,256]{3,2,1,0:T(8,128)(2,1)}, u32[]{:S(2)}) %copy-start) | copy-done | bytes 8388632
  72.8 0.9 copy-done.2
  73.8 3.9 %last.8 = f32[2,32,256]{2,1,0:T(8,128)S(1)} custom-call(bf16[2,32,32,256]{3,2,1,0:T(8,128)(2,1)S(1)} %collective-permute-done.15.first_ref, bf16[2,256,256]{2,1,0:T(8,128)(2,1)S(1)} %copy-done.2, bf16[2,32,256,256]{3,2,1,0:T(8,128)(2,1)S(1)} %copy-done), custom_call_target="tpu_custom_call" | custom-call | flops 536870912 | bytes 9437184 | tf_op jit(solution)/shard_map/last/pallas_call | solution.py:158
  77.7 3.9 %last.10 = f32[2,32,256]{2,1,0:T(8,128)S(1)} custom-call(bf16[2,32,32,256]{3,2,1,0:T(8,128)(2,1)S(1)} %collective-permute-done.19.first_ref, bf16[2,256,256]{2,1,0:T(8,128)(2,1)S(1)} %copy-done.2, bf16[2,32,256,256]{3,2,1,0:T(8,128)(2,1)S(1)} %copy-done), custom_call_target="tpu_custom_call" | custom-call | flops 536870912 | bytes 9437184 | tf_op jit(solution)/shard_map/last/pallas_call | solution.py:158
  81.6 0.1 collective-permute-start.16
  81.7 5.1 %last.12 = f32[2,32,256]{2,1,0:T(8,128)S(1)} custom-call(bf16[2,32,32,256]{3,2,1,0:T(8,128)(2,1)} %collective-permute-done.23.first_ref, bf16[2,256,256]{2,1,0:T(8,128)(2,1)S(1)} %copy-done.2, bf16[2,32,256,256]{3,2,1,0:T(8,128)(2,1)S(1)} %copy-done), custom_call_target="tpu_custom_call" | custom-call | flops 536870912 | bytes 9437184 | tf_op jit(solution)/shard_map/last/pallas_call | solution.py:158
  86.8 0.4 collective-permute-start.20
  87.2 5.0 %last.14 = f32[2,32,256]{2,1,0:T(8,128)S(1)} custom-call(bf16[2,32,32,256]{3,2,1,0:T(8,128)(2,1)} %collective-permute-done.26.first_ref, bf16[2,256,256]{2,1,0:T(8,128)(2,1)S(1)} %copy-done.2, bf16[2,32,256,256]{3,2,1,0:T(8,128)(2,1)S(1)} %bitcast.2), custom_call_target="tpu_custom_call" | custom-call | flops 536870912 | bytes 9437184 | tf_op jit(solution)/shard_map/last/pallas_call | solution.py:158
  92.2 0.2 collective-permute-start.24
  92.5 0.3 collective-permute-start.27
  92.8 5.0 %last.9 = f32[2,32,256]{2,1,0:T(8,128)S(1)} custom-call(bf16[2,32,32,256]{3,2,1,0:T(8,128)(2,1)} %collective-permute-done.7.first_ref, bf16[2,256,256]{2,1,0:T(8,128)(2,1)S(1)} %copy-done.2, bf16[2,32,256,256]{3,2,1,0:T(8,128)(2,1)S(1)} %bitcast.2, f32[2,32,256]{2,1,0:T(8,128)S(1)} %collective-permute-done.16.refs_0_), custom_call_target="tpu_custom_call" | custom-call | flops 536870912 | bytes 9437184 | tf_op jit(solution)/shard_map/last/pallas_call | solution.py:158
  97.8 14.7 %collective-permute-done.18.first_ref = bf16[2,32,32,256]{3,2,1,0:T(8,128)(2,1)} collective-permute-done((bf16[2,32,32,256]{3,2,1,0:T(8,128)(2,1)}, bf16[2,32,32,256]{3,2,1,0:T(8,128)(2,1)}, u32[]{:S(2)}, u32[]{:S(2)}) %collective-permute-start.18) | collective-permute-done | bytes 1048608 | tf_op jit(solution)/shard_map/ppermute | solution.py:40
  112.5 5.0 %last.11 = f32[2,32,256]{2,1,0:T(8,128)S(1)} custom-call(bf16[2,32,32,256]{3,2,1,0:T(8,128)(2,1)} %collective-permute-done.18.first_ref, bf16[2,256,256]{2,1,0:T(8,128)(2,1)S(1)} %copy-done.2, bf16[2,32,256,256]{3,2,1,0:T(8,128)(2,1)S(1)} %bitcast.2, f32[2,32,256]{2,1,0:T(8,128)S(1)} %collective-permute-done.20.refs_0_), custom_call_target="tpu_custom_call" | custom-call | flops 536870912 | bytes 9437184 | tf_op jit(solution)/shard_map/last/pallas_call | solution.py:158
  117.5 2.5 %collective-permute-start.21 = (f32[2,32,256]{2,1,0:T(8,128)S(1)}, f32[2,32,256]{2,1,0:T(8,128)S(1)}, u32[]{:S(2)}, u32[]{:S(2)}) collective-permute-start(f32[2,32,256]{2,1,0:T(8,128)S(1)} %last.11), channel_id=1, source_target_pairs={{0,4},{1,5},{2,6},{3,7},{4,0},{5,1},{6,2},{7,3},{8,12},{9,13},{10,... | collective-permute-start | bytes 196616 | tf_op jit(solution)/shard_map/ppermute | solution.py:40
  120.0 5.0 %last.13 = f32[2,32,256]{2,1,0:T(8,128)S(1)} custom-call(bf16[2,32,32,256]{3,2,1,0:T(8,128)(2,1)} %collective-permute-done.22.first_ref, bf16[2,256,256]{2,1,0:T(8,128)(2,1)S(1)} %copy-done.2, bf16[2,32,256,256]{3,2,1,0:T(8,128)(2,1)S(1)} %bitcast.2, f32[2,32,256]{2,1,0:T(8,128)S(1)} %collective-permute-done.24.refs_0_), custom_call_target="tpu_custom_call" | custom-call | flops 536870912 | bytes 9437184 | tf_op jit(solution)/shard_map/last/pallas_call | solution.py:158
  124.9 1.7 %collective-permute-start.25 = (f32[2,32,256]{2,1,0:T(8,128)S(1)}, f32[2,32,256]{2,1,0:T(8,128)S(1)}, u32[]{:S(2)}, u32[]{:S(2)}) collective-permute-start(f32[2,32,256]{2,1,0:T(8,128)S(1)} %last.13), channel_id=1, source_target_pairs={{0,6},{1,7},{2,4},{3,5},{4,2},{5,3},{6,0},{7,1},{8,14},{9,15},{10,... | collective-permute-start | bytes 196616 | tf_op jit(solution)/shard_map/ppermute | solution.py:40
  126.6 3.9 %last.15 = f32[2,32,256]{2,1,0:T(8,128)S(1)} custom-call(bf16[2,32,32,256]{3,2,1,0:T(8,128)(2,1)S(1)} %get-tuple-element.19.first_ref, bf16[2,256,256]{2,1,0:T(8,128)(2,1)S(1)} %copy-done.3, bf16[2,32,256,256]{3,2,1,0:T(8,128)(2,1)S(1)} %bitcast.2, f32[2,32,256]{2,1,0:T(8,128)S(1)} %collective-permute-done.27.refs_0_), custom_call_target="tpu_custom_call" | custom-call | flops 536870912 | bytes 9437184 | tf_op jit(solution)/shard_map/last/pallas_call | solution.py:158
  130.6 0.6 add_add_fusion
  (51 shorter events, 0.2 us)
Async XLA Ops:
  0.0 7.4 %collective-permute-start.5 = (bf16[2,32,256]{2,1,0:T(8,128)(2,1)}, bf16[2,32,256]{2,1,0:T(8,128)(2,1)S(1)}, u32[]{:S(2)}, u32[]{:S(2)}) collective-permute-start(bf16[2,32,256]{2,1,0:T(8,128)(2,1)} %refs_0_.5), channel_id=1, source_target_pairs={{0,6},{1,7},{2,4},{3,5},{4,2},{5,3},{6,0},{7,1},{8,14},{9,15},{10,... | collective-permute-start | bytes 98312 | tf_op jit(solution)/shard_map/ppermute | solution.py:40
  3.9 4.1 %collective-permute-start.3 = (bf16[2,32,256]{2,1,0:T(8,128)(2,1)}, bf16[2,32,256]{2,1,0:T(8,128)(2,1)S(1)}, u32[]{:S(2)}, u32[]{:S(2)}) collective-permute-start(bf16[2,32,256]{2,1,0:T(8,128)(2,1)} %refs_0_.5), channel_id=1, source_target_pairs={{0,4},{1,5},{2,6},{3,7},{4,0},{5,1},{6,2},{7,3},{8,12},{9,13},{10,... | collective-permute-start | bytes 98312 | tf_op jit(solution)/shard_map/ppermute | solution.py:40
  4.4 5.1 %collective-permute-start.1 = (bf16[2,32,256]{2,1,0:T(8,128)(2,1)}, bf16[2,32,256]{2,1,0:T(8,128)(2,1)S(1)}, u32[]{:S(2)}, u32[]{:S(2)}) collective-permute-start(bf16[2,32,256]{2,1,0:T(8,128)(2,1)} %refs_0_.5), channel_id=1, source_target_pairs={{0,2},{1,3},{2,0},{3,1},{4,6},{5,7},{6,4},{7,5},{8,10},{9,11},{10,... | collective-permute-start | bytes 98312 | tf_op jit(solution)/shard_map/ppermute | solution.py:40
  4.5 5.0 %collective-permute-start = (bf16[2,32,256]{2,1,0:T(8,128)(2,1)}, bf16[2,32,256]{2,1,0:T(8,128)(2,1)S(1)}, u32[]{:S(2)}, u32[]{:S(2)}) collective-permute-start(bf16[2,32,256]{2,1,0:T(8,128)(2,1)} %refs_0_.5), channel_id=1, source_target_pairs={{0,1},{1,0},{2,3},{3,2},{4,5},{5,4},{6,7},{7,6},{8,9},{9,8},{10,11... | collective-permute-start | bytes 98312 | tf_op jit(solution)/shard_map/ppermute | solution.py:40
  4.5 5.5 %collective-permute-start.13 = (bf16[2,32,256]{2,1,0:T(8,128)(2,1)}, bf16[2,32,256]{2,1,0:T(8,128)(2,1)S(1)}, u32[]{:S(2)}, u32[]{:S(2)}) collective-permute-start(bf16[2,32,256]{2,1,0:T(8,128)(2,1)} %refs_12_.1), channel_id=1, source_target_pairs={{0,6},{1,7},{2,4},{3,5},{4,2},{5,3},{6,0},{7,1},{8,14},{9,15},{10,... | collective-permute-start | bytes 98312 | tf_op jit(solution)/shard_map/ppermute | solution.py:40
  7.4 4.1 %collective-permute-start.11 = (bf16[2,32,256]{2,1,0:T(8,128)(2,1)}, bf16[2,32,256]{2,1,0:T(8,128)(2,1)S(1)}, u32[]{:S(2)}, u32[]{:S(2)}) collective-permute-start(bf16[2,32,256]{2,1,0:T(8,128)(2,1)} %refs_12_.1), channel_id=1, source_target_pairs={{0,4},{1,5},{2,6},{3,7},{4,0},{5,1},{6,2},{7,3},{8,12},{9,13},{10,... | collective-permute-start | bytes 98312 | tf_op jit(solution)/shard_map/ppermute | solution.py:40
  8.0 4.1 %collective-permute-start.9 = (bf16[2,32,256]{2,1,0:T(8,128)(2,1)}, bf16[2,32,256]{2,1,0:T(8,128)(2,1)S(1)}, u32[]{:S(2)}, u32[]{:S(2)}) collective-permute-start(bf16[2,32,256]{2,1,0:T(8,128)(2,1)} %refs_12_.1), channel_id=1, source_target_pairs={{0,2},{1,3},{2,0},{3,1},{4,6},{5,7},{6,4},{7,5},{8,10},{9,11},{10,... | collective-permute-start | bytes 98312 | tf_op jit(solution)/shard_map/ppermute | solution.py:40
  9.5 2.7 %collective-permute-start.6 = (bf16[2,32,256]{2,1,0:T(8,128)(2,1)S(1)}, bf16[2,32,256]{2,1,0:T(8,128)(2,1)S(1)}, u32[]{:S(2)}, u32[]{:S(2)}) collective-permute-start(bf16[2,32,256]{2,1,0:T(8,128)(2,1)S(1)} %collective-permute-done.5.refs_6_), channel_id=1, source_target_pairs={{0,1},{1,0},{2,3},{3,2},{4,5},{5,4},{6,7},{7,6},{8,9},{9,8},{10,11... | collective-permute-start | bytes 98312 | tf_op jit(solution)/shard_map/ppermute | solution.py:40
  9.5 2.7 %collective-permute-start.4 = (bf16[2,32,256]{2,1,0:T(8,128)(2,1)S(1)}, bf16[2,32,256]{2,1,0:T(8,128)(2,1)S(1)}, u32[]{:S(2)}, u32[]{:S(2)}) collective-permute-start(bf16[2,32,256]{2,1,0:T(8,128)(2,1)S(1)} %collective-permute-done.3.refs_4_), channel_id=1, source_target_pairs={{0,1},{1,0},{2,3},{3,2},{4,5},{5,4},{6,7},{7,6},{8,9},{9,8},{10,11... | collective-permute-start | bytes 98312 | tf_op jit(solution)/shard_map/ppermute | solution.py:40
  10.0 18.7 %copy-start.6 = (bf16[2,32,256]{2,1,0:T(8,128)(2,1)}, bf16[2,32,256]{2,1,0:T(8,128)(2,1)S(1)}, u32[]{:S(2)}) copy-start(bf16[2,32,256]{2,1,0:T(8,128)(2,1)S(1)} %collective-permute-done.13.refs_6_.refs_9_) | copy-start | bytes 98308
  10.0 2.2 %collective-permute-start.2 = (bf16[2,32,256]{2,1,0:T(8,128)(2,1)S(1)}, bf16[2,32,256]{2,1,0:T(8,128)(2,1)S(1)}, u32[]{:S(2)}, u32[]{:S(2)}) collective-permute-start(bf16[2,32,256]{2,1,0:T(8,128)(2,1)S(1)} %collective-permute-done.1.refs_2_), channel_id=1, source_target_pairs={{0,1},{1,0},{2,3},{3,2},{4,5},{5,4},{6,7},{7,6},{8,9},{9,8},{10,11... | collective-permute-start | bytes 98312 | tf_op jit(solution)/shard_map/ppermute | solution.py:40
  11.5 18.1 %copy-start.7 = (bf16[2,32,256]{2,1,0:T(8,128)(2,1)}, bf16[2,32,256]{2,1,0:T(8,128)(2,1)S(1)}, u32[]{:S(2)}) copy-start(bf16[2,32,256]{2,1,0:T(8,128)(2,1)S(1)} %collective-permute-done.11.refs_4_.refs_10_) | copy-start | bytes 98308
  12.2 18.6 %copy-start.8 = (bf16[2,32,256]{2,1,0:T(8,128)(2,1)}, bf16[2,32,256]{2,1,0:T(8,128)(2,1)S(1)}, u32[]{:S(2)}) copy-start(bf16[2,32,256]{2,1,0:T(8,128)(2,1)S(1)} %collective-permute-done.9.refs_2_.refs_11_) | copy-start | bytes 98308
  12.2 3.4 %copy-start.1 = (bf16[2,32,256,256]{3,2,1,0:T(8,128)(2,1)S(1)}, bf16[2,32,256,256]{3,2,1,0:T(8,128)(2,1)}, u32[]{:S(2)}) copy-start(bf16[2,32,256,256]{3,2,1,0:T(8,128)(2,1)} %refs_8_.3) | copy-start | bytes 25165828
  15.6 0.8 copy-start.4
  16.3 0.8 copy-start.5
  19.9 25.5 %collective-permute-start.15 = (bf16[2,32,32,256]{3,2,1,0:T(8,128)(2,1)S(1)}, bf16[2,32,32,256]{3,2,1,0:T(8,128)(2,1)S(1)}, u32[]{:S(2)}, u32[]{:S(2)}) collective-permute-start(bf16[2,32,32,256]{3,2,1,0:T(8,128)(2,1)S(1)} %get-tuple-element.14), channel_id=1, source_target_pairs={{0,3},{1,2},{2,1},{3,0},{4,7},{5,6},{6,5},{7,4},{8,11},{9,10},{10,... | collective-permute-start | bytes 3145736 | tf_op jit(solution)/shard_map/ppermute | solution.py:40
  20.3 47.6 %collective-permute-start.19 = (bf16[2,32,32,256]{3,2,1,0:T(8,128)(2,1)S(1)}, bf16[2,32,32,256]{3,2,1,0:T(8,128)(2,1)S(1)}, u32[]{:S(2)}, u32[]{:S(2)}) collective-permute-start(bf16[2,32,32,256]{3,2,1,0:T(8,128)(2,1)S(1)} %get-tuple-element.16), channel_id=1, source_target_pairs={{0,5},{1,4},{2,7},{3,6},{4,1},{5,0},{6,3},{7,2},{8,13},{9,12},{10,... | collective-permute-start | bytes 3145736 | tf_op jit(solution)/shard_map/ppermute | solution.py:40
  27.3 54.3 %collective-permute-start.23 = (bf16[2,32,32,256]{3,2,1,0:T(8,128)(2,1)}, bf16[2,32,32,256]{3,2,1,0:T(8,128)(2,1)}, u32[]{:S(2)}, u32[]{:S(2)}) collective-permute-start(bf16[2,32,32,256]{3,2,1,0:T(8,128)(2,1)} %get-tuple-element.18), channel_id=1, source_target_pairs={{0,7},{1,6},{2,5},{3,4},{4,3},{5,2},{6,1},{7,0},{8,15},{9,14},{10,... | collective-permute-start | bytes 3145736 | tf_op jit(solution)/shard_map/ppermute | solution.py:40
  28.1 1.5 %collective-permute-start.8 = (bf16[2,32,256]{2,1,0:T(8,128)(2,1)S(1)}, bf16[2,32,256]{2,1,0:T(8,128)(2,1)S(1)}, u32[]{:S(2)}, u32[]{:S(2)}) collective-permute-start(bf16[2,32,256]{2,1,0:T(8,128)(2,1)S(1)} %copy-done.5), channel_id=1, source_target_pairs={{0,1},{1,0},{2,3},{3,2},{4,5},{5,4},{6,7},{7,6},{8,9},{9,8},{10,11... | collective-permute-start | bytes 98312 | tf_op jit(solution)/shard_map/ppermute | solution.py:40
  28.7 1.2 collective-permute-start.14
  29.6 38.2 %copy-start.9 = (bf16[2,32,256]{2,1,0:T(8,128)(2,1)}, bf16[2,32,256]{2,1,0:T(8,128)(2,1)S(1)}, u32[]{:S(2)}) copy-start(bf16[2,32,256]{2,1,0:T(8,128)(2,1)S(1)} %collective-permute-done.8.refs_1_) | copy-start | bytes 98308
  29.6 1.2 collective-permute-start.12
  29.9 37.9 %copy-start.10 = (bf16[2,32,256]{2,1,0:T(8,128)(2,1)}, bf16[2,32,256]{2,1,0:T(8,128)(2,1)S(1)}, u32[]{:S(2)}) copy-start(bf16[2,32,256]{2,1,0:T(8,128)(2,1)S(1)} %collective-permute-done.14.refs_7_) | copy-start | bytes 98308
  29.9 56.9 %collective-permute-start.26 = (bf16[2,32,32,256]{3,2,1,0:T(8,128)(2,1)}, bf16[2,32,32,256]{3,2,1,0:T(8,128)(2,1)}, u32[]{:S(2)}, u32[]{:S(2)}) collective-permute-start(bf16[2,32,32,256]{3,2,1,0:T(8,128)(2,1)} %get-tuple-element.20), channel_id=1, source_target_pairs={{0,1},{1,0},{2,3},{3,2},{4,5},{5,4},{6,7},{7,6},{8,9},{9,8},{10,11... | collective-permute-start | bytes 3145736 | tf_op jit(solution)/shard_map/ppermute | solution.py:40
  30.8 37.0 %copy-start.11 = (bf16[2,32,256]{2,1,0:T(8,128)(2,1)}, bf16[2,32,256]{2,1,0:T(8,128)(2,1)S(1)}, u32[]{:S(2)}) copy-start(bf16[2,32,256]{2,1,0:T(8,128)(2,1)S(1)} %collective-permute-done.12.refs_5_) | copy-start | bytes 98308
  30.8 1.8 %collective-permute-start.10 = (bf16[2,32,256]{2,1,0:T(8,128)(2,1)S(1)}, bf16[2,32,256]{2,1,0:T(8,128)(2,1)S(1)}, u32[]{:S(2)}, u32[]{:S(2)}) collective-permute-start(bf16[2,32,256]{2,1,0:T(8,128)(2,1)S(1)} %collective-permute-done.9.refs_2_.refs_11_), channel_id=1, source_target_pairs={{0,1},{1,0},{2,3},{3,2},{4,5},{5,4},{6,7},{7,6},{8,9},{9,8},{10,11... | collective-permute-start | bytes 98312 | tf_op jit(solution)/shard_map/ppermute | solution.py:40
  32.6 35.2 %copy-start.12 = (bf16[2,32,256]{2,1,0:T(8,128)(2,1)}, bf16[2,32,256]{2,1,0:T(8,128)(2,1)S(1)}, u32[]{:S(2)}) copy-start(bf16[2,32,256]{2,1,0:T(8,128)(2,1)S(1)} %collective-permute-done.10.refs_3_) | copy-start | bytes 98308
  32.6 59.6 %collective-permute-start.7 = (bf16[2,32,32,256]{3,2,1,0:T(8,128)(2,1)}, bf16[2,32,32,256]{3,2,1,0:T(8,128)(2,1)}, u32[]{:S(2)}, u32[]{:S(2)}) collective-permute-start(bf16[2,32,32,256]{3,2,1,0:T(8,128)(2,1)} %get-tuple-element.13), channel_id=1, source_target_pairs={{0,2},{1,3},{2,0},{3,1},{4,6},{5,7},{6,4},{7,5},{8,10},{9,11},{10,... | collective-permute-start | bytes 3145736 | tf_op jit(solution)/shard_map/ppermute | solution.py:40
  45.4 67.1 %collective-permute-start.18 = (bf16[2,32,32,256]{3,2,1,0:T(8,128)(2,1)}, bf16[2,32,32,256]{3,2,1,0:T(8,128)(2,1)}, u32[]{:S(2)}, u32[]{:S(2)}) collective-permute-start(bf16[2,32,32,256]{3,2,1,0:T(8,128)(2,1)} %get-tuple-element.15), channel_id=1, source_target_pairs={{0,4},{1,5},{2,6},{3,7},{4,0},{5,1},{6,2},{7,3},{8,12},{9,13},{10,... | collective-permute-start | bytes 3145736 | tf_op jit(solution)/shard_map/ppermute | solution.py:40
  67.8 52.1 %collective-permute-start.22 = (bf16[2,32,32,256]{3,2,1,0:T(8,128)(2,1)}, bf16[2,32,32,256]{3,2,1,0:T(8,128)(2,1)}, u32[]{:S(2)}, u32[]{:S(2)}) collective-permute-start(bf16[2,32,32,256]{3,2,1,0:T(8,128)(2,1)} %get-tuple-element.17), channel_id=1, source_target_pairs={{0,6},{1,7},{2,4},{3,5},{4,2},{5,3},{6,0},{7,1},{8,14},{9,15},{10,... | collective-permute-start | bytes 3145736 | tf_op jit(solution)/shard_map/ppermute | solution.py:40
  69.4 3.4 %copy-start = (bf16[2,32,256,256]{3,2,1,0:T(8,128)(2,1)S(1)}, bf16[2,32,256,256]{3,2,1,0:T(8,128)(2,1)}, u32[]{:S(2)}) copy-start(bf16[2,32,256,256]{3,2,1,0:T(8,128)(2,1)} %y_ref.15) | copy-start | bytes 25165828
  72.8 0.9 copy-start.2
  77.7 9.6 %slice-start = ((s8[8388608]{0:T(1024)(128)(4,1)}), s8[4194304]{0:T(1024)(128)(4,1)S(1)}, s32[]{:S(2)}) async-start(s8[8388608]{0:T(1024)(128)(4,1)} %bitcast.1), calls=%async_computation | async-start | bytes 8388608
  81.6 5.6 %slice-start.1 = ((s8[8388608]{0:T(1024)(128)(4,1)}), s8[4194304]{0:T(1024)(128)(4,1)S(1)}, s32[]{:S(2)}) async-start(s8[8388608]{0:T(1024)(128)(4,1)} %bitcast.1), calls=%async_computation.1 | async-start | bytes 8388608
  81.6 10.8 %collective-permute-start.16 = (f32[2,32,256]{2,1,0:T(8,128)S(1)}, f32[2,32,256]{2,1,0:T(8,128)S(1)}, u32[]{:S(2)}, u32[]{:S(2)}) collective-permute-start(f32[2,32,256]{2,1,0:T(8,128)S(1)} %last.8), channel_id=1, source_target_pairs={{0,1},{1,0},{2,3},{3,2},{4,5},{5,4},{6,7},{7,6},{8,9},{9,8},{10,11... | collective-permute-start | bytes 196616 | tf_op jit(solution)/shard_map/ppermute | solution.py:40
  86.8 25.7 %collective-permute-start.20 = (f32[2,32,256]{2,1,0:T(8,128)S(1)}, f32[2,32,256]{2,1,0:T(8,128)S(1)}, u32[]{:S(2)}, u32[]{:S(2)}) collective-permute-start(f32[2,32,256]{2,1,0:T(8,128)S(1)} %last.10), channel_id=1, source_target_pairs={{0,1},{1,0},{2,3},{3,2},{4,5},{5,4},{6,7},{7,6},{8,9},{9,8},{10,11... | collective-permute-start | bytes 196616 | tf_op jit(solution)/shard_map/ppermute | solution.py:40
  92.2 27.7 %collective-permute-start.24 = (f32[2,32,256]{2,1,0:T(8,128)S(1)}, f32[2,32,256]{2,1,0:T(8,128)S(1)}, u32[]{:S(2)}, u32[]{:S(2)}) collective-permute-start(f32[2,32,256]{2,1,0:T(8,128)S(1)} %last.12), channel_id=1, source_target_pairs={{0,1},{1,0},{2,3},{3,2},{4,5},{5,4},{6,7},{7,6},{8,9},{9,8},{10,11... | collective-permute-start | bytes 196616 | tf_op jit(solution)/shard_map/ppermute | solution.py:40
  92.5 34.2 %collective-permute-start.27 = (f32[2,32,256]{2,1,0:T(8,128)S(1)}, f32[2,32,256]{2,1,0:T(8,128)S(1)}, u32[]{:S(2)}, u32[]{:S(2)}) collective-permute-start(f32[2,32,256]{2,1,0:T(8,128)S(1)} %last.14), channel_id=1, source_target_pairs={{0,1},{1,0},{2,3},{3,2},{4,5},{5,4},{6,7},{7,6},{8,9},{9,8},{10,11... | collective-permute-start | bytes 196616 | tf_op jit(solution)/shard_map/ppermute | solution.py:40
  97.8 28.9 %copy-start.3 = (bf16[2,256,256]{2,1,0:T(8,128)(2,1)S(1)}, bf16[2,256,256]{2,1,0:T(8,128)(2,1)}, u32[]{:S(2)}) copy-start(bf16[2,256,256]{2,1,0:T(8,128)(2,1)} %join.1.right_ref) | copy-start | bytes 786436
  112.5 18.0 %collective-permute-start.17 = (f32[2,32,256]{2,1,0:T(8,128)S(1)}, f32[2,32,256]{2,1,0:T(8,128)S(1)}, u32[]{:S(2)}, u32[]{:S(2)}) collective-permute-start(f32[2,32,256]{2,1,0:T(8,128)S(1)} %last.9), channel_id=1, source_target_pairs={{0,2},{1,3},{2,0},{3,1},{4,6},{5,7},{6,4},{7,5},{8,10},{9,11},{10,... | collective-permute-start | bytes 196616 | tf_op jit(solution)/shard_map/ppermute | solution.py:40
  117.5 13.1 %collective-permute-start.21 = (f32[2,32,256]{2,1,0:T(8,128)S(1)}, f32[2,32,256]{2,1,0:T(8,128)S(1)}, u32[]{:S(2)}, u32[]{:S(2)}) collective-permute-start(f32[2,32,256]{2,1,0:T(8,128)S(1)} %last.11), channel_id=1, source_target_pairs={{0,4},{1,5},{2,6},{3,7},{4,0},{5,1},{6,2},{7,3},{8,12},{9,13},{10,... | collective-permute-start | bytes 196616 | tf_op jit(solution)/shard_map/ppermute | solution.py:40
  124.9 5.6 %collective-permute-start.25 = (f32[2,32,256]{2,1,0:T(8,128)S(1)}, f32[2,32,256]{2,1,0:T(8,128)S(1)}, u32[]{:S(2)}, u32[]{:S(2)}) collective-permute-start(f32[2,32,256]{2,1,0:T(8,128)S(1)} %last.13), channel_id=1, source_target_pairs={{0,6},{1,7},{2,4},{3,5},{4,2},{5,3},{6,0},{7,1},{8,14},{9,15},{10,... | collective-permute-start | bytes 196616 | tf_op jit(solution)/shard_map/ppermute | solution.py:40

commit v3 on v2

v3 whole, which is shorter than its diff:
```python
import functools

import jax
import jax.numpy as jnp
from jax import lax
from jax.experimental import pallas as pl
from jax.experimental.pallas import tpu as pltpu
from jax.sharding import PartitionSpec as P

AXIS = "cuts"
LIMIT = 20 * 1024 * 1024
LANES = 128


def plain(core_x, core_y, left_intersection, right_intersection):
    left_full = lax.all_gather(left_intersection, AXIS, axis=1, tiled=True)
    first = jnp.einsum(
        "pik,paij->pakj", left_full, core_x, preferred_element_type=jnp.float32
    ).astype(jnp.bfloat16)
    right_full = lax.all_gather(right_intersection, AXIS, axis=1, tiled=True)
    moved = lax.all_to_all(
        jnp.einsum("pakj,pjl->pakl", first, right_full, preferred_element_type=jnp.float32).astype(
            jnp.bfloat16
        ),
        AXIS,
        split_axis=2,
        concat_axis=1,
        tiled=True,
    )
    mine = lax.psum_scatter(
        jnp.einsum("pakl,pklb->apb", moved, core_y, preferred_element_type=jnp.float32),
        AXIS,
        scatter_dimension=0,
        tiled=True,
    )
    return jnp.transpose(mine, (1, 0, 2))


def swap(value, mask, n):
    return lax.ppermute(value, AXIS, [(i, i ^ mask) for i in range(n)])


def gather_rows(value, n):
    even = {mask: swap(value, mask, n) for mask in range(n - 2, 0, -2)}
    even[0] = value
    rows = [None] * n
    for mask, came in even.items():
        rows[mask], rows[mask + 1] = came, swap(came, 1, n)
    return rows


def stage_kernel(x_ref, out_ref, sems):
    parents, count = sems.shape
    step = x_ref.shape[1] // count
    copies = [
        pltpu.make_async_copy(
            x_ref.at[p, pl.ds(c * step, step)], out_ref.at[p, pl.ds(c * step, step)], sems.at[p, c]
        )
        for p in range(parents)
        for c in range(count)
    ]
    for copy in copies:
        copy.start()
    for copy in copies:
        copy.wait()


def staged(core):
    return pl.pallas_call(
        stage_kernel,
        in_specs=[pl.BlockSpec(memory_space=pl.ANY)],
        out_specs=pl.BlockSpec(memory_space=pl.ANY),
        out_shape=jax.ShapeDtypeStruct(core.shape, core.dtype),
        scratch_shapes=[pltpu.SemaphoreType.DMA((core.shape[0], 4))],
        compiler_params=pltpu.CompilerParams(vmem_limit_bytes=LIMIT),
        cost_estimate=pl.CostEstimate(flops=0, bytes_accessed=4 * core.size, transcendentals=0),
        name="stage",
    )(core)


def at_rows(me, mask, rows):
    return pl.ds(pl.multiple_of((me ^ mask) * rows, rows), rows)


def choose(me, masks, pieces, full, turned, chosen):
    rows = chosen.shape[0] // len(masks)
    for m, piece in enumerate(pieces):
        full[at_rows(me, m, rows), :] = piece[0, :rows]
    turned[...] = full[...].T
    for slot, m in enumerate(masks):
        chosen[slot * rows : (slot + 1) * rows, :] = turned[at_rows(me, m, rows), :]


def apply_right(first, right, second, flat_ref, count, rows):
    width = right.shape[1]
    whole = jnp.dot(first, right, preferred_element_type=jnp.float32)
    for h in range(width // LANES):
        second[h] = whole[:, h * LANES : (h + 1) * LANES]
    for k in range(rows):
        for h in range(width // LANES):
            flat_ref[:, k * width + h * LANES : k * width + (h + 1) * LANES] = second[
                h, pl.ds(k, count, stride=rows), :
            ].astype(jnp.bfloat16)


def first_kernel(n, masks, me_ref, *refs):
    pieces, x_ref = refs[:n], refs[n]
    outs, (full, turned, chosen) = refs[n + 1 : n + 1 + len(masks)], refs[-3:]
    parent, chunk = pl.program_id(0), pl.program_id(1)
    step, rows = outs[0].shape[1], outs[0].shape[2]

    @pl.when(chunk == 0)
    def _():
        choose(me_ref[0], masks, pieces, full, turned, chosen)

    for a in range(step):
        product = jnp.dot(
            chosen[...], x_ref[parent, chunk * step + a], preferred_element_type=jnp.float32
        ).astype(jnp.bfloat16)
        for slot, out in enumerate(outs):
            out[0, a] = product[slot * rows : (slot + 1) * rows, :]


def first_for(me, pieces, core_x, masks):
    n = len(pieces)
    parents, mine, left, right = core_x.shape
    rows = left // n
    step = min(8, mine)
    return pl.pallas_call(
        functools.partial(first_kernel, n, masks),
        grid=(parents, mine // step),
        in_specs=[pl.BlockSpec(memory_space=pltpu.SMEM)]
        + [pl.BlockSpec((1, 2 * rows, left), lambda p, c: (p, 0, 0))] * n
        + [pl.BlockSpec(memory_space=pltpu.VMEM)],
        out_specs=[pl.BlockSpec((1, step, rows, right), lambda p, c: (p, c, 0, 0))] * len(masks),
        out_shape=[jax.ShapeDtypeStruct((parents, mine, rows, right), jnp.bfloat16)] * len(masks),
        scratch_shapes=[
            pltpu.VMEM((left, left), jnp.bfloat16),
            pltpu.VMEM((left, left), jnp.bfloat16),
            pltpu.VMEM((rows * len(masks), left), jnp.bfloat16),
        ],
        compiler_params=pltpu.CompilerParams(vmem_limit_bytes=LIMIT),
        cost_estimate=pl.CostEstimate(
            flops=2 * parents * mine * rows * len(masks) * left * right,
            bytes_accessed=2 * parents * mine * right * (left + rows * len(masks)),
            transcendentals=0,
        ),
        name="first",
    )(me, *pieces, core_x)


def second_kernel(n, masks, me_ref, *refs):
    pieces, x_ref = refs[:n], refs[n]
    outs, (full, turned, chosen, first, second) = refs[-5 - len(masks) : -5], refs[-5:]
    parent = pl.program_id(0)
    mine, rows = outs[0].shape[1], pieces[0].shape[1] // 2
    choose(me_ref[0], masks, pieces, full, turned, chosen)
    for m, piece in enumerate(pieces):
        full[at_rows(me_ref[0], m, rows), :] = piece[0, rows:]
    for a in range(mine):
        product = jnp.dot(chosen[...], x_ref[parent, a], preferred_element_type=jnp.float32).astype(jnp.bfloat16)
        for slot in range(len(masks)):
            first[slot, a * rows : (a + 1) * rows, :] = product[slot * rows : (slot + 1) * rows, :]
    for slot, out in enumerate(outs):
        apply_right(first[slot], full[...], second, out.at[0], mine, rows)


def second_for(me, pieces, core_x, masks, after):
    n = len(pieces)
    parents, mine, left, right = core_x.shape
    rows = left // n
    return pl.pallas_call(
        functools.partial(second_kernel, n, masks),
        grid=(parents,),
        in_specs=[pl.BlockSpec(memory_space=pltpu.SMEM)]
        + [pl.BlockSpec((1, 2 * rows, left), lambda p: (p, 0, 0))] * n
        + [pl.BlockSpec(memory_space=pltpu.VMEM), pl.BlockSpec(memory_space=pl.ANY)],
        out_specs=[pl.BlockSpec((1, mine, rows * right), lambda p: (p, 0, 0))] * len(masks),
        out_shape=[jax.ShapeDtypeStruct((parents, mine, rows * right), jnp.bfloat16)] * len(masks),
        scratch_shapes=[
            pltpu.VMEM((left, left), jnp.bfloat16),
            pltpu.VMEM((left, left), jnp.bfloat16),
            pltpu.VMEM((rows * len(masks), left), jnp.bfloat16),
            pltpu.VMEM((len(masks), mine * rows, right), jnp.bfloat16),
            pltpu.VMEM((right // LANES, mine * rows, LANES), jnp.float32),
        ],
        compiler_params=pltpu.CompilerParams(vmem_limit_bytes=LIMIT),
        cost_estimate=pl.CostEstimate(
            flops=2 * parents * mine * rows * len(masks) * right * (left + right),
            bytes_accessed=2 * parents * mine * right * (left + rows * len(masks)),
            transcendentals=0,
        ),
        name="second",
    )(me, *pieces, core_x, after)


def join_kernel(n, me_ref, *refs):
    pieces, out = refs[:n], refs[n]
    rows = pieces[0].shape[1] // 2
    for m in range(n):
        out[:, at_rows(me_ref[0], m, rows), :] = pieces[m][:, rows:]


def join_right(me, pieces):
    n = len(pieces)
    parents, rows, width = pieces[0].shape
    return pl.pallas_call(
        functools.partial(join_kernel, n),
        in_specs=[pl.BlockSpec(memory_space=pltpu.SMEM)] + [pl.BlockSpec(memory_space=pltpu.VMEM)] * n,
        out_specs=pl.BlockSpec(memory_space=pltpu.VMEM),
        out_shape=jax.ShapeDtypeStruct((parents, n * rows // 2, width), pieces[0].dtype),
        compiler_params=pltpu.CompilerParams(vmem_limit_bytes=LIMIT),
        cost_estimate=pl.CostEstimate(flops=0, bytes_accessed=2 * parents * n * rows * width, transcendentals=0),
        name="join",
    )(me, *pieces)


def last_kernel(held, right_given, came_ref, y_ref, *refs):
    begin_ref = refs[0] if held else None
    parent = pl.program_id(0)
    depth = y_ref.shape[1] * y_ref.shape[2]
    if right_given:
        right_ref, out_ref, second, flat = refs[-4:]
        count, rows = came_ref.shape[1], came_ref.shape[2]
        apply_right(
            came_ref[0].reshape(count * rows, came_ref.shape[3]), right_ref[0], second, flat, count, rows
        )
        wide = flat[...]
    else:
        out_ref = refs[-1]
        wide = came_ref[0]
    total = jnp.dot(wide, y_ref[parent].reshape(depth, y_ref.shape[3]), preferred_element_type=jnp.float32)
    out_ref[0] = total + begin_ref[0] if held else total


def last_for(came, core_y, begin=None, right=None):
    parents, rows, width, out_width = core_y.shape
    count = came.shape[1]
    row = pl.BlockSpec((1, count, out_width), lambda p: (p, 0, 0))
    zeros = (0,) * (came.ndim - 1)
    given = [came, core_y]
    specs = [
        pl.BlockSpec((1,) + came.shape[1:], lambda p: (p,) + zeros),
        pl.BlockSpec(memory_space=pltpu.VMEM),
    ]
    scratch = []
    if begin is not None:
        given, specs = given + [begin], specs + [row]
    if right is not None:
        given, specs = given + [right], specs + [pl.BlockSpec((1,) + right.shape[1:], lambda p: (p, 0, 0))]
        scratch = [
            pltpu.VMEM((width // LANES, count * rows, LANES), jnp.float32),
            pltpu.VMEM((count, rows * width), jnp.bfloat16),
        ]
    return pl.pallas_call(
        functools.partial(last_kernel, begin is not None, right is not None),
        grid=(parents,),
        in_specs=specs,
        out_specs=row,
        out_shape=jax.ShapeDtypeStruct((parents, count, out_width), jnp.float32),
        scratch_shapes=scratch,
        compiler_params=pltpu.CompilerParams(vmem_limit_bytes=LIMIT),
        cost_estimate=pl.CostEstimate(
            flops=2 * parents * count * rows * width * (out_width + (width if scratch else 0)),
            bytes_accessed=2 * parents * rows * width * (count + out_width),
            transcendentals=0,
        ),
        name="last",
    )(*given)


def exchanged(core_x, core_y, left_intersection, right_intersection, n):
    me = lax.axis_index(AXIS).astype(jnp.int32).reshape(1)
    pairs = list(range(2, n, 2))
    pieces = gather_rows(jnp.concatenate([left_intersection, right_intersection], axis=1), n)
    core_x = staged(core_x)
    early = [mask + 1 for mask in pairs[:2]]
    sent = dict(zip(early, first_for(me, pieces, core_x, early)))
    came = {mask: swap(sent[mask], mask, n) for mask in early}
    after = sent[early[0]]
    for masks in [pairs[:2]] + [[mask + 1, mask] for mask in pairs[2:]] + [[1, 0]]:
        sent.update(zip(masks, second_for(me, pieces, core_x, masks, after)))
        after = sent[masks[0]]
        for mask in masks:
            came[mask] = swap(sent[mask], mask, n) if mask else sent[0]
    right = join_right(me, pieces)
    total = []
    for mask in pairs + [0]:
        odd = last_for(came[mask + 1], core_y, right=right if mask + 1 in early else None)
        part = last_for(came[mask], core_y, begin=swap(odd, 1, n))
        total.append(swap(part, mask, n) if mask else part)
    return sum(total[1:], total[0])


def solution(mesh):
    n = mesh.shape[AXIS]

    def shards(core_x, core_y, left_intersection, right_intersection):
        rows = left_intersection.shape[1]
        fits = n >= 4 and n & (n - 1) == 0 and rows % 16 == 0 and core_x.shape[1] % 8 == 0 and core_x.shape[3] % LANES == 0
        if not fits:
            return plain(core_x, core_y, left_intersection, right_intersection)
        return exchanged(core_x, core_y, left_intersection, right_intersection, n)

    return jax.shard_map(
        shards,
        mesh=mesh,
        in_specs=(
            P("node", AXIS, None, None),
            P("node", AXIS, None, None),
            P("node", AXIS, None),
            P("node", AXIS, None),
        ),
        out_specs=P("node", AXIS, None),
        check_vma=False,
    )
```

time: 132 us -> 120 us (0.909)
  Pallas kernels: 46.4 us -> 38.6 us
  waiting for transfers between devices: 52.4 us -> 58.7 us
  starting transfers between devices: 22.3 us -> 16.4 us
  local copies, waits for them, and re-layouts: 9.27 us -> 4.91 us
    ppermute x28 -> x21, waiting for transfers between devices: 52.4 us -> 58.7 us  [swap(): return lax.ppermute(value, AXIS, [(i, i ^ mask) for i in range(n)])]
    ppermute x28 -> x21, starting transfers between devices: 22.3 us -> 16.4 us  [swap(): return lax.ppermute(value, AXIS, [(i, i ^ mask) for i in range(n)])]
    pallas_call x2 -> x1, Pallas kernels: 8.2 us -> 2.85 us  [first_for(): pl.pallas_call(functools.partial(first_kernel, n, masks), grid=(parents,...]
    unnamed x30 -> x7, local copies, waits for them, and re-layouts: 9.27 us -> 4.15 us
    pallas_call x9 -> x13, Pallas kernels: 38.2 us -> 35.8 us  [the longest x8 17.8 us: last_for(): pl.pallas_call(functools.partial(last_kernel, begin is not None, right is...]
  transfers between devices with their start and end apart: 28 -> 21, of which waited for: 8 -> 8; matrix products, arithmetic and copies ran while one was open for 0% -> 0% of each run, Pallas kernels for 33% -> 30%
where the time goes in v3:
time: 120 us; the launch traced here: 119 us
  waiting for transfers between devices  58.7 us (49%)
  Pallas kernels  38.6 us (32%)
  starting transfers between devices  16.4 us (14%)
  local copies, waits for them, and re-layouts  4.91 us (4%)
    ppermute x21, waiting for transfers between devices, swap(): return lax.ppermute(value, AXIS, [(i, i ^ mask) for i in range(n)])  58.7 us
    pallas_call x8, Pallas kernels, last_for(): pl.pallas_call(functools.partial(last_kernel, begin is not None, right is...  17.8 us
    pallas_call x3, Pallas kernels, second_for(): pl.pallas_call(functools.partial(second_kernel, n, masks), grid=(parents,...  17.3 us
    ppermute x21, starting transfers between devices, swap(): return lax.ppermute(value, AXIS, [(i, i ^ mask) for i in range(n)])  16.4 us
    unnamed x7, local copies, waits for them, and re-layouts  4.15 us
    pallas_call x1, Pallas kernels, first_for(): pl.pallas_call(functools.partial(first_kernel, n, masks), grid=(parents,...  2.85 us
  transfers between devices with their start and end apart: 21, of which 8 were waited for; matrix products, arithmetic and copies ran while one was open for 0% of the time, Pallas kernels for 30%

profile of v3, /device:TPU:0, one launch (start us, length us, event | category | flops | bytes accessed | tf_op | source)
XLA Modules:
  0.0 119.5 jit_solution(13659082533411130737)
XLA Ops:
  0.0 0.8 constant_dynamic-update-slice_fusion.1
  0.8 0.8 constant_dynamic-update-slice_fusion.refs_0_
  1.5 3.9 %collective-permute-start.5 = (bf16[2,64,256]{2,1,0:T(8,128)(2,1)S(1)}, bf16[2,64,256]{2,1,0:T(8,128)(2,1)S(1)}, u32[]{:S(2)}, u32[]{:S(2)}) collective-permute-start(bf16[2,64,256]{2,1,0:T(8,128)(2,1)S(1)} %constant_dynamic-update-slice_fusion.refs_0_), channel_id=1, source_target_pairs={{0,6},{1,7},{2,4},{3,5},{4,2},{5,3},{6,0},{7,1},{8,14},{9,15},{10,... | collective-permute-start | bytes 196616 | tf_op jit(solution)/shard_map/ppermute | solution.py:40
  5.4 0.5 collective-permute-start.3
  5.9 0.1 collective-permute-start.1
  6.0 1.7 %collective-permute-done.5.refs_6_ = bf16[2,64,256]{2,1,0:T(8,128)(2,1)S(1)} collective-permute-done((bf16[2,64,256]{2,1,0:T(8,128)(2,1)S(1)}, bf16[2,64,256]{2,1,0:T(8,128)(2,1)S(1)}, u32[]{:S(2)}, u32[]{:S(2)}) %collective-permute-start.5) | collective-permute-done | bytes 65568 | tf_op jit(solution)/shard_map/ppermute | solution.py:40
  7.7 2.0 %collective-permute-done.3.refs_4_ = bf16[2,64,256]{2,1,0:T(8,128)(2,1)S(1)} collective-permute-done((bf16[2,64,256]{2,1,0:T(8,128)(2,1)S(1)}, bf16[2,64,256]{2,1,0:T(8,128)(2,1)S(1)}, u32[]{:S(2)}, u32[]{:S(2)}) %collective-permute-start.3) | collective-permute-done | bytes 65568 | tf_op jit(solution)/shard_map/ppermute | solution.py:40
  9.7 0.5 collective-permute-done.1.refs_2_
  10.2 0.0 collective-permute-start.2
  10.2 3.4 %copy-done = bf16[2,32,256,256]{3,2,1,0:T(8,128)(2,1)S(1)} copy-done((bf16[2,32,256,256]{3,2,1,0:T(8,128)(2,1)S(1)}, bf16[2,32,256,256]{3,2,1,0:T(8,128)(2,1)}, u32[]{:S(2)}) %copy-start) | copy-done | bytes 8388632
  13.6 0.6 stage.1.refs_8_
  14.3 2.8 %first.1 = (bf16[2,32,32,256]{3,2,1,0:T(8,128)(2,1)S(1)}, bf16[2,32,32,256]{3,2,1,0:T(8,128)(2,1)S(1)}) custom-call(s32[1]{0:T(128)} %bitcast.me_ref, bf16[2,64,256]{2,1,0:T(8,128)(2,1)S(1)} %constant_dynamic-update-slice_fusion.refs_0_, bf16[2,64,256]{2,1,0:T(8,128)(2,1)S(1)} %collective-permute-done.refs_1_, ...), custom_call_target="tpu_custom_call" | custom-call | flops 536870912 | bytes 10485760 | tf_op jit(solution)/shard_map/first/pallas_call | solution.py:129
  17.1 1.7 %collective-permute-start.12 = (bf16[2,32,32,256]{3,2,1,0:T(8,128)(2,1)S(1)}, bf16[2,32,32,256]{3,2,1,0:T(8,128)(2,1)S(1)}, u32[]{:S(2)}, u32[]{:S(2)}) collective-permute-start(bf16[2,32,32,256]{3,2,1,0:T(8,128)(2,1)S(1)} %get-tuple-element.16), channel_id=1, source_target_pairs={{0,5},{1,4},{2,7},{3,6},{4,1},{5,0},{6,3},{7,2},{8,13},{9,12},{10,... | collective-permute-start | bytes 3145736 | tf_op jit(solution)/shard_map/ppermute | solution.py:40
  18.8 0.1 collective-permute-start.8
  19.0 5.8 %second.3 = (bf16[2,32,8192]{2,1,0:T(8,128)(2,1)S(1)}, bf16[2,32,8192]{2,1,0:T(8,128)(2,1)S(1)}) custom-call(s32[1]{0:T(128)} %bitcast.me_ref, bf16[2,64,256]{2,1,0:T(8,128)(2,1)S(1)} %constant_dynamic-update-slice_fusion.refs_0_, bf16[2,64,256]{2,1,0:T(8,128)(2,1)S(1)} %collective-permute-done.refs_1_, ...), custom_call_target="tpu_custom_call" | custom-call | flops 1073741824 | bytes 10485760 | tf_op jit(solution)/shard_map/second/pallas_call | solution.py:172
  24.7 0.9 collective-permute-start.11
  25.7 5.8 %second.4 = (bf16[2,32,8192]{2,1,0:T(8,128)(2,1)S(1)}, bf16[2,32,8192]{2,1,0:T(8,128)(2,1)S(1)}) custom-call(s32[1]{0:T(128)} %bitcast.me_ref, bf16[2,64,256]{2,1,0:T(8,128)(2,1)S(1)} %constant_dynamic-update-slice_fusion.refs_0_, bf16[2,64,256]{2,1,0:T(8,128)(2,1)S(1)} %collective-permute-done.refs_1_, ...), custom_call_target="tpu_custom_call" | custom-call | flops 1073741824 | bytes 10485760 | tf_op jit(solution)/shard_map/second/pallas_call | solution.py:172
  31.5 0.0 slice-start.1
  31.5 2.0 %collective-permute-start.16 = (bf16[2,32,8192]{2,1,0:T(8,128)(2,1)S(1)}, bf16[2,32,8192]{2,1,0:T(8,128)(2,1)S(1)}, u32[]{:S(2)}, u32[]{:S(2)}) collective-permute-start(bf16[2,32,8192]{2,1,0:T(8,128)(2,1)S(1)} %get-tuple-element.18.refs_9_), channel_id=1, source_target_pairs={{0,7},{1,6},{2,5},{3,4},{4,3},{5,2},{6,1},{7,0},{8,15},{9,14},{10,... | collective-permute-start | bytes 3145736 | tf_op jit(solution)/shard_map/ppermute | solution.py:40
  33.4 5.8 %second.5 = (bf16[2,32,8192]{2,1,0:T(8,128)(2,1)S(1)}, bf16[2,32,8192]{2,1,0:T(8,128)(2,1)S(1)}) custom-call(s32[1]{0:T(128)} %bitcast.me_ref, bf16[2,64,256]{2,1,0:T(8,128)(2,1)S(1)} %constant_dynamic-update-slice_fusion.refs_0_, bf16[2,64,256]{2,1,0:T(8,128)(2,1)S(1)} %collective-permute-done.refs_1_, ...), custom_call_target="tpu_custom_call" | custom-call | flops 1073741824 | bytes 10485760 | tf_op jit(solution)/shard_map/second/pallas_call | solution.py:172
  39.2 0.4 collective-permute-start.19
  39.6 2.8 %collective-permute-done.12.came_ref = bf16[2,32,32,256]{3,2,1,0:T(8,128)(2,1)S(1)} collective-permute-done((bf16[2,32,32,256]{3,2,1,0:T(8,128)(2,1)S(1)}, bf16[2,32,32,256]{3,2,1,0:T(8,128)(2,1)S(1)}, u32[]{:S(2)}, u32[]{:S(2)}) %collective-permute-start.12) | collective-permute-done | bytes 1048608 | tf_op jit(solution)/shard_map/ppermute | solution.py:40
  42.3 1.0 collective-permute-start.7
  43.3 0.8 collective-permute-done.8.came_ref
  44.1 0.9 collective-permute-start.15
  45.1 3.9 %last.10 = f32[2,32,256]{2,1,0:T(8,128)S(1)} custom-call(bf16[2,32,32,256]{3,2,1,0:T(8,128)(2,1)S(1)} %collective-permute-done.12.came_ref, bf16[2,32,256,256]{3,2,1,0:T(8,128)(2,1)S(1)} %bitcast.2, bf16[2,256,256]{2,1,0:T(8,128)(2,1)S(1)} %join.1.refs_0_), custom_call_target="tpu_custom_call" | custom-call | flops 536870912 | bytes 9437184 | tf_op jit(solution)/shard_map/last/pallas_call | solution.py:255
  49.0 38.6 %collective-permute-done.11.came_ref = bf16[2,32,8192]{2,1,0:T(8,128)(2,1)S(1)} collective-permute-done((bf16[2,32,8192]{2,1,0:T(8,128)(2,1)S(1)}, bf16[2,32,8192]{2,1,0:T(8,128)(2,1)S(1)}, u32[]{:S(2)}, u32[]{:S(2)}) %collective-permute-start.11) | collective-permute-done | bytes 1048608 | tf_op jit(solution)/shard_map/ppermute | solution.py:40
  87.6 3.9 %last.8 = f32[2,32,256]{2,1,0:T(8,128)S(1)} custom-call(bf16[2,32,32,256]{3,2,1,0:T(8,128)(2,1)S(1)} %collective-permute-done.8.came_ref, bf16[2,32,256,256]{3,2,1,0:T(8,128)(2,1)S(1)} %bitcast.2, bf16[2,256,256]{2,1,0:T(8,128)(2,1)S(1)} %join.1.refs_0_), custom_call_target="tpu_custom_call" | custom-call | flops 536870912 | bytes 9437184 | tf_op jit(solution)/shard_map/last/pallas_call | solution.py:255
  91.5 0.0 collective-permute-done.16.came_ref
  91.5 0.6 collective-permute-start.9
  92.1 1.7 %last.12 = f32[2,32,256]{2,1,0:T(8,128)S(1)} custom-call(bf16[2,32,8192]{2,1,0:T(8,128)(2,1)S(1)} %collective-permute-done.16.came_ref, bf16[2,32,256,256]{3,2,1,0:T(8,128)(2,1)S(1)} %bitcast.2), custom_call_target="tpu_custom_call" | custom-call | flops 268435456 | bytes 9437184 | tf_op jit(solution)/shard_map/last/pallas_call | solution.py:255
  93.8 0.0 collective-permute-done.19.came_ref
  93.8 0.1 collective-permute-start.17
  93.9 1.7 %last.14 = f32[2,32,256]{2,1,0:T(8,128)S(1)} custom-call(bf16[2,32,8192]{2,1,0:T(8,128)(2,1)S(1)} %collective-permute-done.19.came_ref, bf16[2,32,256,256]{3,2,1,0:T(8,128)(2,1)S(1)} %bitcast.2), custom_call_target="tpu_custom_call" | custom-call | flops 268435456 | bytes 9437184 | tf_op jit(solution)/shard_map/last/pallas_call | solution.py:255
  95.6 0.0 collective-permute-done.13.refs_0_
  95.6 0.5 collective-permute-start.20
  96.1 1.7 %last.11 = f32[2,32,256]{2,1,0:T(8,128)S(1)} custom-call(bf16[2,32,8192]{2,1,0:T(8,128)(2,1)S(1)} %collective-permute-done.11.came_ref, bf16[2,32,256,256]{3,2,1,0:T(8,128)(2,1)S(1)} %bitcast.2, f32[2,32,256]{2,1,0:T(8,128)S(1)} %collective-permute-done.13.refs_0_), custom_call_target="tpu_custom_call" | custom-call | flops 268435456 | bytes 9437184 | tf_op jit(solution)/shard_map/last/pallas_call | solution.py:255
  97.8 0.0 collective-permute-done.7.came_ref
  97.8 1.6 %collective-permute-start.14 = (f32[2,32,256]{2,1,0:T(8,128)S(1)}, f32[2,32,256]{2,1,0:T(8,128)S(1)}, u32[]{:S(2)}, u32[]{:S(2)}) collective-permute-start(f32[2,32,256]{2,1,0:T(8,128)S(1)} %last.11), channel_id=1, source_target_pairs={{0,4},{1,5},{2,6},{3,7},{4,0},{5,1},{6,2},{7,3},{8,12},{9,13},{10,... | collective-permute-start | bytes 196616 | tf_op jit(solution)/shard_map/ppermute | solution.py:40
  99.4 1.7 %last.9 = f32[2,32,256]{2,1,0:T(8,128)S(1)} custom-call(bf16[2,32,8192]{2,1,0:T(8,128)(2,1)S(1)} %collective-permute-done.7.came_ref, bf16[2,32,256,256]{3,2,1,0:T(8,128)(2,1)S(1)} %bitcast.2, f32[2,32,256]{2,1,0:T(8,128)S(1)} %collective-permute-done.9.refs_0_), custom_call_target="tpu_custom_call" | custom-call | flops 268435456 | bytes 9437184 | tf_op jit(solution)/shard_map/last/pallas_call | solution.py:255
  101.1 0.6 collective-permute-start.10
  101.6 10.3 %collective-permute-done.15.came_ref = bf16[2,32,8192]{2,1,0:T(8,128)(2,1)S(1)} collective-permute-done((bf16[2,32,8192]{2,1,0:T(8,128)(2,1)S(1)}, bf16[2,32,8192]{2,1,0:T(8,128)(2,1)S(1)}, u32[]{:S(2)}, u32[]{:S(2)}) %collective-permute-start.15) | collective-permute-done | bytes 1048608 | tf_op jit(solution)/shard_map/ppermute | solution.py:40
  111.9 1.7 %last.13 = f32[2,32,256]{2,1,0:T(8,128)S(1)} custom-call(bf16[2,32,8192]{2,1,0:T(8,128)(2,1)S(1)} %collective-permute-done.15.came_ref, bf16[2,32,256,256]{3,2,1,0:T(8,128)(2,1)S(1)} %bitcast.2, f32[2,32,256]{2,1,0:T(8,128)S(1)} %collective-permute-done.17.refs_0_), custom_call_target="tpu_custom_call" | custom-call | flops 268435456 | bytes 9437184 | tf_op jit(solution)/shard_map/last/pallas_call | solution.py:255
  113.6 1.5 %collective-permute-start.18 = (f32[2,32,256]{2,1,0:T(8,128)S(1)}, f32[2,32,256]{2,1,0:T(8,128)S(1)}, u32[]{:S(2)}, u32[]{:S(2)}) collective-permute-start(f32[2,32,256]{2,1,0:T(8,128)S(1)} %last.13), channel_id=1, source_target_pairs={{0,6},{1,7},{2,4},{3,5},{4,2},{5,3},{6,0},{7,1},{8,14},{9,15},{10,... | collective-permute-start | bytes 196616 | tf_op jit(solution)/shard_map/ppermute | solution.py:40
  115.1 1.6 %last.15 = f32[2,32,256]{2,1,0:T(8,128)S(1)} custom-call(bf16[2,32,8192]{2,1,0:T(8,128)(2,1)S(1)} %get-tuple-element.19.came_ref, bf16[2,32,256,256]{3,2,1,0:T(8,128)(2,1)S(1)} %bitcast.2, f32[2,32,256]{2,1,0:T(8,128)S(1)} %collective-permute-done.20.refs_0_), custom_call_target="tpu_custom_call" | custom-call | flops 268435456 | bytes 9437184 | tf_op jit(solution)/shard_map/last/pallas_call | solution.py:255
  116.8 0.0 collective-permute-done.14
  116.8 2.0 %collective-permute-done.18 = f32[2,32,256]{2,1,0:T(8,128)S(1)} collective-permute-done((f32[2,32,256]{2,1,0:T(8,128)S(1)}, f32[2,32,256]{2,1,0:T(8,128)S(1)}, u32[]{:S(2)}, u32[]{:S(2)}) %collective-permute-start.18) | collective-permute-done | bytes 65568 | tf_op jit(solution)/shard_map/ppermute | solution.py:40
  118.8 0.6 add_add_fusion
  (18 shorter events, 0.1 us)
Async XLA Ops:
  1.5 6.1 %collective-permute-start.5 = (bf16[2,64,256]{2,1,0:T(8,128)(2,1)S(1)}, bf16[2,64,256]{2,1,0:T(8,128)(2,1)S(1)}, u32[]{:S(2)}, u32[]{:S(2)}) collective-permute-start(bf16[2,64,256]{2,1,0:T(8,128)(2,1)S(1)} %constant_dynamic-update-slice_fusion.refs_0_), channel_id=1, source_target_pairs={{0,6},{1,7},{2,4},{3,5},{4,2},{5,3},{6,0},{7,1},{8,14},{9,15},{10,... | collective-permute-start | bytes 196616 | tf_op jit(solution)/shard_map/ppermute | solution.py:40
  5.4 4.3 %collective-permute-start.3 = (bf16[2,64,256]{2,1,0:T(8,128)(2,1)S(1)}, bf16[2,64,256]{2,1,0:T(8,128)(2,1)S(1)}, u32[]{:S(2)}, u32[]{:S(2)}) collective-permute-start(bf16[2,64,256]{2,1,0:T(8,128)(2,1)S(1)} %constant_dynamic-update-slice_fusion.refs_0_), channel_id=1, source_target_pairs={{0,4},{1,5},{2,6},{3,7},{4,0},{5,1},{6,2},{7,3},{8,12},{9,13},{10,... | collective-permute-start | bytes 196616 | tf_op jit(solution)/shard_map/ppermute | solution.py:40
  5.9 4.3 %collective-permute-start.1 = (bf16[2,64,256]{2,1,0:T(8,128)(2,1)S(1)}, bf16[2,64,256]{2,1,0:T(8,128)(2,1)S(1)}, u32[]{:S(2)}, u32[]{:S(2)}) collective-permute-start(bf16[2,64,256]{2,1,0:T(8,128)(2,1)S(1)} %constant_dynamic-update-slice_fusion.refs_0_), channel_id=1, source_target_pairs={{0,2},{1,3},{2,0},{3,1},{4,6},{5,7},{6,4},{7,5},{8,10},{9,11},{10,... | collective-permute-start | bytes 196616 | tf_op jit(solution)/shard_map/ppermute | solution.py:40
  6.0 8.3 %collective-permute-start = (bf16[2,64,256]{2,1,0:T(8,128)(2,1)S(1)}, bf16[2,64,256]{2,1,0:T(8,128)(2,1)S(1)}, u32[]{:S(2)}, u32[]{:S(2)}) collective-permute-start(bf16[2,64,256]{2,1,0:T(8,128)(2,1)S(1)} %constant_dynamic-update-slice_fusion.refs_0_), channel_id=1, source_target_pairs={{0,1},{1,0},{2,3},{3,2},{4,5},{5,4},{6,7},{7,6},{8,9},{9,8},{10,11... | collective-permute-start | bytes 196616 | tf_op jit(solution)/shard_map/ppermute | solution.py:40
  7.7 6.6 %collective-permute-start.6 = (bf16[2,64,256]{2,1,0:T(8,128)(2,1)S(1)}, bf16[2,64,256]{2,1,0:T(8,128)(2,1)S(1)}, u32[]{:S(2)}, u32[]{:S(2)}) collective-permute-start(bf16[2,64,256]{2,1,0:T(8,128)(2,1)S(1)} %collective-permute-done.5.refs_6_), channel_id=1, source_target_pairs={{0,1},{1,0},{2,3},{3,2},{4,5},{5,4},{6,7},{7,6},{8,9},{9,8},{10,11... | collective-permute-start | bytes 196616 | tf_op jit(solution)/shard_map/ppermute | solution.py:40
  9.7 4.6 %collective-permute-start.4 = (bf16[2,64,256]{2,1,0:T(8,128)(2,1)S(1)}, bf16[2,64,256]{2,1,0:T(8,128)(2,1)S(1)}, u32[]{:S(2)}, u32[]{:S(2)}) collective-permute-start(bf16[2,64,256]{2,1,0:T(8,128)(2,1)S(1)} %collective-permute-done.3.refs_4_), channel_id=1, source_target_pairs={{0,1},{1,0},{2,3},{3,2},{4,5},{5,4},{6,7},{7,6},{8,9},{9,8},{10,11... | collective-permute-start | bytes 196616 | tf_op jit(solution)/shard_map/ppermute | solution.py:40
  10.2 4.1 %collective-permute-start.2 = (bf16[2,64,256]{2,1,0:T(8,128)(2,1)S(1)}, bf16[2,64,256]{2,1,0:T(8,128)(2,1)S(1)}, u32[]{:S(2)}, u32[]{:S(2)}) collective-permute-start(bf16[2,64,256]{2,1,0:T(8,128)(2,1)S(1)} %collective-permute-done.1.refs_2_), channel_id=1, source_target_pairs={{0,1},{1,0},{2,3},{3,2},{4,5},{5,4},{6,7},{7,6},{8,9},{9,8},{10,11... | collective-permute-start | bytes 196616 | tf_op jit(solution)/shard_map/ppermute | solution.py:40
  10.2 3.4 %copy-start = (bf16[2,32,256,256]{3,2,1,0:T(8,128)(2,1)S(1)}, bf16[2,32,256,256]{3,2,1,0:T(8,128)(2,1)}, u32[]{:S(2)}) copy-start(bf16[2,32,256,256]{3,2,1,0:T(8,128)(2,1)} %x_ref.1) | copy-start | bytes 25165828
  17.1 25.2 %collective-permute-start.12 = (bf16[2,32,32,256]{3,2,1,0:T(8,128)(2,1)S(1)}, bf16[2,32,32,256]{3,2,1,0:T(8,128)(2,1)S(1)}, u32[]{:S(2)}, u32[]{:S(2)}) collective-permute-start(bf16[2,32,32,256]{3,2,1,0:T(8,128)(2,1)S(1)} %get-tuple-element.16), channel_id=1, source_target_pairs={{0,5},{1,4},{2,7},{3,6},{4,1},{5,0},{6,3},{7,2},{8,13},{9,12},{10,... | collective-permute-start | bytes 3145736 | tf_op jit(solution)/shard_map/ppermute | solution.py:40
  18.8 25.3 %collective-permute-start.8 = (bf16[2,32,32,256]{3,2,1,0:T(8,128)(2,1)S(1)}, bf16[2,32,32,256]{3,2,1,0:T(8,128)(2,1)S(1)}, u32[]{:S(2)}, u32[]{:S(2)}) collective-permute-start(bf16[2,32,32,256]{3,2,1,0:T(8,128)(2,1)S(1)} %get-tuple-element.13.refs_9_), channel_id=1, source_target_pairs={{0,3},{1,2},{2,1},{3,0},{4,7},{5,6},{6,5},{7,4},{8,11},{9,10},{10,... | collective-permute-start | bytes 3145736 | tf_op jit(solution)/shard_map/ppermute | solution.py:40
  24.7 62.9 %collective-permute-start.11 = (bf16[2,32,8192]{2,1,0:T(8,128)(2,1)S(1)}, bf16[2,32,8192]{2,1,0:T(8,128)(2,1)S(1)}, u32[]{:S(2)}, u32[]{:S(2)}) collective-permute-start(bf16[2,32,8192]{2,1,0:T(8,128)(2,1)S(1)} %get-tuple-element.15), channel_id=1, source_target_pairs={{0,4},{1,5},{2,6},{3,7},{4,0},{5,1},{6,2},{7,3},{8,12},{9,13},{10,... | collective-permute-start | bytes 3145736 | tf_op jit(solution)/shard_map/ppermute | solution.py:40
  25.7 19.3 %slice-start = ((s8[8388608]{0:T(1024)(128)(4,1)}), s8[4194304]{0:T(1024)(128)(4,1)S(1)}, s32[]{:S(2)}) async-start(s8[8388608]{0:T(1024)(128)(4,1)} %bitcast.1), calls=%async_computation | async-start | bytes 8388608
  31.5 13.6 %slice-start.1 = ((s8[8388608]{0:T(1024)(128)(4,1)}), s8[4194304]{0:T(1024)(128)(4,1)S(1)}, s32[]{:S(2)}) async-start(s8[8388608]{0:T(1024)(128)(4,1)} %bitcast.1), calls=%async_computation.1 | async-start | bytes 8388608
  31.5 60.1 %collective-permute-start.16 = (bf16[2,32,8192]{2,1,0:T(8,128)(2,1)S(1)}, bf16[2,32,8192]{2,1,0:T(8,128)(2,1)S(1)}, u32[]{:S(2)}, u32[]{:S(2)}) collective-permute-start(bf16[2,32,8192]{2,1,0:T(8,128)(2,1)S(1)} %get-tuple-element.18.refs_9_), channel_id=1, source_target_pairs={{0,7},{1,6},{2,5},{3,4},{4,3},{5,2},{6,1},{7,0},{8,15},{9,14},{10,... | collective-permute-start | bytes 3145736 | tf_op jit(solution)/shard_map/ppermute | solution.py:40
  39.2 54.6 %collective-permute-start.19 = (bf16[2,32,8192]{2,1,0:T(8,128)(2,1)S(1)}, bf16[2,32,8192]{2,1,0:T(8,128)(2,1)S(1)}, u32[]{:S(2)}, u32[]{:S(2)}) collective-permute-start(bf16[2,32,8192]{2,1,0:T(8,128)(2,1)S(1)} %get-tuple-element.20), channel_id=1, source_target_pairs={{0,1},{1,0},{2,3},{3,2},{4,5},{5,4},{6,7},{7,6},{8,9},{9,8},{10,11... | collective-permute-start | bytes 3145736 | tf_op jit(solution)/shard_map/ppermute | solution.py:40
  42.3 55.5 %collective-permute-start.7 = (bf16[2,32,8192]{2,1,0:T(8,128)(2,1)S(1)}, bf16[2,32,8192]{2,1,0:T(8,128)(2,1)S(1)}, u32[]{:S(2)}, u32[]{:S(2)}) collective-permute-start(bf16[2,32,8192]{2,1,0:T(8,128)(2,1)S(1)} %get-tuple-element.14.refs_9_), channel_id=1, source_target_pairs={{0,2},{1,3},{2,0},{3,1},{4,6},{5,7},{6,4},{7,5},{8,10},{9,11},{10,... | collective-permute-start | bytes 3145736 | tf_op jit(solution)/shard_map/ppermute | solution.py:40
  44.1 67.8 %collective-permute-start.15 = (bf16[2,32,8192]{2,1,0:T(8,128)(2,1)S(1)}, bf16[2,32,8192]{2,1,0:T(8,128)(2,1)S(1)}, u32[]{:S(2)}, u32[]{:S(2)}) collective-permute-start(bf16[2,32,8192]{2,1,0:T(8,128)(2,1)S(1)} %get-tuple-element.17), channel_id=1, source_target_pairs={{0,6},{1,7},{2,4},{3,5},{4,2},{5,3},{6,0},{7,1},{8,14},{9,15},{10,... | collective-permute-start | bytes 3145736 | tf_op jit(solution)/shard_map/ppermute | solution.py:40
  87.6 8.0 %collective-permute-start.13 = (f32[2,32,256]{2,1,0:T(8,128)S(1)}, f32[2,32,256]{2,1,0:T(8,128)S(1)}, u32[]{:S(2)}, u32[]{:S(2)}) collective-permute-start(f32[2,32,256]{2,1,0:T(8,128)S(1)} %last.10), channel_id=1, source_target_pairs={{0,1},{1,0},{2,3},{3,2},{4,5},{5,4},{6,7},{7,6},{8,9},{9,8},{10,11... | collective-permute-start | bytes 196616 | tf_op jit(solution)/shard_map/ppermute | solution.py:40
  91.5 7.9 %collective-permute-start.9 = (f32[2,32,256]{2,1,0:T(8,128)S(1)}, f32[2,32,256]{2,1,0:T(8,128)S(1)}, u32[]{:S(2)}, u32[]{:S(2)}) collective-permute-start(f32[2,32,256]{2,1,0:T(8,128)S(1)} %last.8), channel_id=1, source_target_pairs={{0,1},{1,0},{2,3},{3,2},{4,5},{5,4},{6,7},{7,6},{8,9},{9,8},{10,11... | collective-permute-start | bytes 196616 | tf_op jit(solution)/shard_map/ppermute | solution.py:40
  93.8 18.1 %collective-permute-start.17 = (f32[2,32,256]{2,1,0:T(8,128)S(1)}, f32[2,32,256]{2,1,0:T(8,128)S(1)}, u32[]{:S(2)}, u32[]{:S(2)}) collective-permute-start(f32[2,32,256]{2,1,0:T(8,128)S(1)} %last.12), channel_id=1, source_target_pairs={{0,1},{1,0},{2,3},{3,2},{4,5},{5,4},{6,7},{7,6},{8,9},{9,8},{10,11... | collective-permute-start | bytes 196616 | tf_op jit(solution)/shard_map/ppermute | solution.py:40
  95.6 19.5 %collective-permute-start.20 = (f32[2,32,256]{2,1,0:T(8,128)S(1)}, f32[2,32,256]{2,1,0:T(8,128)S(1)}, u32[]{:S(2)}, u32[]{:S(2)}) collective-permute-start(f32[2,32,256]{2,1,0:T(8,128)S(1)} %last.14), channel_id=1, source_target_pairs={{0,1},{1,0},{2,3},{3,2},{4,5},{5,4},{6,7},{7,6},{8,9},{9,8},{10,11... | collective-permute-start | bytes 196616 | tf_op jit(solution)/shard_map/ppermute | solution.py:40
  97.8 19.0 %collective-permute-start.14 = (f32[2,32,256]{2,1,0:T(8,128)S(1)}, f32[2,32,256]{2,1,0:T(8,128)S(1)}, u32[]{:S(2)}, u32[]{:S(2)}) collective-permute-start(f32[2,32,256]{2,1,0:T(8,128)S(1)} %last.11), channel_id=1, source_target_pairs={{0,4},{1,5},{2,6},{3,7},{4,0},{5,1},{6,2},{7,3},{8,12},{9,13},{10,... | collective-permute-start | bytes 196616 | tf_op jit(solution)/shard_map/ppermute | solution.py:40
  101.1 15.7 %collective-permute-start.10 = (f32[2,32,256]{2,1,0:T(8,128)S(1)}, f32[2,32,256]{2,1,0:T(8,128)S(1)}, u32[]{:S(2)}, u32[]{:S(2)}) collective-permute-start(f32[2,32,256]{2,1,0:T(8,128)S(1)} %last.9), channel_id=1, source_target_pairs={{0,2},{1,3},{2,0},{3,1},{4,6},{5,7},{6,4},{7,5},{8,10},{9,11},{10,... | collective-permute-start | bytes 196616 | tf_op jit(solution)/shard_map/ppermute | solution.py:40
  113.6 5.2 %collective-permute-start.18 = (f32[2,32,256]{2,1,0:T(8,128)S(1)}, f32[2,32,256]{2,1,0:T(8,128)S(1)}, u32[]{:S(2)}, u32[]{:S(2)}) collective-permute-start(f32[2,32,256]{2,1,0:T(8,128)S(1)} %last.13), channel_id=1, source_target_pairs={{0,6},{1,7},{2,4},{3,5},{4,2},{5,3},{6,0},{7,1},{8,14},{9,15},{10,... | collective-permute-start | bytes 196616 | tf_op jit(solution)/shard_map/ppermute | solution.py:40

commit v4 on v3

--- a/solution.py
+++ b/solution.py
@@ -9,6 +9,7 @@
 
 AXIS = "cuts"
 LIMIT = 20 * 1024 * 1024
+MOST = 44 * 1024 * 1024
 LANES = 128
 
 
@@ -40,6 +41,11 @@
     return lax.ppermute(value, AXIS, [(i, i ^ mask) for i in range(n)])
 
 
+def packed(left, right):
+    rows = left.shape[1]
+    return jnp.pad(left, ((0, 0), (0, rows), (0, 0))) + jnp.pad(right, ((0, 0), (rows, 0), (0, 0)))
+
+
 def gather_rows(value, n):
     even = {mask: swap(value, mask, n) for mask in range(n - 2, 0, -2)}
     even[0] = value
@@ -47,35 +53,6 @@
     for mask, came in even.items():
         rows[mask], rows[mask + 1] = came, swap(came, 1, n)
     return rows
-
-
-def stage_kernel(x_ref, out_ref, sems):
-    parents, count = sems.shape
-    step = x_ref.shape[1] // count
-    copies = [
-        pltpu.make_async_copy(
-            x_ref.at[p, pl.ds(c * step, step)], out_ref.at[p, pl.ds(c * step, step)], sems.at[p, c]
-        )
-        for p in range(parents)
-        for c in range(count)
-    ]
-    for copy in copies:
-        copy.start()
-    for copy in copies:
-        copy.wait()
-
-
-def staged(core):
-    return pl.pallas_call(
-        stage_kernel,
-        in_specs=[pl.BlockSpec(memory_space=pl.ANY)],
-        out_specs=pl.BlockSpec(memory_space=pl.ANY),
-        out_shape=jax.ShapeDtypeStruct(core.shape, core.dtype),
-        scratch_shapes=[pltpu.SemaphoreType.DMA((core.shape[0], 4))],
-        compiler_params=pltpu.CompilerParams(vmem_limit_bytes=LIMIT),
-        cost_estimate=pl.CostEstimate(flops=0, bytes_accessed=4 * core.size, transcendentals=0),
-        name="stage",
-    )(core)
 
 
 def at_rows(me, mask, rows):
@@ -104,18 +81,30 @@
 
 
 def first_kernel(n, masks, me_ref, *refs):
-    pieces, x_ref = refs[:n], refs[n]
-    outs, (full, turned, chosen) = refs[n + 1 : n + 1 + len(masks)], refs[-3:]
+    pieces, x_ref, outs = refs[:n], refs[n], refs[n + 1 : -5]
+    full, turned, chosen, held, sems = refs[-5:]
     parent, chunk = pl.program_id(0), pl.program_id(1)
+    parents, chunks = sems.shape
     step, rows = outs[0].shape[1], outs[0].shape[2]
+
+    def copy(p, c):
+        at = pl.ds(c * step, step)
+        return pltpu.make_async_copy(x_ref.at[p, at], held.at[p, at], sems.at[p, c])
+
+    @pl.when((parent == 0) & (chunk == 0))
+    def _():
+        for p in range(parents):
+            for c in range(chunks):
+                copy(p, c).start()
 
     @pl.when(chunk == 0)
     def _():
         choose(me_ref[0], masks, pieces, full, turned, chosen)
 
+    copy(parent, chunk).wait()
     for a in range(step):
         product = jnp.dot(
-            chosen[...], x_ref[parent, chunk * step + a], preferred_element_type=jnp.float32
+            chosen[...], held[parent, chunk * step + a], preferred_element_type=jnp.float32
         ).astype(jnp.bfloat16)
         for slot, out in enumerate(outs):
             out[0, a] = product[slot * rows : (slot + 1) * rows, :]
@@ -131,15 +120,17 @@
         grid=(parents, mine // step),
         in_specs=[pl.BlockSpec(memory_space=pltpu.SMEM)]
         + [pl.BlockSpec((1, 2 * rows, left), lambda p, c: (p, 0, 0))] * n
-        + [pl.BlockSpec(memory_space=pltpu.VMEM)],
+        + [pl.BlockSpec(memory_space=pl.ANY)],
         out_specs=[pl.BlockSpec((1, step, rows, right), lambda p, c: (p, c, 0, 0))] * len(masks),
         out_shape=[jax.ShapeDtypeStruct((parents, mine, rows, right), jnp.bfloat16)] * len(masks),
         scratch_shapes=[
             pltpu.VMEM((left, left), jnp.bfloat16),
             pltpu.VMEM((left, left), jnp.bfloat16),
             pltpu.VMEM((rows * len(masks), left), jnp.bfloat16),
+            pltpu.VMEM(core_x.shape, jnp.bfloat16),
+            pltpu.SemaphoreType.DMA((parents, mine // step)),
         ],
-        compiler_params=pltpu.CompilerParams(vmem_limit_bytes=LIMIT),
+        compiler_params=pltpu.CompilerParams(vmem_limit_bytes=MOST),
         cost_estimate=pl.CostEstimate(
             flops=2 * parents * mine * rows * len(masks) * left * right,
             bytes_accessed=2 * parents * mine * right * (left + rows * len(masks)),
@@ -151,7 +142,7 @@
 
 def second_kernel(n, masks, me_ref, *refs):
     pieces, x_ref = refs[:n], refs[n]
-    outs, (full, turned, chosen, first, second) = refs[-5 - len(masks) : -5], refs[-5:]
+    outs, (full, turned, chosen, first, second) = refs[n + 2 : -5], refs[-5:]
     parent = pl.program_id(0)
     mine, rows = outs[0].shape[1], pieces[0].shape[1] // 2
     choose(me_ref[0], masks, pieces, full, turned, chosen)
@@ -161,22 +152,33 @@
         product = jnp.dot(chosen[...], x_ref[parent, a], preferred_element_type=jnp.float32).astype(jnp.bfloat16)
         for slot in range(len(masks)):
             first[slot, a * rows : (a + 1) * rows, :] = product[slot * rows : (slot + 1) * rows, :]
-    for slot, out in enumerate(outs):
-        apply_right(first[slot], full[...], second, out.at[0], mine, rows)
-
-
-def second_for(me, pieces, core_x, masks, after):
+    for slot in range(len(masks)):
+        if len(outs) == len(masks) or slot < len(masks) - 1:
+            apply_right(first[slot], full[...], second, outs[slot].at[0], mine, rows)
+        else:
+            for p, out in enumerate(outs[slot:]):
+
+                @pl.when(parent == p)
+                def _(slot=slot, out=out):
+                    apply_right(first[slot], full[...], second, out.at[0], mine, rows)
+
+
+def second_for(me, pieces, core_x, masks, after, split=False):
     n = len(pieces)
     parents, mine, left, right = core_x.shape
     rows = left // n
+    wide = rows * right
+    whole = len(masks) - split
     return pl.pallas_call(
         functools.partial(second_kernel, n, masks),
         grid=(parents,),
         in_specs=[pl.BlockSpec(memory_space=pltpu.SMEM)]
         + [pl.BlockSpec((1, 2 * rows, left), lambda p: (p, 0, 0))] * n
         + [pl.BlockSpec(memory_space=pltpu.VMEM), pl.BlockSpec(memory_space=pl.ANY)],
-        out_specs=[pl.BlockSpec((1, mine, rows * right), lambda p: (p, 0, 0))] * len(masks),
-        out_shape=[jax.ShapeDtypeStruct((parents, mine, rows * right), jnp.bfloat16)] * len(masks),
+        out_specs=[pl.BlockSpec((1, mine, wide), lambda p: (p, 0, 0))] * whole
+        + [pl.BlockSpec((1, mine, wide), lambda p: (0, 0, 0))] * (parents * split),
+        out_shape=[jax.ShapeDtypeStruct((parents, mine, wide), jnp.bfloat16)] * whole
+        + [jax.ShapeDtypeStruct((1, mine, wide), jnp.bfloat16)] * (parents * split),
         scratch_shapes=[
             pltpu.VMEM((left, left), jnp.bfloat16),
             pltpu.VMEM((left, left), jnp.bfloat16),
@@ -215,48 +217,41 @@
     )(me, *pieces)
 
 
-def last_kernel(held, right_given, came_ref, y_ref, *refs):
-    begin_ref = refs[0] if held else None
-    parent = pl.program_id(0)
+def last_kernel(parents, held, only, right_given, came, *refs):
+    refs = list(refs)
+    given, y_ref = [refs.pop(0) for _ in range(came)], refs.pop(0)
+    begin_ref = refs.pop(0) if held else None
+    right_ref = refs.pop(0) if right_given else None
+    out_ref = refs.pop(0)
     depth = y_ref.shape[1] * y_ref.shape[2]
-    if right_given:
-        right_ref, out_ref, second, flat = refs[-4:]
-        count, rows = came_ref.shape[1], came_ref.shape[2]
-        apply_right(
-            came_ref[0].reshape(count * rows, came_ref.shape[3]), right_ref[0], second, flat, count, rows
-        )
-        wide = flat[...]
-    else:
-        out_ref = refs[-1]
-        wide = came_ref[0]
-    total = jnp.dot(wide, y_ref[parent].reshape(depth, y_ref.shape[3]), preferred_element_type=jnp.float32)
-    out_ref[0] = total + begin_ref[0] if held else total
-
-
-def last_for(came, core_y, begin=None, right=None):
-    parents, rows, width, out_width = core_y.shape
-    count = came.shape[1]
-    row = pl.BlockSpec((1, count, out_width), lambda p: (p, 0, 0))
-    zeros = (0,) * (came.ndim - 1)
-    given = [came, core_y]
-    specs = [
-        pl.BlockSpec((1,) + came.shape[1:], lambda p: (p,) + zeros),
-        pl.BlockSpec(memory_space=pltpu.VMEM),
-    ]
+    wide = [(ref, i) for ref in given for i in range(ref.shape[0])]
+    for slot in range(parents):
+        parent = slot if only is None else only
+        ref, i = wide[slot]
+        if right_given:
+            second, flat = refs
+            _, count, rows, right = ref.shape
+            apply_right(ref[i].reshape(count * rows, right), right_ref[parent], second, flat, count, rows)
+            ref, i = flat, Ellipsis
+        total = jnp.dot(ref[i], y_ref[parent].reshape(depth, y_ref.shape[3]), preferred_element_type=jnp.float32)
+        out_ref[slot] = total + begin_ref[parent] if held else total
+
+
+def last_for(came, core_y, begin=None, right=None, only=None):
+    total, rows, width, out_width = core_y.shape
+    parents, count = total if only is None else 1, came[0].shape[1]
+    given = came + [core_y] + [x for x in (begin, right) if x is not None]
+    whole = pl.BlockSpec(memory_space=pltpu.VMEM)
     scratch = []
-    if begin is not None:
-        given, specs = given + [begin], specs + [row]
     if right is not None:
-        given, specs = given + [right], specs + [pl.BlockSpec((1,) + right.shape[1:], lambda p: (p, 0, 0))]
         scratch = [
             pltpu.VMEM((width // LANES, count * rows, LANES), jnp.float32),
             pltpu.VMEM((count, rows * width), jnp.bfloat16),
         ]
     return pl.pallas_call(
-        functools.partial(last_kernel, begin is not None, right is not None),
-        grid=(parents,),
-        in_specs=specs,
-        out_specs=row,
+        functools.partial(last_kernel, parents, begin is not None, only, right is not None, len(came)),
+        in_specs=[whole] * len(given),
+        out_specs=whole,
         out_shape=jax.ShapeDtypeStruct((parents, count, out_width), jnp.float32),
         scratch_shapes=scratch,
         compiler_params=pltpu.CompilerParams(vmem_limit_bytes=LIMIT),
@@ -269,27 +264,56 @@
     )(*given)
 
 
+def sum_kernel(parents, *refs):
+    out_ref = refs[-1]
+    for p in range(parents):
+        total = refs[0][p]
+        for ref in refs[1 : -1 - parents]:
+            total += ref[p]
+        out_ref[p] = total + refs[p - 1 - parents][0]
+
+
+def summed(whole, cut):
+    return pl.pallas_call(
+        functools.partial(sum_kernel, len(cut)),
+        in_specs=[pl.BlockSpec(memory_space=pltpu.VMEM)] * (len(whole) + len(cut)),
+        out_specs=pl.BlockSpec(memory_space=pltpu.VMEM),
+        out_shape=jax.ShapeDtypeStruct(whole[0].shape, whole[0].dtype),
+        compiler_params=pltpu.CompilerParams(vmem_limit_bytes=LIMIT),
+        cost_estimate=pl.CostEstimate(flops=whole[0].size, bytes_accessed=8 * whole[0].size, transcendentals=0),
+        name="sum",
+    )(*whole, *cut)
+
+
 def exchanged(core_x, core_y, left_intersection, right_intersection, n):
     me = lax.axis_index(AXIS).astype(jnp.int32).reshape(1)
+    parents = core_x.shape[0]
     pairs = list(range(2, n, 2))
-    pieces = gather_rows(jnp.concatenate([left_intersection, right_intersection], axis=1), n)
-    core_x = staged(core_x)
+    pieces = gather_rows(packed(left_intersection, right_intersection), n)
     early = [mask + 1 for mask in pairs[:2]]
-    sent = dict(zip(early, first_for(me, pieces, core_x, early)))
-    came = {mask: swap(sent[mask], mask, n) for mask in early}
-    after = sent[early[0]]
+    made = first_for(me, pieces, core_x, early)
+    came = {mask: [swap(part, mask, n)] for mask, part in zip(early, made)}
+    after = made[0]
+    end = pairs[-1]
     for masks in [pairs[:2]] + [[mask + 1, mask] for mask in pairs[2:]] + [[1, 0]]:
-        sent.update(zip(masks, second_for(me, pieces, core_x, masks, after)))
-        after = sent[masks[0]]
+        made = second_for(me, pieces, core_x, masks, after, end in masks)
+        after = made[0]
         for mask in masks:
-            came[mask] = swap(sent[mask], mask, n) if mask else sent[0]
+            if mask == end:
+                came[mask] = [swap(part, mask, n) for part in made[-parents:]]
+            else:
+                part = made[masks.index(mask)]
+                came[mask] = [swap(part, mask, n) if mask else part]
     right = join_right(me, pieces)
-    total = []
-    for mask in pairs + [0]:
-        odd = last_for(came[mask + 1], core_y, right=right if mask + 1 in early else None)
-        part = last_for(came[mask], core_y, begin=swap(odd, 1, n))
-        total.append(swap(part, mask, n) if mask else part)
-    return sum(total[1:], total[0])
+    whole, cut = [], []
+    for mask in [0] + pairs:
+        odd = swap(last_for(came[mask + 1], core_y, right=right if mask + 1 in early else None), 1, n)
+        if mask == end:
+            cut = [swap(last_for([came[mask][p]], core_y, odd, only=p), mask, n) for p in range(parents)]
+        else:
+            part = last_for(came[mask], core_y, odd)
+            whole.append(swap(part, mask, n) if mask else part)
+    return summed(whole, cut)
 
 
 def solution(mesh):

time: 120 us -> 116 us (0.967)
  local copies, waits for them, and re-layouts: 4.91 us -> 0.02 us
  starting transfers between devices: 16.4 us -> 20.3 us
  waiting for transfers between devices: 58.7 us -> 56.7 us
    unnamed x7 -> x6, local copies, waits for them, and re-layouts: 4.15 us -> 0.02 us
    ppermute x21 -> x23, starting transfers between devices: 16.4 us -> 20.3 us  [swap(): return lax.ppermute(value, AXIS, [(i, i ^ mask) for i in range(n)])]
    pallas_call x9 -> x10, Pallas kernels: 18.5 us -> 16.1 us  [the longest x9 15.4 us: last_for(): pl.pallas_call(functools.partial(last_kernel, parents, begin is not None,...]
    ppermute x21 -> x23, waiting for transfers between devices: 58.7 us -> 56.7 us  [swap(): return lax.ppermute(value, AXIS, [(i, i ^ mask) for i in range(n)])]
    pallas_call x1, Pallas kernels: 2.85 us -> 4.55 us  [first_for(): pl.pallas_call(functools.partial(first_kernel, n, masks), grid=(parents,...]
  transfers between devices with their start and end apart: 21 -> 23, of which waited for: 8 -> 12; matrix products, arithmetic and copies ran while one was open for 0% -> 0% of each run, Pallas kernels for 30% -> 29%
where the time goes in v4:
time: 116 us
  waiting for transfers between devices  56.7 us (49%)
  Pallas kernels  38.4 us (33%)
  starting transfers between devices  20.3 us (18%)
    ppermute x23, waiting for transfers between devices, swap(): return lax.ppermute(value, AXIS, [(i, i ^ mask) for i in range(n)])  56.7 us
    ppermute x23, starting transfers between devices, swap(): return lax.ppermute(value, AXIS, [(i, i ^ mask) for i in range(n)])  20.3 us
    pallas_call x3, Pallas kernels, second_for(): pl.pallas_call(functools.partial(second_kernel, n, masks), grid=(parents,...  17.8 us
    pallas_call x9, Pallas kernels, last_for(): pl.pallas_call(functools.partial(last_kernel, parents, begin is not None,...  15.4 us
    pallas_call x1, Pallas kernels, first_for(): pl.pallas_call(functools.partial(first_kernel, n, masks), grid=(parents,...  4.55 us
  transfers between devices with their start and end apart: 23, of which 12 were waited for; matrix products, arithmetic and copies ran while one was open for 0% of the time, Pallas kernels for 29%

profile of v4, /device:TPU:0, one launch (start us, length us, event | category | flops | bytes accessed | tf_op | source)
XLA Modules:
  0.0 116.3 jit_solution(18206473372260813101)
XLA Ops:
  0.0 0.8 pad_add_fusion.refs_0_
  0.8 3.9 %collective-permute-start.5 = (bf16[2,64,256]{2,1,0:T(8,128)(2,1)S(1)}, bf16[2,64,256]{2,1,0:T(8,128)(2,1)S(1)}, u32[]{:S(2)}, u32[]{:S(2)}) collective-permute-start(bf16[2,64,256]{2,1,0:T(8,128)(2,1)S(1)} %pad_add_fusion.refs_0_), channel_id=1, source_target_pairs={{0,6},{1,7},{2,4},{3,5},{4,2},{5,3},{6,0},{7,1},{8,14},{9,15},{10,... | collective-permute-start | bytes 196616 | tf_op jit(solution)/shard_map/ppermute | solution.py:41
  4.7 0.5 collective-permute-start.3
  5.2 0.1 collective-permute-start.1
  5.3 1.6 %collective-permute-done.5.refs_6_ = bf16[2,64,256]{2,1,0:T(8,128)(2,1)S(1)} collective-permute-done((bf16[2,64,256]{2,1,0:T(8,128)(2,1)S(1)}, bf16[2,64,256]{2,1,0:T(8,128)(2,1)S(1)}, u32[]{:S(2)}, u32[]{:S(2)}) %collective-permute-start.5) | collective-permute-done | bytes 65568 | tf_op jit(solution)/shard_map/ppermute | solution.py:41
  6.9 2.0 %collective-permute-done.3.refs_4_ = bf16[2,64,256]{2,1,0:T(8,128)(2,1)S(1)} collective-permute-done((bf16[2,64,256]{2,1,0:T(8,128)(2,1)S(1)}, bf16[2,64,256]{2,1,0:T(8,128)(2,1)S(1)}, u32[]{:S(2)}, u32[]{:S(2)}) %collective-permute-start.3) | collective-permute-done | bytes 65568 | tf_op jit(solution)/shard_map/ppermute | solution.py:41
  8.9 0.5 collective-permute-done.1.refs_2_
  9.5 0.7 collective-permute-done.4.refs_5_
  10.2 0.5 collective-permute-done.2.refs_3_
  10.7 4.5 %first.1 = (bf16[2,32,32,256]{3,2,1,0:T(8,128)(2,1)S(1)}, bf16[2,32,32,256]{3,2,1,0:T(8,128)(2,1)S(1)}) custom-call(s32[1]{0:T(128)} %bitcast.me_ref, bf16[2,64,256]{2,1,0:T(8,128)(2,1)S(1)} %pad_add_fusion.refs_0_, bf16[2,64,256]{2,1,0:T(8,128)(2,1)S(1)} %collective-permute-done.refs_1_, bf16[2,64,256]{2,1,0:T(8,128)(2,1)S(1)} %collective-permute-done.1.refs_2_, ...), custom_call_target="tpu_custom_call" | custom-call | flops 536870912 | bytes 10485760 | tf_op jit(solution)/shard_map/first/pallas_call | solution.py:118
  15.3 1.2 %collective-permute-start.14 = (bf16[2,32,32,256]{3,2,1,0:T(8,128)(2,1)S(1)}, bf16[2,32,32,256]{3,2,1,0:T(8,128)(2,1)S(1)}, u32[]{:S(2)}, u32[]{:S(2)}) collective-permute-start(bf16[2,32,32,256]{3,2,1,0:T(8,128)(2,1)S(1)} %get-tuple-element.20), channel_id=1, source_target_pairs={{0,5},{1,4},{2,7},{3,6},{4,1},{5,0},{6,3},{7,2},{8,13},{9,12},{10,... | collective-permute-start | bytes 3145736 | tf_op jit(solution)/shard_map/ppermute | solution.py:41
  16.5 0.6 collective-permute-start.10
  17.1 5.8 %second.3 = (bf16[2,32,8192]{2,1,0:T(8,128)(2,1)S(1)}, bf16[2,32,8192]{2,1,0:T(8,128)(2,1)S(1)}) custom-call(s32[1]{0:T(128)} %bitcast.me_ref, bf16[2,64,256]{2,1,0:T(8,128)(2,1)S(1)} %pad_add_fusion.refs_0_, bf16[2,64,256]{2,1,0:T(8,128)(2,1)S(1)} %collective-permute-done.refs_1_, bf16[2,64,256]{2,1,0:T(8,128)(2,1)S(1)} %collective-permute-done.1.refs_2_, ...), custom_call_target="tpu_custom_call" | custom-call | flops 1073741824 | bytes 10485760 | tf_op jit(solution)/shard_map/second/pallas_call | solution.py:172
  22.9 0.5 collective-permute-start.13
  23.3 1.6 %collective-permute-start.9 = (bf16[2,32,8192]{2,1,0:T(8,128)(2,1)S(1)}, bf16[2,32,8192]{2,1,0:T(8,128)(2,1)S(1)}, u32[]{:S(2)}, u32[]{:S(2)}) collective-permute-start(bf16[2,32,8192]{2,1,0:T(8,128)(2,1)S(1)} %get-tuple-element.15.refs_9_), channel_id=1, source_target_pairs={{0,2},{1,3},{2,0},{3,1},{4,6},{5,7},{6,4},{7,5},{8,10},{9,11},{10,... | collective-permute-start | bytes 3145736 | tf_op jit(solution)/shard_map/ppermute | solution.py:41
  24.9 6.1 %second.4 = (bf16[2,32,8192]{2,1,0:T(8,128)(2,1)S(1)}, bf16[1,32,8192]{2,1,0:T(8,128)(2,1)S(1)}, bf16[1,32,8192]{2,1,0:T(8,128)(2,1)S(1)}) custom-call(s32[1]{0:T(128)} %bitcast.me_ref, bf16[2,64,256]{2,1,0:T(8,128)(2,1)S(1)} %pad_add_fusion.refs_0_, bf16[2,64,256]{2,1,0:T(8,128)(2,1)S(1)} %collective-permute-done.refs_1_, ...), custom_call_target="tpu_custom_call" | custom-call | flops 1073741824 | bytes 10485760 | tf_op jit(solution)/shard_map/second/pallas_call | solution.py:172
  31.1 0.6 collective-permute-start.18
  31.7 5.9 %second.5 = (bf16[2,32,8192]{2,1,0:T(8,128)(2,1)S(1)}, bf16[2,32,8192]{2,1,0:T(8,128)(2,1)S(1)}) custom-call(s32[1]{0:T(128)} %bitcast.me_ref, bf16[2,64,256]{2,1,0:T(8,128)(2,1)S(1)} %pad_add_fusion.refs_0_, bf16[2,64,256]{2,1,0:T(8,128)(2,1)S(1)} %collective-permute-done.refs_1_, bf16[2,64,256]{2,1,0:T(8,128)(2,1)S(1)} %collective-permute-done.1.refs_2_, ...), custom_call_target="tpu_custom_call" | custom-call | flops 1073741824 | bytes 10485760 | tf_op jit(solution)/shard_map/second/pallas_call | solution.py:172
  37.6 3.0 %collective-permute-done.14.refs_0_ = bf16[2,32,32,256]{3,2,1,0:T(8,128)(2,1)S(1)} collective-permute-done((bf16[2,32,32,256]{3,2,1,0:T(8,128)(2,1)S(1)}, bf16[2,32,32,256]{3,2,1,0:T(8,128)(2,1)S(1)}, u32[]{:S(2)}, u32[]{:S(2)}) %collective-permute-start.14) | collective-permute-done | bytes 1048608 | tf_op jit(solution)/shard_map/ppermute | solution.py:41
  40.6 0.5 collective-permute-start.7
  41.1 0.2 collective-permute-done.10.refs_0_
  41.3 1.3 %collective-permute-start.17 = (bf16[1,32,8192]{2,1,0:T(8,128)(2,1)S(1)}, bf16[1,32,8192]{2,1,0:T(8,128)(2,1)S(1)}, u32[]{:S(2)}, u32[]{:S(2)}) collective-permute-start(bf16[1,32,8192]{2,1,0:T(8,128)(2,1)S(1)} %get-tuple-element.21), channel_id=1, source_target_pairs={{0,6},{1,7},{2,4},{3,5},{4,2},{5,3},{6,0},{7,1},{8,14},{9,15},{10,... | collective-permute-start | bytes 1572872 | tf_op jit(solution)/shard_map/ppermute | solution.py:41
  42.6 20.7 %collective-permute-done.13.refs_0_ = bf16[2,32,8192]{2,1,0:T(8,128)(2,1)S(1)} collective-permute-done((bf16[2,32,8192]{2,1,0:T(8,128)(2,1)S(1)}, bf16[2,32,8192]{2,1,0:T(8,128)(2,1)S(1)}, u32[]{:S(2)}, u32[]{:S(2)}) %collective-permute-start.13) | collective-permute-done | bytes 1048608 | tf_op jit(solution)/shard_map/ppermute | solution.py:41
  63.3 1.5 %collective-permute-start.21 = (bf16[1,32,8192]{2,1,0:T(8,128)(2,1)S(1)}, bf16[1,32,8192]{2,1,0:T(8,128)(2,1)S(1)}, u32[]{:S(2)}, u32[]{:S(2)}) collective-permute-start(bf16[1,32,8192]{2,1,0:T(8,128)(2,1)S(1)} %get-tuple-element.22), channel_id=1, source_target_pairs={{0,6},{1,7},{2,4},{3,5},{4,2},{5,3},{6,0},{7,1},{8,14},{9,15},{10,... | collective-permute-start | bytes 1572872 | tf_op jit(solution)/shard_map/ppermute | solution.py:41
  64.8 3.0 %last.13 = f32[2,32,256]{2,1,0:T(8,128)S(1)} custom-call(bf16[2,32,32,256]{3,2,1,0:T(8,128)(2,1)S(1)} %collective-permute-done.14.refs_0_, bf16[2,32,256,256]{3,2,1,0:T(8,128)(2,1)S(1)} %bitcast.2, bf16[2,256,256]{2,1,0:T(8,128)(2,1)S(1)} %join.1.refs_2_), custom_call_target="tpu_custom_call" | custom-call | flops 536870912 | bytes 9437184 | tf_op jit(solution)/shard_map/last/pallas_call | solution.py:251
  67.8 0.1 collective-permute-start.15
  67.9 3.0 %last.11 = f32[2,32,256]{2,1,0:T(8,128)S(1)} custom-call(bf16[2,32,32,256]{3,2,1,0:T(8,128)(2,1)S(1)} %collective-permute-done.10.refs_0_, bf16[2,32,256,256]{3,2,1,0:T(8,128)(2,1)S(1)} %bitcast.2, bf16[2,256,256]{2,1,0:T(8,128)(2,1)S(1)} %join.1.refs_2_), custom_call_target="tpu_custom_call" | custom-call | flops 536870912 | bytes 9437184 | tf_op jit(solution)/shard_map/last/pallas_call | solution.py:251
  71.0 15.2 %collective-permute-done.18.refs_0_ = bf16[2,32,8192]{2,1,0:T(8,128)(2,1)S(1)} collective-permute-done((bf16[2,32,8192]{2,1,0:T(8,128)(2,1)S(1)}, bf16[2,32,8192]{2,1,0:T(8,128)(2,1)S(1)}, u32[]{:S(2)}, u32[]{:S(2)}) %collective-permute-start.18) | collective-permute-done | bytes 1048608 | tf_op jit(solution)/shard_map/ppermute | solution.py:41
  86.2 1.1 collective-permute-start.11
  87.3 1.5 %last.15 = f32[2,32,256]{2,1,0:T(8,128)S(1)} custom-call(bf16[2,32,8192]{2,1,0:T(8,128)(2,1)S(1)} %collective-permute-done.18.refs_0_, bf16[2,32,256,256]{3,2,1,0:T(8,128)(2,1)S(1)} %bitcast.2), custom_call_target="tpu_custom_call" | custom-call | flops 268435456 | bytes 9437184 | tf_op jit(solution)/shard_map/last/pallas_call | solution.py:251
  88.8 0.1 collective-permute-start.19
  88.9 1.5 %last.9 = f32[2,32,256]{2,1,0:T(8,128)S(1)} custom-call(bf16[2,32,8192]{2,1,0:T(8,128)(2,1)S(1)} %collective-permute-done.7.refs_0_, bf16[2,32,256,256]{3,2,1,0:T(8,128)(2,1)S(1)} %bitcast.2), custom_call_target="tpu_custom_call" | custom-call | flops 268435456 | bytes 9437184 | tf_op jit(solution)/shard_map/last/pallas_call | solution.py:251
  90.4 0.6 collective-permute-start.8
  91.0 1.5 %last.14 = f32[2,32,256]{2,1,0:T(8,128)S(1)} custom-call(bf16[2,32,8192]{2,1,0:T(8,128)(2,1)S(1)} %collective-permute-done.13.refs_0_, bf16[2,32,256,256]{3,2,1,0:T(8,128)(2,1)S(1)} %bitcast.2, f32[2,32,256]{2,1,0:T(8,128)S(1)} %collective-permute-done.15.refs_2_), custom_call_target="tpu_custom_call" | custom-call | flops 268435456 | bytes 9437184 | tf_op jit(solution)/shard_map/last/pallas_call | solution.py:251
  92.5 0.0 collective-permute-done.11.refs_2_
  92.5 1.6 %collective-permute-start.16 = (f32[2,32,256]{2,1,0:T(8,128)S(1)}, f32[2,32,256]{2,1,0:T(8,128)S(1)}, u32[]{:S(2)}, u32[]{:S(2)}) collective-permute-start(f32[2,32,256]{2,1,0:T(8,128)S(1)} %last.14), channel_id=1, source_target_pairs={{0,4},{1,5},{2,6},{3,7},{4,0},{5,1},{6,2},{7,3},{8,12},{9,13},{10,... | collective-permute-start | bytes 196616 | tf_op jit(solution)/shard_map/ppermute | solution.py:41
  94.1 1.5 %last.12 = f32[2,32,256]{2,1,0:T(8,128)S(1)} custom-call(bf16[2,32,8192]{2,1,0:T(8,128)(2,1)S(1)} %collective-permute-done.9.refs_0_, bf16[2,32,256,256]{3,2,1,0:T(8,128)(2,1)S(1)} %bitcast.2, f32[2,32,256]{2,1,0:T(8,128)S(1)} %collective-permute-done.11.refs_2_), custom_call_target="tpu_custom_call" | custom-call | flops 268435456 | bytes 9437184 | tf_op jit(solution)/shard_map/last/pallas_call | solution.py:251
  95.7 3.1 %collective-permute-done.17.refs_0_ = bf16[1,32,8192]{2,1,0:T(8,128)(2,1)S(1)} collective-permute-done((bf16[1,32,8192]{2,1,0:T(8,128)(2,1)S(1)}, bf16[1,32,8192]{2,1,0:T(8,128)(2,1)S(1)}, u32[]{:S(2)}, u32[]{:S(2)}) %collective-permute-start.17) | collective-permute-done | bytes 524320 | tf_op jit(solution)/shard_map/ppermute | solution.py:41
  98.8 0.5 collective-permute-start.12
  99.2 0.8 last.16
  100.1 2.6 %collective-permute-start.20 = (f32[1,32,256]{2,1,0:T(8,128)S(1)}, f32[1,32,256]{2,1,0:T(8,128)S(1)}, u32[]{:S(2)}, u32[]{:S(2)}) collective-permute-start(f32[1,32,256]{2,1,0:T(8,128)S(1)} %last.16), channel_id=1, source_target_pairs={{0,6},{1,7},{2,4},{3,5},{4,2},{5,3},{6,0},{7,1},{8,14},{9,15},{10,... | collective-permute-start | bytes 98312 | tf_op jit(solution)/shard_map/ppermute | solution.py:41
  102.6 7.3 %collective-permute-done.21.refs_0_ = bf16[1,32,8192]{2,1,0:T(8,128)(2,1)S(1)} collective-permute-done((bf16[1,32,8192]{2,1,0:T(8,128)(2,1)S(1)}, bf16[1,32,8192]{2,1,0:T(8,128)(2,1)S(1)}, u32[]{:S(2)}, u32[]{:S(2)}) %collective-permute-start.21) | collective-permute-done | bytes 524320 | tf_op jit(solution)/shard_map/ppermute | solution.py:41
  109.9 0.8 last.17
  110.8 1.5 %collective-permute-start.22 = (f32[1,32,256]{2,1,0:T(8,128)S(1)}, f32[1,32,256]{2,1,0:T(8,128)S(1)}, u32[]{:S(2)}, u32[]{:S(2)}) collective-permute-start(f32[1,32,256]{2,1,0:T(8,128)S(1)} %last.17), channel_id=1, source_target_pairs={{0,6},{1,7},{2,4},{3,5},{4,2},{5,3},{6,0},{7,1},{8,14},{9,15},{10,... | collective-permute-start | bytes 98312 | tf_op jit(solution)/shard_map/ppermute | solution.py:41
  112.3 1.5 %last.10.refs_0_ = f32[2,32,256]{2,1,0:T(8,128)S(1)} custom-call(bf16[2,32,8192]{2,1,0:T(8,128)(2,1)S(1)} %get-tuple-element.17.refs_0_, bf16[2,32,256,256]{3,2,1,0:T(8,128)(2,1)S(1)} %bitcast.2, f32[2,32,256]{2,1,0:T(8,128)S(1)} %collective-permute-done.8.refs_2_), custom_call_target="tpu_custom_call" | custom-call | flops 268435456 | bytes 9437184 | tf_op jit(solution)/shard_map/last/pallas_call | solution.py:251
  113.9 0.0 collective-permute-done.20.refs_3_
  113.9 1.8 %collective-permute-done.22.refs_4_ = f32[1,32,256]{2,1,0:T(8,128)S(1)} collective-permute-done((f32[1,32,256]{2,1,0:T(8,128)S(1)}, f32[1,32,256]{2,1,0:T(8,128)S(1)}, u32[]{:S(2)}, u32[]{:S(2)}) %collective-permute-start.22) | collective-permute-done | bytes 32800 | tf_op jit(solution)/shard_map/ppermute | solution.py:41
  115.6 0.6 sum.1
  (21 shorter events, 0.1 us)
Async XLA Ops:
  0.8 6.1 %collective-permute-start.5 = (bf16[2,64,256]{2,1,0:T(8,128)(2,1)S(1)}, bf16[2,64,256]{2,1,0:T(8,128)(2,1)S(1)}, u32[]{:S(2)}, u32[]{:S(2)}) collective-permute-start(bf16[2,64,256]{2,1,0:T(8,128)(2,1)S(1)} %pad_add_fusion.refs_0_), channel_id=1, source_target_pairs={{0,6},{1,7},{2,4},{3,5},{4,2},{5,3},{6,0},{7,1},{8,14},{9,15},{10,... | collective-permute-start | bytes 196616 | tf_op jit(solution)/shard_map/ppermute | solution.py:41
  4.7 4.3 %collective-permute-start.3 = (bf16[2,64,256]{2,1,0:T(8,128)(2,1)S(1)}, bf16[2,64,256]{2,1,0:T(8,128)(2,1)S(1)}, u32[]{:S(2)}, u32[]{:S(2)}) collective-permute-start(bf16[2,64,256]{2,1,0:T(8,128)(2,1)S(1)} %pad_add_fusion.refs_0_), channel_id=1, source_target_pairs={{0,4},{1,5},{2,6},{3,7},{4,0},{5,1},{6,2},{7,3},{8,12},{9,13},{10,... | collective-permute-start | bytes 196616 | tf_op jit(solution)/shard_map/ppermute | solution.py:41
  5.2 4.3 %collective-permute-start.1 = (bf16[2,64,256]{2,1,0:T(8,128)(2,1)S(1)}, bf16[2,64,256]{2,1,0:T(8,128)(2,1)S(1)}, u32[]{:S(2)}, u32[]{:S(2)}) collective-permute-start(bf16[2,64,256]{2,1,0:T(8,128)(2,1)S(1)} %pad_add_fusion.refs_0_), channel_id=1, source_target_pairs={{0,2},{1,3},{2,0},{3,1},{4,6},{5,7},{6,4},{7,5},{8,10},{9,11},{10,... | collective-permute-start | bytes 196616 | tf_op jit(solution)/shard_map/ppermute | solution.py:41
  5.3 4.2 %collective-permute-start = (bf16[2,64,256]{2,1,0:T(8,128)(2,1)S(1)}, bf16[2,64,256]{2,1,0:T(8,128)(2,1)S(1)}, u32[]{:S(2)}, u32[]{:S(2)}) collective-permute-start(bf16[2,64,256]{2,1,0:T(8,128)(2,1)S(1)} %pad_add_fusion.refs_0_), channel_id=1, source_target_pairs={{0,1},{1,0},{2,3},{3,2},{4,5},{5,4},{6,7},{7,6},{8,9},{9,8},{10,11... | collective-permute-start | bytes 196616 | tf_op jit(solution)/shard_map/ppermute | solution.py:41
  6.9 2.5 %collective-permute-start.6 = (bf16[2,64,256]{2,1,0:T(8,128)(2,1)S(1)}, bf16[2,64,256]{2,1,0:T(8,128)(2,1)S(1)}, u32[]{:S(2)}, u32[]{:S(2)}) collective-permute-start(bf16[2,64,256]{2,1,0:T(8,128)(2,1)S(1)} %collective-permute-done.5.refs_6_), channel_id=1, source_target_pairs={{0,1},{1,0},{2,3},{3,2},{4,5},{5,4},{6,7},{7,6},{8,9},{9,8},{10,11... | collective-permute-start | bytes 196616 | tf_op jit(solution)/shard_map/ppermute | solution.py:41
  8.9 1.3 %collective-permute-start.4 = (bf16[2,64,256]{2,1,0:T(8,128)(2,1)S(1)}, bf16[2,64,256]{2,1,0:T(8,128)(2,1)S(1)}, u32[]{:S(2)}, u32[]{:S(2)}) collective-permute-start(bf16[2,64,256]{2,1,0:T(8,128)(2,1)S(1)} %collective-permute-done.3.refs_4_), channel_id=1, source_target_pairs={{0,1},{1,0},{2,3},{3,2},{4,5},{5,4},{6,7},{7,6},{8,9},{9,8},{10,11... | collective-permute-start | bytes 196616 | tf_op jit(solution)/shard_map/ppermute | solution.py:41
  9.4 1.3 %collective-permute-start.2 = (bf16[2,64,256]{2,1,0:T(8,128)(2,1)S(1)}, bf16[2,64,256]{2,1,0:T(8,128)(2,1)S(1)}, u32[]{:S(2)}, u32[]{:S(2)}) collective-permute-start(bf16[2,64,256]{2,1,0:T(8,128)(2,1)S(1)} %collective-permute-done.1.refs_2_), channel_id=1, source_target_pairs={{0,1},{1,0},{2,3},{3,2},{4,5},{5,4},{6,7},{7,6},{8,9},{9,8},{10,11... | collective-permute-start | bytes 196616 | tf_op jit(solution)/shard_map/ppermute | solution.py:41
  9.5 7.6 %copy-start = (bf16[2,32,256,256]{3,2,1,0:T(8,128)(2,1)S(1)}, bf16[2,32,256,256]{3,2,1,0:T(8,128)(2,1)}, u32[]{:S(2)}) copy-start(bf16[2,32,256,256]{3,2,1,0:T(8,128)(2,1)} %refs_8_.7) | copy-start | bytes 25165828
  15.3 25.3 %collective-permute-start.14 = (bf16[2,32,32,256]{3,2,1,0:T(8,128)(2,1)S(1)}, bf16[2,32,32,256]{3,2,1,0:T(8,128)(2,1)S(1)}, u32[]{:S(2)}, u32[]{:S(2)}) collective-permute-start(bf16[2,32,32,256]{3,2,1,0:T(8,128)(2,1)S(1)} %get-tuple-element.20), channel_id=1, source_target_pairs={{0,5},{1,4},{2,7},{3,6},{4,1},{5,0},{6,3},{7,2},{8,13},{9,12},{10,... | collective-permute-start | bytes 3145736 | tf_op jit(solution)/shard_map/ppermute | solution.py:41
  16.5 24.8 %collective-permute-start.10 = (bf16[2,32,32,256]{3,2,1,0:T(8,128)(2,1)S(1)}, bf16[2,32,32,256]{3,2,1,0:T(8,128)(2,1)S(1)}, u32[]{:S(2)}, u32[]{:S(2)}) collective-permute-start(bf16[2,32,32,256]{3,2,1,0:T(8,128)(2,1)S(1)} %get-tuple-element.14.refs_9_), channel_id=1, source_target_pairs={{0,3},{1,2},{2,1},{3,0},{4,7},{5,6},{6,5},{7,4},{8,11},{9,10},{10,... | collective-permute-start | bytes 3145736 | tf_op jit(solution)/shard_map/ppermute | solution.py:41
  22.9 40.4 %collective-permute-start.13 = (bf16[2,32,8192]{2,1,0:T(8,128)(2,1)S(1)}, bf16[2,32,8192]{2,1,0:T(8,128)(2,1)S(1)}, u32[]{:S(2)}, u32[]{:S(2)}) collective-permute-start(bf16[2,32,8192]{2,1,0:T(8,128)(2,1)S(1)} %get-tuple-element.19), channel_id=1, source_target_pairs={{0,4},{1,5},{2,6},{3,7},{4,0},{5,1},{6,2},{7,3},{8,12},{9,13},{10,... | collective-permute-start | bytes 3145736 | tf_op jit(solution)/shard_map/ppermute | solution.py:41
  23.3 41.4 %slice-start = ((s8[8388608]{0:T(1024)(128)(4,1)}), s8[4194304]{0:T(1024)(128)(4,1)S(1)}, s32[]{:S(2)}) async-start(s8[8388608]{0:T(1024)(128)(4,1)} %bitcast.1), calls=%async_computation | async-start | bytes 8388608
  23.3 44.5 %collective-permute-start.9 = (bf16[2,32,8192]{2,1,0:T(8,128)(2,1)S(1)}, bf16[2,32,8192]{2,1,0:T(8,128)(2,1)S(1)}, u32[]{:S(2)}, u32[]{:S(2)}) collective-permute-start(bf16[2,32,8192]{2,1,0:T(8,128)(2,1)S(1)} %get-tuple-element.15.refs_9_), channel_id=1, source_target_pairs={{0,2},{1,3},{2,0},{3,1},{4,6},{5,7},{6,4},{7,5},{8,10},{9,11},{10,... | collective-permute-start | bytes 3145736 | tf_op jit(solution)/shard_map/ppermute | solution.py:41
  31.1 33.7 %slice-start.1 = ((s8[8388608]{0:T(1024)(128)(4,1)}), s8[4194304]{0:T(1024)(128)(4,1)S(1)}, s32[]{:S(2)}) async-start(s8[8388608]{0:T(1024)(128)(4,1)} %bitcast.1), calls=%async_computation.1 | async-start | bytes 8388608
  31.1 55.1 %collective-permute-start.18 = (bf16[2,32,8192]{2,1,0:T(8,128)(2,1)S(1)}, bf16[2,32,8192]{2,1,0:T(8,128)(2,1)S(1)}, u32[]{:S(2)}, u32[]{:S(2)}) collective-permute-start(bf16[2,32,8192]{2,1,0:T(8,128)(2,1)S(1)} %get-tuple-element.16.refs_9_), channel_id=1, source_target_pairs={{0,7},{1,6},{2,5},{3,4},{4,3},{5,2},{6,1},{7,0},{8,15},{9,14},{10,... | collective-permute-start | bytes 3145736 | tf_op jit(solution)/shard_map/ppermute | solution.py:41
  40.6 48.2 %collective-permute-start.7 = (bf16[2,32,8192]{2,1,0:T(8,128)(2,1)S(1)}, bf16[2,32,8192]{2,1,0:T(8,128)(2,1)S(1)}, u32[]{:S(2)}, u32[]{:S(2)}) collective-permute-start(bf16[2,32,8192]{2,1,0:T(8,128)(2,1)S(1)} %get-tuple-element.18), channel_id=1, source_target_pairs={{0,1},{1,0},{2,3},{3,2},{4,5},{5,4},{6,7},{7,6},{8,9},{9,8},{10,11... | collective-permute-start | bytes 3145736 | tf_op jit(solution)/shard_map/ppermute | solution.py:41
  41.3 57.5 %collective-permute-start.17 = (bf16[1,32,8192]{2,1,0:T(8,128)(2,1)S(1)}, bf16[1,32,8192]{2,1,0:T(8,128)(2,1)S(1)}, u32[]{:S(2)}, u32[]{:S(2)}) collective-permute-start(bf16[1,32,8192]{2,1,0:T(8,128)(2,1)S(1)} %get-tuple-element.21), channel_id=1, source_target_pairs={{0,6},{1,7},{2,4},{3,5},{4,2},{5,3},{6,0},{7,1},{8,14},{9,15},{10,... | collective-permute-start | bytes 1572872 | tf_op jit(solution)/shard_map/ppermute | solution.py:41
  63.3 46.7 %collective-permute-start.21 = (bf16[1,32,8192]{2,1,0:T(8,128)(2,1)S(1)}, bf16[1,32,8192]{2,1,0:T(8,128)(2,1)S(1)}, u32[]{:S(2)}, u32[]{:S(2)}) collective-permute-start(bf16[1,32,8192]{2,1,0:T(8,128)(2,1)S(1)} %get-tuple-element.22), channel_id=1, source_target_pairs={{0,6},{1,7},{2,4},{3,5},{4,2},{5,3},{6,0},{7,1},{8,14},{9,15},{10,... | collective-permute-start | bytes 1572872 | tf_op jit(solution)/shard_map/ppermute | solution.py:41
  67.8 22.6 %collective-permute-start.15 = (f32[2,32,256]{2,1,0:T(8,128)S(1)}, f32[2,32,256]{2,1,0:T(8,128)S(1)}, u32[]{:S(2)}, u32[]{:S(2)}) collective-permute-start(f32[2,32,256]{2,1,0:T(8,128)S(1)} %last.13), channel_id=1, source_target_pairs={{0,1},{1,0},{2,3},{3,2},{4,5},{5,4},{6,7},{7,6},{8,9},{9,8},{10,11... | collective-permute-start | bytes 196616 | tf_op jit(solution)/shard_map/ppermute | solution.py:41
  86.2 6.4 %collective-permute-start.11 = (f32[2,32,256]{2,1,0:T(8,128)S(1)}, f32[2,32,256]{2,1,0:T(8,128)S(1)}, u32[]{:S(2)}, u32[]{:S(2)}) collective-permute-start(f32[2,32,256]{2,1,0:T(8,128)S(1)} %last.11), channel_id=1, source_target_pairs={{0,1},{1,0},{2,3},{3,2},{4,5},{5,4},{6,7},{7,6},{8,9},{9,8},{10,11... | collective-permute-start | bytes 196616 | tf_op jit(solution)/shard_map/ppermute | solution.py:41
  88.8 10.4 %collective-permute-start.19 = (f32[2,32,256]{2,1,0:T(8,128)S(1)}, f32[2,32,256]{2,1,0:T(8,128)S(1)}, u32[]{:S(2)}, u32[]{:S(2)}) collective-permute-start(f32[2,32,256]{2,1,0:T(8,128)S(1)} %last.15), channel_id=1, source_target_pairs={{0,1},{1,0},{2,3},{3,2},{4,5},{5,4},{6,7},{7,6},{8,9},{9,8},{10,11... | collective-permute-start | bytes 196616 | tf_op jit(solution)/shard_map/ppermute | solution.py:41
  90.4 21.9 %collective-permute-start.8 = (f32[2,32,256]{2,1,0:T(8,128)S(1)}, f32[2,32,256]{2,1,0:T(8,128)S(1)}, u32[]{:S(2)}, u32[]{:S(2)}) collective-permute-start(f32[2,32,256]{2,1,0:T(8,128)S(1)} %last.9), channel_id=1, source_target_pairs={{0,1},{1,0},{2,3},{3,2},{4,5},{5,4},{6,7},{7,6},{8,9},{9,8},{10,11... | collective-permute-start | bytes 196616 | tf_op jit(solution)/shard_map/ppermute | solution.py:41
  92.5 23.1 %collective-permute-start.16 = (f32[2,32,256]{2,1,0:T(8,128)S(1)}, f32[2,32,256]{2,1,0:T(8,128)S(1)}, u32[]{:S(2)}, u32[]{:S(2)}) collective-permute-start(f32[2,32,256]{2,1,0:T(8,128)S(1)} %last.14), channel_id=1, source_target_pairs={{0,4},{1,5},{2,6},{3,7},{4,0},{5,1},{6,2},{7,3},{8,12},{9,13},{10,... | collective-permute-start | bytes 196616 | tf_op jit(solution)/shard_map/ppermute | solution.py:41
  98.8 16.9 %collective-permute-start.12 = (f32[2,32,256]{2,1,0:T(8,128)S(1)}, f32[2,32,256]{2,1,0:T(8,128)S(1)}, u32[]{:S(2)}, u32[]{:S(2)}) collective-permute-start(f32[2,32,256]{2,1,0:T(8,128)S(1)} %last.12), channel_id=1, source_target_pairs={{0,2},{1,3},{2,0},{3,1},{4,6},{5,7},{6,4},{7,5},{8,10},{9,11},{10,... | collective-permute-start | bytes 196616 | tf_op jit(solution)/shard_map/ppermute | solution.py:41
  100.1 13.8 %collective-permute-start.20 = (f32[1,32,256]{2,1,0:T(8,128)S(1)}, f32[1,32,256]{2,1,0:T(8,128)S(1)}, u32[]{:S(2)}, u32[]{:S(2)}) collective-permute-start(f32[1,32,256]{2,1,0:T(8,128)S(1)} %last.16), channel_id=1, source_target_pairs={{0,6},{1,7},{2,4},{3,5},{4,2},{5,3},{6,0},{7,1},{8,14},{9,15},{10,... | collective-permute-start | bytes 98312 | tf_op jit(solution)/shard_map/ppermute | solution.py:41
  110.8 4.9 %collective-permute-start.22 = (f32[1,32,256]{2,1,0:T(8,128)S(1)}, f32[1,32,256]{2,1,0:T(8,128)S(1)}, u32[]{:S(2)}, u32[]{:S(2)}) collective-permute-start(f32[1,32,256]{2,1,0:T(8,128)S(1)} %last.17), channel_id=1, source_target_pairs={{0,6},{1,7},{2,4},{3,5},{4,2},{5,3},{6,0},{7,1},{8,14},{9,15},{10,... | collective-permute-start | bytes 98312 | tf_op jit(solution)/shard_map/ppermute | solution.py:41

commit v5 on v4

--- a/solution.py
+++ b/solution.py
@@ -142,25 +142,25 @@
 
 def second_kernel(n, masks, me_ref, *refs):
     pieces, x_ref = refs[:n], refs[n]
-    outs, (full, turned, chosen, first, second) = refs[n + 2 : -5], refs[-5:]
+    outs, (full, turned, chosen, first, second, right) = refs[n + 2 : -6], refs[-6:]
     parent = pl.program_id(0)
     mine, rows = outs[0].shape[1], pieces[0].shape[1] // 2
     choose(me_ref[0], masks, pieces, full, turned, chosen)
     for m, piece in enumerate(pieces):
-        full[at_rows(me_ref[0], m, rows), :] = piece[0, rows:]
+        right[at_rows(me_ref[0], m, rows), :] = piece[0, rows:]
     for a in range(mine):
         product = jnp.dot(chosen[...], x_ref[parent, a], preferred_element_type=jnp.float32).astype(jnp.bfloat16)
         for slot in range(len(masks)):
             first[slot, a * rows : (a + 1) * rows, :] = product[slot * rows : (slot + 1) * rows, :]
     for slot in range(len(masks)):
         if len(outs) == len(masks) or slot < len(masks) - 1:
-            apply_right(first[slot], full[...], second, outs[slot].at[0], mine, rows)
+            apply_right(first[slot], right[...], second, outs[slot].at[0], mine, rows)
         else:
             for p, out in enumerate(outs[slot:]):
 
                 @pl.when(parent == p)
                 def _(slot=slot, out=out):
-                    apply_right(first[slot], full[...], second, out.at[0], mine, rows)
+                    apply_right(first[slot], right[...], second, out.at[0], mine, rows)
 
 
 def second_for(me, pieces, core_x, masks, after, split=False):
@@ -185,6 +185,7 @@
             pltpu.VMEM((rows * len(masks), left), jnp.bfloat16),
             pltpu.VMEM((len(masks), mine * rows, right), jnp.bfloat16),
             pltpu.VMEM((right // LANES, mine * rows, LANES), jnp.float32),
+            pltpu.VMEM((right, right), jnp.bfloat16),
         ],
         compiler_params=pltpu.CompilerParams(vmem_limit_bytes=LIMIT),
         cost_estimate=pl.CostEstimate(

time: 116 us -> 116 us (level)
  no operation moved by 1% of the time
where the time goes in v5:
time: 116 us
  waiting for transfers between devices  56.7 us (49%)
  Pallas kernels  38.4 us (33%)
  starting transfers between devices  20.3 us (18%)
    ppermute x23, waiting for transfers between devices, swap(): return lax.ppermute(value, AXIS, [(i, i ^ mask) for i in range(n)])  56.7 us
    ppermute x23, starting transfers between devices, swap(): return lax.ppermute(value, AXIS, [(i, i ^ mask) for i in range(n)])  20.3 us
    pallas_call x3, Pallas kernels, second_for(): pl.pallas_call(functools.partial(second_kernel, n, masks), grid=(parents,...  17.8 us
    pallas_call x9, Pallas kernels, last_for(): pl.pallas_call(functools.partial(last_kernel, parents, begin is not None,...  15.4 us
    pallas_call x1, Pallas kernels, first_for(): pl.pallas_call(functools.partial(first_kernel, n, masks), grid=(parents,...  4.55 us
  transfers between devices with their start and end apart: 23, of which 12 were waited for; matrix products, arithmetic and copies ran while one was open for 0% of the time, Pallas kernels for 29%

profile of v5, /device:TPU:0, one launch (start us, length us, event | category | flops | bytes accessed | tf_op | source)
XLA Modules:
  0.0 116.3 jit_solution(7684437031654128146)
XLA Ops:
  0.0 0.8 pad_add_fusion.refs_0_
  0.8 3.9 %collective-permute-start.5 = (bf16[2,64,256]{2,1,0:T(8,128)(2,1)S(1)}, bf16[2,64,256]{2,1,0:T(8,128)(2,1)S(1)}, u32[]{:S(2)}, u32[]{:S(2)}) collective-permute-start(bf16[2,64,256]{2,1,0:T(8,128)(2,1)S(1)} %pad_add_fusion.refs_0_), channel_id=1, source_target_pairs={{0,6},{1,7},{2,4},{3,5},{4,2},{5,3},{6,0},{7,1},{8,14},{9,15},{10,... | collective-permute-start | bytes 196616 | tf_op jit(solution)/shard_map/ppermute | solution.py:41
  4.7 0.5 collective-permute-start.3
  5.2 0.1 collective-permute-start.1
  5.3 1.6 %collective-permute-done.5.refs_6_ = bf16[2,64,256]{2,1,0:T(8,128)(2,1)S(1)} collective-permute-done((bf16[2,64,256]{2,1,0:T(8,128)(2,1)S(1)}, bf16[2,64,256]{2,1,0:T(8,128)(2,1)S(1)}, u32[]{:S(2)}, u32[]{:S(2)}) %collective-permute-start.5) | collective-permute-done | bytes 65568 | tf_op jit(solution)/shard_map/ppermute | solution.py:41
  6.9 2.0 %collective-permute-done.3.refs_4_ = bf16[2,64,256]{2,1,0:T(8,128)(2,1)S(1)} collective-permute-done((bf16[2,64,256]{2,1,0:T(8,128)(2,1)S(1)}, bf16[2,64,256]{2,1,0:T(8,128)(2,1)S(1)}, u32[]{:S(2)}, u32[]{:S(2)}) %collective-permute-start.3) | collective-permute-done | bytes 65568 | tf_op jit(solution)/shard_map/ppermute | solution.py:41
  8.9 0.5 collective-permute-done.1.refs_2_
  9.5 0.7 collective-permute-done.4.refs_5_
  10.2 0.5 collective-permute-done.2.refs_3_
  10.7 4.5 %first.1 = (bf16[2,32,32,256]{3,2,1,0:T(8,128)(2,1)S(1)}, bf16[2,32,32,256]{3,2,1,0:T(8,128)(2,1)S(1)}) custom-call(s32[1]{0:T(128)} %bitcast.me_ref, bf16[2,64,256]{2,1,0:T(8,128)(2,1)S(1)} %pad_add_fusion.refs_0_, bf16[2,64,256]{2,1,0:T(8,128)(2,1)S(1)} %collective-permute-done.refs_1_, bf16[2,64,256]{2,1,0:T(8,128)(2,1)S(1)} %collective-permute-done.1.refs_2_, ...), custom_call_target="tpu_custom_call" | custom-call | flops 536870912 | bytes 10485760 | tf_op jit(solution)/shard_map/first/pallas_call | solution.py:118
  15.3 1.2 %collective-permute-start.14 = (bf16[2,32,32,256]{3,2,1,0:T(8,128)(2,1)S(1)}, bf16[2,32,32,256]{3,2,1,0:T(8,128)(2,1)S(1)}, u32[]{:S(2)}, u32[]{:S(2)}) collective-permute-start(bf16[2,32,32,256]{3,2,1,0:T(8,128)(2,1)S(1)} %get-tuple-element.20), channel_id=1, source_target_pairs={{0,5},{1,4},{2,7},{3,6},{4,1},{5,0},{6,3},{7,2},{8,13},{9,12},{10,... | collective-permute-start | bytes 3145736 | tf_op jit(solution)/shard_map/ppermute | solution.py:41
  16.5 0.6 collective-permute-start.10
  17.1 5.8 %second.3 = (bf16[2,32,8192]{2,1,0:T(8,128)(2,1)S(1)}, bf16[2,32,8192]{2,1,0:T(8,128)(2,1)S(1)}) custom-call(s32[1]{0:T(128)} %bitcast.me_ref, bf16[2,64,256]{2,1,0:T(8,128)(2,1)S(1)} %pad_add_fusion.refs_0_, bf16[2,64,256]{2,1,0:T(8,128)(2,1)S(1)} %collective-permute-done.refs_1_, bf16[2,64,256]{2,1,0:T(8,128)(2,1)S(1)} %collective-permute-done.1.refs_2_, ...), custom_call_target="tpu_custom_call" | custom-call | flops 1073741824 | bytes 10485760 | tf_op jit(solution)/shard_map/second/pallas_call | solution.py:172
  22.9 0.5 collective-permute-start.13
  23.3 1.6 %collective-permute-start.9 = (bf16[2,32,8192]{2,1,0:T(8,128)(2,1)S(1)}, bf16[2,32,8192]{2,1,0:T(8,128)(2,1)S(1)}, u32[]{:S(2)}, u32[]{:S(2)}) collective-permute-start(bf16[2,32,8192]{2,1,0:T(8,128)(2,1)S(1)} %get-tuple-element.15.refs_9_), channel_id=1, source_target_pairs={{0,2},{1,3},{2,0},{3,1},{4,6},{5,7},{6,4},{7,5},{8,10},{9,11},{10,... | collective-permute-start | bytes 3145736 | tf_op jit(solution)/shard_map/ppermute | solution.py:41
  24.9 6.1 %second.4 = (bf16[2,32,8192]{2,1,0:T(8,128)(2,1)S(1)}, bf16[1,32,8192]{2,1,0:T(8,128)(2,1)S(1)}, bf16[1,32,8192]{2,1,0:T(8,128)(2,1)S(1)}) custom-call(s32[1]{0:T(128)} %bitcast.me_ref, bf16[2,64,256]{2,1,0:T(8,128)(2,1)S(1)} %pad_add_fusion.refs_0_, bf16[2,64,256]{2,1,0:T(8,128)(2,1)S(1)} %collective-permute-done.refs_1_, ...), custom_call_target="tpu_custom_call" | custom-call | flops 1073741824 | bytes 10485760 | tf_op jit(solution)/shard_map/second/pallas_call | solution.py:172
  31.1 0.6 collective-permute-start.18
  31.7 5.9 %second.5 = (bf16[2,32,8192]{2,1,0:T(8,128)(2,1)S(1)}, bf16[2,32,8192]{2,1,0:T(8,128)(2,1)S(1)}) custom-call(s32[1]{0:T(128)} %bitcast.me_ref, bf16[2,64,256]{2,1,0:T(8,128)(2,1)S(1)} %pad_add_fusion.refs_0_, bf16[2,64,256]{2,1,0:T(8,128)(2,1)S(1)} %collective-permute-done.refs_1_, bf16[2,64,256]{2,1,0:T(8,128)(2,1)S(1)} %collective-permute-done.1.refs_2_, ...), custom_call_target="tpu_custom_call" | custom-call | flops 1073741824 | bytes 10485760 | tf_op jit(solution)/shard_map/second/pallas_call | solution.py:172
  37.6 3.0 %collective-permute-done.14.refs_0_ = bf16[2,32,32,256]{3,2,1,0:T(8,128)(2,1)S(1)} collective-permute-done((bf16[2,32,32,256]{3,2,1,0:T(8,128)(2,1)S(1)}, bf16[2,32,32,256]{3,2,1,0:T(8,128)(2,1)S(1)}, u32[]{:S(2)}, u32[]{:S(2)}) %collective-permute-start.14) | collective-permute-done | bytes 1048608 | tf_op jit(solution)/shard_map/ppermute | solution.py:41
  40.6 0.5 collective-permute-start.7
  41.1 0.2 collective-permute-done.10.refs_0_
  41.3 1.3 %collective-permute-start.17 = (bf16[1,32,8192]{2,1,0:T(8,128)(2,1)S(1)}, bf16[1,32,8192]{2,1,0:T(8,128)(2,1)S(1)}, u32[]{:S(2)}, u32[]{:S(2)}) collective-permute-start(bf16[1,32,8192]{2,1,0:T(8,128)(2,1)S(1)} %get-tuple-element.21), channel_id=1, source_target_pairs={{0,6},{1,7},{2,4},{3,5},{4,2},{5,3},{6,0},{7,1},{8,14},{9,15},{10,... | collective-permute-start | bytes 1572872 | tf_op jit(solution)/shard_map/ppermute | solution.py:41
  42.6 20.7 %collective-permute-done.13.refs_0_ = bf16[2,32,8192]{2,1,0:T(8,128)(2,1)S(1)} collective-permute-done((bf16[2,32,8192]{2,1,0:T(8,128)(2,1)S(1)}, bf16[2,32,8192]{2,1,0:T(8,128)(2,1)S(1)}, u32[]{:S(2)}, u32[]{:S(2)}) %collective-permute-start.13) | collective-permute-done | bytes 1048608 | tf_op jit(solution)/shard_map/ppermute | solution.py:41
  63.3 1.5 %collective-permute-start.21 = (bf16[1,32,8192]{2,1,0:T(8,128)(2,1)S(1)}, bf16[1,32,8192]{2,1,0:T(8,128)(2,1)S(1)}, u32[]{:S(2)}, u32[]{:S(2)}) collective-permute-start(bf16[1,32,8192]{2,1,0:T(8,128)(2,1)S(1)} %get-tuple-element.22), channel_id=1, source_target_pairs={{0,6},{1,7},{2,4},{3,5},{4,2},{5,3},{6,0},{7,1},{8,14},{9,15},{10,... | collective-permute-start | bytes 1572872 | tf_op jit(solution)/shard_map/ppermute | solution.py:41
  64.8 3.0 %last.13 = f32[2,32,256]{2,1,0:T(8,128)S(1)} custom-call(bf16[2,32,32,256]{3,2,1,0:T(8,128)(2,1)S(1)} %collective-permute-done.14.refs_0_, bf16[2,32,256,256]{3,2,1,0:T(8,128)(2,1)S(1)} %bitcast.2, bf16[2,256,256]{2,1,0:T(8,128)(2,1)S(1)} %join.1.refs_2_), custom_call_target="tpu_custom_call" | custom-call | flops 536870912 | bytes 9437184 | tf_op jit(solution)/shard_map/last/pallas_call | solution.py:252
  67.8 0.1 collective-permute-start.15
  67.9 3.0 %last.11 = f32[2,32,256]{2,1,0:T(8,128)S(1)} custom-call(bf16[2,32,32,256]{3,2,1,0:T(8,128)(2,1)S(1)} %collective-permute-done.10.refs_0_, bf16[2,32,256,256]{3,2,1,0:T(8,128)(2,1)S(1)} %bitcast.2, bf16[2,256,256]{2,1,0:T(8,128)(2,1)S(1)} %join.1.refs_2_), custom_call_target="tpu_custom_call" | custom-call | flops 536870912 | bytes 9437184 | tf_op jit(solution)/shard_map/last/pallas_call | solution.py:252
  71.0 15.2 %collective-permute-done.18.refs_0_ = bf16[2,32,8192]{2,1,0:T(8,128)(2,1)S(1)} collective-permute-done((bf16[2,32,8192]{2,1,0:T(8,128)(2,1)S(1)}, bf16[2,32,8192]{2,1,0:T(8,128)(2,1)S(1)}, u32[]{:S(2)}, u32[]{:S(2)}) %collective-permute-start.18) | collective-permute-done | bytes 1048608 | tf_op jit(solution)/shard_map/ppermute | solution.py:41
  86.2 1.1 collective-permute-start.11
  87.3 1.5 %last.15 = f32[2,32,256]{2,1,0:T(8,128)S(1)} custom-call(bf16[2,32,8192]{2,1,0:T(8,128)(2,1)S(1)} %collective-permute-done.18.refs_0_, bf16[2,32,256,256]{3,2,1,0:T(8,128)(2,1)S(1)} %bitcast.2), custom_call_target="tpu_custom_call" | custom-call | flops 268435456 | bytes 9437184 | tf_op jit(solution)/shard_map/last/pallas_call | solution.py:252
  88.8 0.1 collective-permute-start.19
  88.9 1.5 %last.9 = f32[2,32,256]{2,1,0:T(8,128)S(1)} custom-call(bf16[2,32,8192]{2,1,0:T(8,128)(2,1)S(1)} %collective-permute-done.7.refs_0_, bf16[2,32,256,256]{3,2,1,0:T(8,128)(2,1)S(1)} %bitcast.2), custom_call_target="tpu_custom_call" | custom-call | flops 268435456 | bytes 9437184 | tf_op jit(solution)/shard_map/last/pallas_call | solution.py:252
  90.4 0.6 collective-permute-start.8
  91.0 1.5 %last.14 = f32[2,32,256]{2,1,0:T(8,128)S(1)} custom-call(bf16[2,32,8192]{2,1,0:T(8,128)(2,1)S(1)} %collective-permute-done.13.refs_0_, bf16[2,32,256,256]{3,2,1,0:T(8,128)(2,1)S(1)} %bitcast.2, f32[2,32,256]{2,1,0:T(8,128)S(1)} %collective-permute-done.15.refs_2_), custom_call_target="tpu_custom_call" | custom-call | flops 268435456 | bytes 9437184 | tf_op jit(solution)/shard_map/last/pallas_call | solution.py:252
  92.5 0.0 collective-permute-done.11.refs_2_
  92.5 1.6 %collective-permute-start.16 = (f32[2,32,256]{2,1,0:T(8,128)S(1)}, f32[2,32,256]{2,1,0:T(8,128)S(1)}, u32[]{:S(2)}, u32[]{:S(2)}) collective-permute-start(f32[2,32,256]{2,1,0:T(8,128)S(1)} %last.14), channel_id=1, source_target_pairs={{0,4},{1,5},{2,6},{3,7},{4,0},{5,1},{6,2},{7,3},{8,12},{9,13},{10,... | collective-permute-start | bytes 196616 | tf_op jit(solution)/shard_map/ppermute | solution.py:41
  94.1 1.5 %last.12 = f32[2,32,256]{2,1,0:T(8,128)S(1)} custom-call(bf16[2,32,8192]{2,1,0:T(8,128)(2,1)S(1)} %collective-permute-done.9.refs_0_, bf16[2,32,256,256]{3,2,1,0:T(8,128)(2,1)S(1)} %bitcast.2, f32[2,32,256]{2,1,0:T(8,128)S(1)} %collective-permute-done.11.refs_2_), custom_call_target="tpu_custom_call" | custom-call | flops 268435456 | bytes 9437184 | tf_op jit(solution)/shard_map/last/pallas_call | solution.py:252
  95.7 3.1 %collective-permute-done.17.refs_0_ = bf16[1,32,8192]{2,1,0:T(8,128)(2,1)S(1)} collective-permute-done((bf16[1,32,8192]{2,1,0:T(8,128)(2,1)S(1)}, bf16[1,32,8192]{2,1,0:T(8,128)(2,1)S(1)}, u32[]{:S(2)}, u32[]{:S(2)}) %collective-permute-start.17) | collective-permute-done | bytes 524320 | tf_op jit(solution)/shard_map/ppermute | solution.py:41
  98.8 0.5 collective-permute-start.12
  99.2 0.8 last.16
  100.1 2.6 %collective-permute-start.20 = (f32[1,32,256]{2,1,0:T(8,128)S(1)}, f32[1,32,256]{2,1,0:T(8,128)S(1)}, u32[]{:S(2)}, u32[]{:S(2)}) collective-permute-start(f32[1,32,256]{2,1,0:T(8,128)S(1)} %last.16), channel_id=1, source_target_pairs={{0,6},{1,7},{2,4},{3,5},{4,2},{5,3},{6,0},{7,1},{8,14},{9,15},{10,... | collective-permute-start | bytes 98312 | tf_op jit(solution)/shard_map/ppermute | solution.py:41
  102.6 7.3 %collective-permute-done.21.refs_0_ = bf16[1,32,8192]{2,1,0:T(8,128)(2,1)S(1)} collective-permute-done((bf16[1,32,8192]{2,1,0:T(8,128)(2,1)S(1)}, bf16[1,32,8192]{2,1,0:T(8,128)(2,1)S(1)}, u32[]{:S(2)}, u32[]{:S(2)}) %collective-permute-start.21) | collective-permute-done | bytes 524320 | tf_op jit(solution)/shard_map/ppermute | solution.py:41
  109.9 0.8 last.17
  110.8 1.5 %collective-permute-start.22 = (f32[1,32,256]{2,1,0:T(8,128)S(1)}, f32[1,32,256]{2,1,0:T(8,128)S(1)}, u32[]{:S(2)}, u32[]{:S(2)}) collective-permute-start(f32[1,32,256]{2,1,0:T(8,128)S(1)} %last.17), channel_id=1, source_target_pairs={{0,6},{1,7},{2,4},{3,5},{4,2},{5,3},{6,0},{7,1},{8,14},{9,15},{10,... | collective-permute-start | bytes 98312 | tf_op jit(solution)/shard_map/ppermute | solution.py:41
  112.3 1.5 %last.10.refs_0_ = f32[2,32,256]{2,1,0:T(8,128)S(1)} custom-call(bf16[2,32,8192]{2,1,0:T(8,128)(2,1)S(1)} %get-tuple-element.17.refs_0_, bf16[2,32,256,256]{3,2,1,0:T(8,128)(2,1)S(1)} %bitcast.2, f32[2,32,256]{2,1,0:T(8,128)S(1)} %collective-permute-done.8.refs_2_), custom_call_target="tpu_custom_call" | custom-call | flops 268435456 | bytes 9437184 | tf_op jit(solution)/shard_map/last/pallas_call | solution.py:252
  113.9 0.0 collective-permute-done.20.refs_3_
  113.9 1.8 %collective-permute-done.22.refs_4_ = f32[1,32,256]{2,1,0:T(8,128)S(1)} collective-permute-done((f32[1,32,256]{2,1,0:T(8,128)S(1)}, f32[1,32,256]{2,1,0:T(8,128)S(1)}, u32[]{:S(2)}, u32[]{:S(2)}) %collective-permute-start.22) | collective-permute-done | bytes 32800 | tf_op jit(solution)/shard_map/ppermute | solution.py:41
  115.6 0.6 sum.1
  (21 shorter events, 0.1 us)
Async XLA Ops:
  0.8 6.1 %collective-permute-start.5 = (bf16[2,64,256]{2,1,0:T(8,128)(2,1)S(1)}, bf16[2,64,256]{2,1,0:T(8,128)(2,1)S(1)}, u32[]{:S(2)}, u32[]{:S(2)}) collective-permute-start(bf16[2,64,256]{2,1,0:T(8,128)(2,1)S(1)} %pad_add_fusion.refs_0_), channel_id=1, source_target_pairs={{0,6},{1,7},{2,4},{3,5},{4,2},{5,3},{6,0},{7,1},{8,14},{9,15},{10,... | collective-permute-start | bytes 196616 | tf_op jit(solution)/shard_map/ppermute | solution.py:41
  4.7 4.3 %collective-permute-start.3 = (bf16[2,64,256]{2,1,0:T(8,128)(2,1)S(1)}, bf16[2,64,256]{2,1,0:T(8,128)(2,1)S(1)}, u32[]{:S(2)}, u32[]{:S(2)}) collective-permute-start(bf16[2,64,256]{2,1,0:T(8,128)(2,1)S(1)} %pad_add_fusion.refs_0_), channel_id=1, source_target_pairs={{0,4},{1,5},{2,6},{3,7},{4,0},{5,1},{6,2},{7,3},{8,12},{9,13},{10,... | collective-permute-start | bytes 196616 | tf_op jit(solution)/shard_map/ppermute | solution.py:41
  5.2 4.3 %collective-permute-start.1 = (bf16[2,64,256]{2,1,0:T(8,128)(2,1)S(1)}, bf16[2,64,256]{2,1,0:T(8,128)(2,1)S(1)}, u32[]{:S(2)}, u32[]{:S(2)}) collective-permute-start(bf16[2,64,256]{2,1,0:T(8,128)(2,1)S(1)} %pad_add_fusion.refs_0_), channel_id=1, source_target_pairs={{0,2},{1,3},{2,0},{3,1},{4,6},{5,7},{6,4},{7,5},{8,10},{9,11},{10,... | collective-permute-start | bytes 196616 | tf_op jit(solution)/shard_map/ppermute | solution.py:41
  5.3 4.2 %collective-permute-start = (bf16[2,64,256]{2,1,0:T(8,128)(2,1)S(1)}, bf16[2,64,256]{2,1,0:T(8,128)(2,1)S(1)}, u32[]{:S(2)}, u32[]{:S(2)}) collective-permute-start(bf16[2,64,256]{2,1,0:T(8,128)(2,1)S(1)} %pad_add_fusion.refs_0_), channel_id=1, source_target_pairs={{0,1},{1,0},{2,3},{3,2},{4,5},{5,4},{6,7},{7,6},{8,9},{9,8},{10,11... | collective-permute-start | bytes 196616 | tf_op jit(solution)/shard_map/ppermute | solution.py:41
  6.9 2.5 %collective-permute-start.6 = (bf16[2,64,256]{2,1,0:T(8,128)(2,1)S(1)}, bf16[2,64,256]{2,1,0:T(8,128)(2,1)S(1)}, u32[]{:S(2)}, u32[]{:S(2)}) collective-permute-start(bf16[2,64,256]{2,1,0:T(8,128)(2,1)S(1)} %collective-permute-done.5.refs_6_), channel_id=1, source_target_pairs={{0,1},{1,0},{2,3},{3,2},{4,5},{5,4},{6,7},{7,6},{8,9},{9,8},{10,11... | collective-permute-start | bytes 196616 | tf_op jit(solution)/shard_map/ppermute | solution.py:41
  8.9 1.3 %collective-permute-start.4 = (bf16[2,64,256]{2,1,0:T(8,128)(2,1)S(1)}, bf16[2,64,256]{2,1,0:T(8,128)(2,1)S(1)}, u32[]{:S(2)}, u32[]{:S(2)}) collective-permute-start(bf16[2,64,256]{2,1,0:T(8,128)(2,1)S(1)} %collective-permute-done.3.refs_4_), channel_id=1, source_target_pairs={{0,1},{1,0},{2,3},{3,2},{4,5},{5,4},{6,7},{7,6},{8,9},{9,8},{10,11... | collective-permute-start | bytes 196616 | tf_op jit(solution)/shard_map/ppermute | solution.py:41
  9.4 1.3 %collective-permute-start.2 = (bf16[2,64,256]{2,1,0:T(8,128)(2,1)S(1)}, bf16[2,64,256]{2,1,0:T(8,128)(2,1)S(1)}, u32[]{:S(2)}, u32[]{:S(2)}) collective-permute-start(bf16[2,64,256]{2,1,0:T(8,128)(2,1)S(1)} %collective-permute-done.1.refs_2_), channel_id=1, source_target_pairs={{0,1},{1,0},{2,3},{3,2},{4,5},{5,4},{6,7},{7,6},{8,9},{9,8},{10,11... | collective-permute-start | bytes 196616 | tf_op jit(solution)/shard_map/ppermute | solution.py:41
  9.5 7.6 %copy-start = (bf16[2,32,256,256]{3,2,1,0:T(8,128)(2,1)S(1)}, bf16[2,32,256,256]{3,2,1,0:T(8,128)(2,1)}, u32[]{:S(2)}) copy-start(bf16[2,32,256,256]{3,2,1,0:T(8,128)(2,1)} %refs_8_.7) | copy-start | bytes 25165828
  15.3 25.3 %collective-permute-start.14 = (bf16[2,32,32,256]{3,2,1,0:T(8,128)(2,1)S(1)}, bf16[2,32,32,256]{3,2,1,0:T(8,128)(2,1)S(1)}, u32[]{:S(2)}, u32[]{:S(2)}) collective-permute-start(bf16[2,32,32,256]{3,2,1,0:T(8,128)(2,1)S(1)} %get-tuple-element.20), channel_id=1, source_target_pairs={{0,5},{1,4},{2,7},{3,6},{4,1},{5,0},{6,3},{7,2},{8,13},{9,12},{10,... | collective-permute-start | bytes 3145736 | tf_op jit(solution)/shard_map/ppermute | solution.py:41
  16.5 24.8 %collective-permute-start.10 = (bf16[2,32,32,256]{3,2,1,0:T(8,128)(2,1)S(1)}, bf16[2,32,32,256]{3,2,1,0:T(8,128)(2,1)S(1)}, u32[]{:S(2)}, u32[]{:S(2)}) collective-permute-start(bf16[2,32,32,256]{3,2,1,0:T(8,128)(2,1)S(1)} %get-tuple-element.14.refs_9_), channel_id=1, source_target_pairs={{0,3},{1,2},{2,1},{3,0},{4,7},{5,6},{6,5},{7,4},{8,11},{9,10},{10,... | collective-permute-start | bytes 3145736 | tf_op jit(solution)/shard_map/ppermute | solution.py:41
  22.9 40.4 %collective-permute-start.13 = (bf16[2,32,8192]{2,1,0:T(8,128)(2,1)S(1)}, bf16[2,32,8192]{2,1,0:T(8,128)(2,1)S(1)}, u32[]{:S(2)}, u32[]{:S(2)}) collective-permute-start(bf16[2,32,8192]{2,1,0:T(8,128)(2,1)S(1)} %get-tuple-element.19), channel_id=1, source_target_pairs={{0,4},{1,5},{2,6},{3,7},{4,0},{5,1},{6,2},{7,3},{8,12},{9,13},{10,... | collective-permute-start | bytes 3145736 | tf_op jit(solution)/shard_map/ppermute | solution.py:41
  23.3 41.4 %slice-start = ((s8[8388608]{0:T(1024)(128)(4,1)}), s8[4194304]{0:T(1024)(128)(4,1)S(1)}, s32[]{:S(2)}) async-start(s8[8388608]{0:T(1024)(128)(4,1)} %bitcast.1), calls=%async_computation | async-start | bytes 8388608
  23.3 44.5 %collective-permute-start.9 = (bf16[2,32,8192]{2,1,0:T(8,128)(2,1)S(1)}, bf16[2,32,8192]{2,1,0:T(8,128)(2,1)S(1)}, u32[]{:S(2)}, u32[]{:S(2)}) collective-permute-start(bf16[2,32,8192]{2,1,0:T(8,128)(2,1)S(1)} %get-tuple-element.15.refs_9_), channel_id=1, source_target_pairs={{0,2},{1,3},{2,0},{3,1},{4,6},{5,7},{6,4},{7,5},{8,10},{9,11},{10,... | collective-permute-start | bytes 3145736 | tf_op jit(solution)/shard_map/ppermute | solution.py:41
  31.0 33.7 %slice-start.1 = ((s8[8388608]{0:T(1024)(128)(4,1)}), s8[4194304]{0:T(1024)(128)(4,1)S(1)}, s32[]{:S(2)}) async-start(s8[8388608]{0:T(1024)(128)(4,1)} %bitcast.1), calls=%async_computation.1 | async-start | bytes 8388608
  31.1 55.1 %collective-permute-start.18 = (bf16[2,32,8192]{2,1,0:T(8,128)(2,1)S(1)}, bf16[2,32,8192]{2,1,0:T(8,128)(2,1)S(1)}, u32[]{:S(2)}, u32[]{:S(2)}) collective-permute-start(bf16[2,32,8192]{2,1,0:T(8,128)(2,1)S(1)} %get-tuple-element.16.refs_9_), channel_id=1, source_target_pairs={{0,7},{1,6},{2,5},{3,4},{4,3},{5,2},{6,1},{7,0},{8,15},{9,14},{10,... | collective-permute-start | bytes 3145736 | tf_op jit(solution)/shard_map/ppermute | solution.py:41
  40.6 48.2 %collective-permute-start.7 = (bf16[2,32,8192]{2,1,0:T(8,128)(2,1)S(1)}, bf16[2,32,8192]{2,1,0:T(8,128)(2,1)S(1)}, u32[]{:S(2)}, u32[]{:S(2)}) collective-permute-start(bf16[2,32,8192]{2,1,0:T(8,128)(2,1)S(1)} %get-tuple-element.18), channel_id=1, source_target_pairs={{0,1},{1,0},{2,3},{3,2},{4,5},{5,4},{6,7},{7,6},{8,9},{9,8},{10,11... | collective-permute-start | bytes 3145736 | tf_op jit(solution)/shard_map/ppermute | solution.py:41
  41.3 57.5 %collective-permute-start.17 = (bf16[1,32,8192]{2,1,0:T(8,128)(2,1)S(1)}, bf16[1,32,8192]{2,1,0:T(8,128)(2,1)S(1)}, u32[]{:S(2)}, u32[]{:S(2)}) collective-permute-start(bf16[1,32,8192]{2,1,0:T(8,128)(2,1)S(1)} %get-tuple-element.21), channel_id=1, source_target_pairs={{0,6},{1,7},{2,4},{3,5},{4,2},{5,3},{6,0},{7,1},{8,14},{9,15},{10,... | collective-permute-start | bytes 1572872 | tf_op jit(solution)/shard_map/ppermute | solution.py:41
  63.3 46.7 %collective-permute-start.21 = (bf16[1,32,8192]{2,1,0:T(8,128)(2,1)S(1)}, bf16[1,32,8192]{2,1,0:T(8,128)(2,1)S(1)}, u32[]{:S(2)}, u32[]{:S(2)}) collective-permute-start(bf16[1,32,8192]{2,1,0:T(8,128)(2,1)S(1)} %get-tuple-element.22), channel_id=1, source_target_pairs={{0,6},{1,7},{2,4},{3,5},{4,2},{5,3},{6,0},{7,1},{8,14},{9,15},{10,... | collective-permute-start | bytes 1572872 | tf_op jit(solution)/shard_map/ppermute | solution.py:41
  67.8 22.6 %collective-permute-start.15 = (f32[2,32,256]{2,1,0:T(8,128)S(1)}, f32[2,32,256]{2,1,0:T(8,128)S(1)}, u32[]{:S(2)}, u32[]{:S(2)}) collective-permute-start(f32[2,32,256]{2,1,0:T(8,128)S(1)} %last.13), channel_id=1, source_target_pairs={{0,1},{1,0},{2,3},{3,2},{4,5},{5,4},{6,7},{7,6},{8,9},{9,8},{10,11... | collective-permute-start | bytes 196616 | tf_op jit(solution)/shard_map/ppermute | solution.py:41
  86.2 6.4 %collective-permute-start.11 = (f32[2,32,256]{2,1,0:T(8,128)S(1)}, f32[2,32,256]{2,1,0:T(8,128)S(1)}, u32[]{:S(2)}, u32[]{:S(2)}) collective-permute-start(f32[2,32,256]{2,1,0:T(8,128)S(1)} %last.11), channel_id=1, source_target_pairs={{0,1},{1,0},{2,3},{3,2},{4,5},{5,4},{6,7},{7,6},{8,9},{9,8},{10,11... | collective-permute-start | bytes 196616 | tf_op jit(solution)/shard_map/ppermute | solution.py:41
  88.8 10.4 %collective-permute-start.19 = (f32[2,32,256]{2,1,0:T(8,128)S(1)}, f32[2,32,256]{2,1,0:T(8,128)S(1)}, u32[]{:S(2)}, u32[]{:S(2)}) collective-permute-start(f32[2,32,256]{2,1,0:T(8,128)S(1)} %last.15), channel_id=1, source_target_pairs={{0,1},{1,0},{2,3},{3,2},{4,5},{5,4},{6,7},{7,6},{8,9},{9,8},{10,11... | collective-permute-start | bytes 196616 | tf_op jit(solution)/shard_map/ppermute | solution.py:41
  90.4 21.9 %collective-permute-start.8 = (f32[2,32,256]{2,1,0:T(8,128)S(1)}, f32[2,32,256]{2,1,0:T(8,128)S(1)}, u32[]{:S(2)}, u32[]{:S(2)}) collective-permute-start(f32[2,32,256]{2,1,0:T(8,128)S(1)} %last.9), channel_id=1, source_target_pairs={{0,1},{1,0},{2,3},{3,2},{4,5},{5,4},{6,7},{7,6},{8,9},{9,8},{10,11... | collective-permute-start | bytes 196616 | tf_op jit(solution)/shard_map/ppermute | solution.py:41
  92.5 23.1 %collective-permute-start.16 = (f32[2,32,256]{2,1,0:T(8,128)S(1)}, f32[2,32,256]{2,1,0:T(8,128)S(1)}, u32[]{:S(2)}, u32[]{:S(2)}) collective-permute-start(f32[2,32,256]{2,1,0:T(8,128)S(1)} %last.14), channel_id=1, source_target_pairs={{0,4},{1,5},{2,6},{3,7},{4,0},{5,1},{6,2},{7,3},{8,12},{9,13},{10,... | collective-permute-start | bytes 196616 | tf_op jit(solution)/shard_map/ppermute | solution.py:41
  98.8 16.9 %collective-permute-start.12 = (f32[2,32,256]{2,1,0:T(8,128)S(1)}, f32[2,32,256]{2,1,0:T(8,128)S(1)}, u32[]{:S(2)}, u32[]{:S(2)}) collective-permute-start(f32[2,32,256]{2,1,0:T(8,128)S(1)} %last.12), channel_id=1, source_target_pairs={{0,2},{1,3},{2,0},{3,1},{4,6},{5,7},{6,4},{7,5},{8,10},{9,11},{10,... | collective-permute-start | bytes 196616 | tf_op jit(solution)/shard_map/ppermute | solution.py:41
  100.1 13.8 %collective-permute-start.20 = (f32[1,32,256]{2,1,0:T(8,128)S(1)}, f32[1,32,256]{2,1,0:T(8,128)S(1)}, u32[]{:S(2)}, u32[]{:S(2)}) collective-permute-start(f32[1,32,256]{2,1,0:T(8,128)S(1)} %last.16), channel_id=1, source_target_pairs={{0,6},{1,7},{2,4},{3,5},{4,2},{5,3},{6,0},{7,1},{8,14},{9,15},{10,... | collective-permute-start | bytes 98312 | tf_op jit(solution)/shard_map/ppermute | solution.py:41
  110.8 4.9 %collective-permute-start.22 = (f32[1,32,256]{2,1,0:T(8,128)S(1)}, f32[1,32,256]{2,1,0:T(8,128)S(1)}, u32[]{:S(2)}, u32[]{:S(2)}) collective-permute-start(f32[1,32,256]{2,1,0:T(8,128)S(1)} %last.17), channel_id=1, source_target_pairs={{0,6},{1,7},{2,4},{3,5},{4,2},{5,3},{6,0},{7,1},{8,14},{9,15},{10,... | collective-permute-start | bytes 98312 | tf_op jit(solution)/shard_map/ppermute | solution.py:41

commit v6 on v5

--- a/solution.py
+++ b/solution.py
@@ -114,7 +114,7 @@
     n = len(pieces)
     parents, mine, left, right = core_x.shape
     rows = left // n
-    step = min(8, mine)
+    step = 16 if mine % 16 == 0 else min(8, mine)
     return pl.pallas_call(
         functools.partial(first_kernel, n, masks),
         grid=(parents, mine // step),

time: 116 us -> 116 us (level)
  no operation moved by 1% of the time
where the time goes in v6:
time: 116 us
  waiting for transfers between devices  56.7 us (49%)
  Pallas kernels  38.4 us (33%)
  starting transfers between devices  20.3 us (18%)
    ppermute x23, waiting for transfers between devices, swap(): return lax.ppermute(value, AXIS, [(i, i ^ mask) for i in range(n)])  56.7 us
    ppermute x23, starting transfers between devices, swap(): return lax.ppermute(value, AXIS, [(i, i ^ mask) for i in range(n)])  20.3 us
    pallas_call x3, Pallas kernels, second_for(): pl.pallas_call(functools.partial(second_kernel, n, masks), grid=(parents,...  17.8 us
    pallas_call x9, Pallas kernels, last_for(): pl.pallas_call(functools.partial(last_kernel, parents, begin is not None,...  15.4 us
    pallas_call x1, Pallas kernels, first_for(): pl.pallas_call(functools.partial(first_kernel, n, masks), grid=(parents,...  4.5 us
  transfers between devices with their start and end apart: 23, of which 12 were waited for; matrix products, arithmetic and copies ran while one was open for 0% of the time, Pallas kernels for 29%

profile of v6, /device:TPU:0, one launch (start us, length us, event | category | flops | bytes accessed | tf_op | source)
XLA Modules:
  0.0 116.2 jit_solution(4143176708113456926)
XLA Ops:
  0.0 0.8 pad_add_fusion.refs_0_
  0.8 3.9 %collective-permute-start.5 = (bf16[2,64,256]{2,1,0:T(8,128)(2,1)S(1)}, bf16[2,64,256]{2,1,0:T(8,128)(2,1)S(1)}, u32[]{:S(2)}, u32[]{:S(2)}) collective-permute-start(bf16[2,64,256]{2,1,0:T(8,128)(2,1)S(1)} %pad_add_fusion.refs_0_), channel_id=1, source_target_pairs={{0,6},{1,7},{2,4},{3,5},{4,2},{5,3},{6,0},{7,1},{8,14},{9,15},{10,... | collective-permute-start | bytes 196616 | tf_op jit(solution)/shard_map/ppermute | solution.py:41
  4.7 0.5 collective-permute-start.3
  5.2 0.1 collective-permute-start.1
  5.3 1.6 %collective-permute-done.5.refs_6_ = bf16[2,64,256]{2,1,0:T(8,128)(2,1)S(1)} collective-permute-done((bf16[2,64,256]{2,1,0:T(8,128)(2,1)S(1)}, bf16[2,64,256]{2,1,0:T(8,128)(2,1)S(1)}, u32[]{:S(2)}, u32[]{:S(2)}) %collective-permute-start.5) | collective-permute-done | bytes 65568 | tf_op jit(solution)/shard_map/ppermute | solution.py:41
  6.9 2.0 %collective-permute-done.3.refs_4_ = bf16[2,64,256]{2,1,0:T(8,128)(2,1)S(1)} collective-permute-done((bf16[2,64,256]{2,1,0:T(8,128)(2,1)S(1)}, bf16[2,64,256]{2,1,0:T(8,128)(2,1)S(1)}, u32[]{:S(2)}, u32[]{:S(2)}) %collective-permute-start.3) | collective-permute-done | bytes 65568 | tf_op jit(solution)/shard_map/ppermute | solution.py:41
  8.9 0.5 collective-permute-done.1.refs_2_
  9.5 0.7 collective-permute-done.4.refs_5_
  10.2 0.5 collective-permute-done.2.refs_3_
  10.7 4.5 %first.1 = (bf16[2,32,32,256]{3,2,1,0:T(8,128)(2,1)S(1)}, bf16[2,32,32,256]{3,2,1,0:T(8,128)(2,1)S(1)}) custom-call(s32[1]{0:T(128)} %bitcast.me_ref, bf16[2,64,256]{2,1,0:T(8,128)(2,1)S(1)} %pad_add_fusion.refs_0_, bf16[2,64,256]{2,1,0:T(8,128)(2,1)S(1)} %collective-permute-done.refs_1_, bf16[2,64,256]{2,1,0:T(8,128)(2,1)S(1)} %collective-permute-done.1.refs_2_, ...), custom_call_target="tpu_custom_call" | custom-call | flops 536870912 | bytes 10485760 | tf_op jit(solution)/shard_map/first/pallas_call | solution.py:118
  15.2 1.2 %collective-permute-start.14 = (bf16[2,32,32,256]{3,2,1,0:T(8,128)(2,1)S(1)}, bf16[2,32,32,256]{3,2,1,0:T(8,128)(2,1)S(1)}, u32[]{:S(2)}, u32[]{:S(2)}) collective-permute-start(bf16[2,32,32,256]{3,2,1,0:T(8,128)(2,1)S(1)} %get-tuple-element.20), channel_id=1, source_target_pairs={{0,5},{1,4},{2,7},{3,6},{4,1},{5,0},{6,3},{7,2},{8,13},{9,12},{10,... | collective-permute-start | bytes 3145736 | tf_op jit(solution)/shard_map/ppermute | solution.py:41
  16.4 0.6 collective-permute-start.10
  17.1 5.8 %second.3 = (bf16[2,32,8192]{2,1,0:T(8,128)(2,1)S(1)}, bf16[2,32,8192]{2,1,0:T(8,128)(2,1)S(1)}) custom-call(s32[1]{0:T(128)} %bitcast.me_ref, bf16[2,64,256]{2,1,0:T(8,128)(2,1)S(1)} %pad_add_fusion.refs_0_, bf16[2,64,256]{2,1,0:T(8,128)(2,1)S(1)} %collective-permute-done.refs_1_, bf16[2,64,256]{2,1,0:T(8,128)(2,1)S(1)} %collective-permute-done.1.refs_2_, ...), custom_call_target="tpu_custom_call" | custom-call | flops 1073741824 | bytes 10485760 | tf_op jit(solution)/shard_map/second/pallas_call | solution.py:172
  22.8 0.5 collective-permute-start.13
  23.3 1.6 %collective-permute-start.9 = (bf16[2,32,8192]{2,1,0:T(8,128)(2,1)S(1)}, bf16[2,32,8192]{2,1,0:T(8,128)(2,1)S(1)}, u32[]{:S(2)}, u32[]{:S(2)}) collective-permute-start(bf16[2,32,8192]{2,1,0:T(8,128)(2,1)S(1)} %get-tuple-element.15.refs_9_), channel_id=1, source_target_pairs={{0,2},{1,3},{2,0},{3,1},{4,6},{5,7},{6,4},{7,5},{8,10},{9,11},{10,... | collective-permute-start | bytes 3145736 | tf_op jit(solution)/shard_map/ppermute | solution.py:41
  24.9 6.1 %second.4 = (bf16[2,32,8192]{2,1,0:T(8,128)(2,1)S(1)}, bf16[1,32,8192]{2,1,0:T(8,128)(2,1)S(1)}, bf16[1,32,8192]{2,1,0:T(8,128)(2,1)S(1)}) custom-call(s32[1]{0:T(128)} %bitcast.me_ref, bf16[2,64,256]{2,1,0:T(8,128)(2,1)S(1)} %pad_add_fusion.refs_0_, bf16[2,64,256]{2,1,0:T(8,128)(2,1)S(1)} %collective-permute-done.refs_1_, ...), custom_call_target="tpu_custom_call" | custom-call | flops 1073741824 | bytes 10485760 | tf_op jit(solution)/shard_map/second/pallas_call | solution.py:172
  31.0 0.6 collective-permute-start.18
  31.6 5.9 %second.5 = (bf16[2,32,8192]{2,1,0:T(8,128)(2,1)S(1)}, bf16[2,32,8192]{2,1,0:T(8,128)(2,1)S(1)}) custom-call(s32[1]{0:T(128)} %bitcast.me_ref, bf16[2,64,256]{2,1,0:T(8,128)(2,1)S(1)} %pad_add_fusion.refs_0_, bf16[2,64,256]{2,1,0:T(8,128)(2,1)S(1)} %collective-permute-done.refs_1_, bf16[2,64,256]{2,1,0:T(8,128)(2,1)S(1)} %collective-permute-done.1.refs_2_, ...), custom_call_target="tpu_custom_call" | custom-call | flops 1073741824 | bytes 10485760 | tf_op jit(solution)/shard_map/second/pallas_call | solution.py:172
  37.6 3.0 %collective-permute-done.14.refs_0_ = bf16[2,32,32,256]{3,2,1,0:T(8,128)(2,1)S(1)} collective-permute-done((bf16[2,32,32,256]{3,2,1,0:T(8,128)(2,1)S(1)}, bf16[2,32,32,256]{3,2,1,0:T(8,128)(2,1)S(1)}, u32[]{:S(2)}, u32[]{:S(2)}) %collective-permute-start.14) | collective-permute-done | bytes 1048608 | tf_op jit(solution)/shard_map/ppermute | solution.py:41
  40.5 0.5 collective-permute-start.7
  41.0 0.2 collective-permute-done.10.refs_0_
  41.2 1.3 %collective-permute-start.17 = (bf16[1,32,8192]{2,1,0:T(8,128)(2,1)S(1)}, bf16[1,32,8192]{2,1,0:T(8,128)(2,1)S(1)}, u32[]{:S(2)}, u32[]{:S(2)}) collective-permute-start(bf16[1,32,8192]{2,1,0:T(8,128)(2,1)S(1)} %get-tuple-element.21), channel_id=1, source_target_pairs={{0,6},{1,7},{2,4},{3,5},{4,2},{5,3},{6,0},{7,1},{8,14},{9,15},{10,... | collective-permute-start | bytes 1572872 | tf_op jit(solution)/shard_map/ppermute | solution.py:41
  42.5 20.7 %collective-permute-done.13.refs_0_ = bf16[2,32,8192]{2,1,0:T(8,128)(2,1)S(1)} collective-permute-done((bf16[2,32,8192]{2,1,0:T(8,128)(2,1)S(1)}, bf16[2,32,8192]{2,1,0:T(8,128)(2,1)S(1)}, u32[]{:S(2)}, u32[]{:S(2)}) %collective-permute-start.13) | collective-permute-done | bytes 1048608 | tf_op jit(solution)/shard_map/ppermute | solution.py:41
  63.2 1.5 %collective-permute-start.21 = (bf16[1,32,8192]{2,1,0:T(8,128)(2,1)S(1)}, bf16[1,32,8192]{2,1,0:T(8,128)(2,1)S(1)}, u32[]{:S(2)}, u32[]{:S(2)}) collective-permute-start(bf16[1,32,8192]{2,1,0:T(8,128)(2,1)S(1)} %get-tuple-element.22), channel_id=1, source_target_pairs={{0,6},{1,7},{2,4},{3,5},{4,2},{5,3},{6,0},{7,1},{8,14},{9,15},{10,... | collective-permute-start | bytes 1572872 | tf_op jit(solution)/shard_map/ppermute | solution.py:41
  64.7 3.0 %last.13 = f32[2,32,256]{2,1,0:T(8,128)S(1)} custom-call(bf16[2,32,32,256]{3,2,1,0:T(8,128)(2,1)S(1)} %collective-permute-done.14.refs_0_, bf16[2,32,256,256]{3,2,1,0:T(8,128)(2,1)S(1)} %bitcast.2, bf16[2,256,256]{2,1,0:T(8,128)(2,1)S(1)} %join.1.refs_2_), custom_call_target="tpu_custom_call" | custom-call | flops 536870912 | bytes 9437184 | tf_op jit(solution)/shard_map/last/pallas_call | solution.py:252
  67.8 0.1 collective-permute-start.15
  67.9 3.0 %last.11 = f32[2,32,256]{2,1,0:T(8,128)S(1)} custom-call(bf16[2,32,32,256]{3,2,1,0:T(8,128)(2,1)S(1)} %collective-permute-done.10.refs_0_, bf16[2,32,256,256]{3,2,1,0:T(8,128)(2,1)S(1)} %bitcast.2, bf16[2,256,256]{2,1,0:T(8,128)(2,1)S(1)} %join.1.refs_2_), custom_call_target="tpu_custom_call" | custom-call | flops 536870912 | bytes 9437184 | tf_op jit(solution)/shard_map/last/pallas_call | solution.py:252
  70.9 15.2 %collective-permute-done.18.refs_0_ = bf16[2,32,8192]{2,1,0:T(8,128)(2,1)S(1)} collective-permute-done((bf16[2,32,8192]{2,1,0:T(8,128)(2,1)S(1)}, bf16[2,32,8192]{2,1,0:T(8,128)(2,1)S(1)}, u32[]{:S(2)}, u32[]{:S(2)}) %collective-permute-start.18) | collective-permute-done | bytes 1048608 | tf_op jit(solution)/shard_map/ppermute | solution.py:41
  86.1 1.1 collective-permute-start.11
  87.2 1.5 %last.15 = f32[2,32,256]{2,1,0:T(8,128)S(1)} custom-call(bf16[2,32,8192]{2,1,0:T(8,128)(2,1)S(1)} %collective-permute-done.18.refs_0_, bf16[2,32,256,256]{3,2,1,0:T(8,128)(2,1)S(1)} %bitcast.2), custom_call_target="tpu_custom_call" | custom-call | flops 268435456 | bytes 9437184 | tf_op jit(solution)/shard_map/last/pallas_call | solution.py:252
  88.7 0.1 collective-permute-start.19
  88.8 1.5 %last.9 = f32[2,32,256]{2,1,0:T(8,128)S(1)} custom-call(bf16[2,32,8192]{2,1,0:T(8,128)(2,1)S(1)} %collective-permute-done.7.refs_0_, bf16[2,32,256,256]{3,2,1,0:T(8,128)(2,1)S(1)} %bitcast.2), custom_call_target="tpu_custom_call" | custom-call | flops 268435456 | bytes 9437184 | tf_op jit(solution)/shard_map/last/pallas_call | solution.py:252
  90.4 0.6 collective-permute-start.8
  90.9 1.5 %last.14 = f32[2,32,256]{2,1,0:T(8,128)S(1)} custom-call(bf16[2,32,8192]{2,1,0:T(8,128)(2,1)S(1)} %collective-permute-done.13.refs_0_, bf16[2,32,256,256]{3,2,1,0:T(8,128)(2,1)S(1)} %bitcast.2, f32[2,32,256]{2,1,0:T(8,128)S(1)} %collective-permute-done.15.refs_2_), custom_call_target="tpu_custom_call" | custom-call | flops 268435456 | bytes 9437184 | tf_op jit(solution)/shard_map/last/pallas_call | solution.py:252
  92.5 0.0 collective-permute-done.11.refs_2_
  92.5 1.6 %collective-permute-start.16 = (f32[2,32,256]{2,1,0:T(8,128)S(1)}, f32[2,32,256]{2,1,0:T(8,128)S(1)}, u32[]{:S(2)}, u32[]{:S(2)}) collective-permute-start(f32[2,32,256]{2,1,0:T(8,128)S(1)} %last.14), channel_id=1, source_target_pairs={{0,4},{1,5},{2,6},{3,7},{4,0},{5,1},{6,2},{7,3},{8,12},{9,13},{10,... | collective-permute-start | bytes 196616 | tf_op jit(solution)/shard_map/ppermute | solution.py:41
  94.1 1.5 %last.12 = f32[2,32,256]{2,1,0:T(8,128)S(1)} custom-call(bf16[2,32,8192]{2,1,0:T(8,128)(2,1)S(1)} %collective-permute-done.9.refs_0_, bf16[2,32,256,256]{3,2,1,0:T(8,128)(2,1)S(1)} %bitcast.2, f32[2,32,256]{2,1,0:T(8,128)S(1)} %collective-permute-done.11.refs_2_), custom_call_target="tpu_custom_call" | custom-call | flops 268435456 | bytes 9437184 | tf_op jit(solution)/shard_map/last/pallas_call | solution.py:252
  95.6 3.1 %collective-permute-done.17.refs_0_ = bf16[1,32,8192]{2,1,0:T(8,128)(2,1)S(1)} collective-permute-done((bf16[1,32,8192]{2,1,0:T(8,128)(2,1)S(1)}, bf16[1,32,8192]{2,1,0:T(8,128)(2,1)S(1)}, u32[]{:S(2)}, u32[]{:S(2)}) %collective-permute-start.17) | collective-permute-done | bytes 524320 | tf_op jit(solution)/shard_map/ppermute | solution.py:41
  98.7 0.5 collective-permute-start.12
  99.2 0.8 last.16
  100.0 2.6 %collective-permute-start.20 = (f32[1,32,256]{2,1,0:T(8,128)S(1)}, f32[1,32,256]{2,1,0:T(8,128)S(1)}, u32[]{:S(2)}, u32[]{:S(2)}) collective-permute-start(f32[1,32,256]{2,1,0:T(8,128)S(1)} %last.16), channel_id=1, source_target_pairs={{0,6},{1,7},{2,4},{3,5},{4,2},{5,3},{6,0},{7,1},{8,14},{9,15},{10,... | collective-permute-start | bytes 98312 | tf_op jit(solution)/shard_map/ppermute | solution.py:41
  102.6 7.3 %collective-permute-done.21.refs_0_ = bf16[1,32,8192]{2,1,0:T(8,128)(2,1)S(1)} collective-permute-done((bf16[1,32,8192]{2,1,0:T(8,128)(2,1)S(1)}, bf16[1,32,8192]{2,1,0:T(8,128)(2,1)S(1)}, u32[]{:S(2)}, u32[]{:S(2)}) %collective-permute-start.21) | collective-permute-done | bytes 524320 | tf_op jit(solution)/shard_map/ppermute | solution.py:41
  109.9 0.8 last.17
  110.7 1.5 %collective-permute-start.22 = (f32[1,32,256]{2,1,0:T(8,128)S(1)}, f32[1,32,256]{2,1,0:T(8,128)S(1)}, u32[]{:S(2)}, u32[]{:S(2)}) collective-permute-start(f32[1,32,256]{2,1,0:T(8,128)S(1)} %last.17), channel_id=1, source_target_pairs={{0,6},{1,7},{2,4},{3,5},{4,2},{5,3},{6,0},{7,1},{8,14},{9,15},{10,... | collective-permute-start | bytes 98312 | tf_op jit(solution)/shard_map/ppermute | solution.py:41
  112.3 1.5 %last.10.refs_0_ = f32[2,32,256]{2,1,0:T(8,128)S(1)} custom-call(bf16[2,32,8192]{2,1,0:T(8,128)(2,1)S(1)} %get-tuple-element.17.refs_0_, bf16[2,32,256,256]{3,2,1,0:T(8,128)(2,1)S(1)} %bitcast.2, f32[2,32,256]{2,1,0:T(8,128)S(1)} %collective-permute-done.8.refs_2_), custom_call_target="tpu_custom_call" | custom-call | flops 268435456 | bytes 9437184 | tf_op jit(solution)/shard_map/last/pallas_call | solution.py:252
  113.8 0.0 collective-permute-done.20.refs_3_
  113.8 1.8 %collective-permute-done.22.refs_4_ = f32[1,32,256]{2,1,0:T(8,128)S(1)} collective-permute-done((f32[1,32,256]{2,1,0:T(8,128)S(1)}, f32[1,32,256]{2,1,0:T(8,128)S(1)}, u32[]{:S(2)}, u32[]{:S(2)}) %collective-permute-start.22) | collective-permute-done | bytes 32800 | tf_op jit(solution)/shard_map/ppermute | solution.py:41
  115.6 0.6 sum.1
  (21 shorter events, 0.1 us)
Async XLA Ops:
  0.8 6.1 %collective-permute-start.5 = (bf16[2,64,256]{2,1,0:T(8,128)(2,1)S(1)}, bf16[2,64,256]{2,1,0:T(8,128)(2,1)S(1)}, u32[]{:S(2)}, u32[]{:S(2)}) collective-permute-start(bf16[2,64,256]{2,1,0:T(8,128)(2,1)S(1)} %pad_add_fusion.refs_0_), channel_id=1, source_target_pairs={{0,6},{1,7},{2,4},{3,5},{4,2},{5,3},{6,0},{7,1},{8,14},{9,15},{10,... | collective-permute-start | bytes 196616 | tf_op jit(solution)/shard_map/ppermute | solution.py:41
  4.7 4.3 %collective-permute-start.3 = (bf16[2,64,256]{2,1,0:T(8,128)(2,1)S(1)}, bf16[2,64,256]{2,1,0:T(8,128)(2,1)S(1)}, u32[]{:S(2)}, u32[]{:S(2)}) collective-permute-start(bf16[2,64,256]{2,1,0:T(8,128)(2,1)S(1)} %pad_add_fusion.refs_0_), channel_id=1, source_target_pairs={{0,4},{1,5},{2,6},{3,7},{4,0},{5,1},{6,2},{7,3},{8,12},{9,13},{10,... | collective-permute-start | bytes 196616 | tf_op jit(solution)/shard_map/ppermute | solution.py:41
  5.2 4.3 %collective-permute-start.1 = (bf16[2,64,256]{2,1,0:T(8,128)(2,1)S(1)}, bf16[2,64,256]{2,1,0:T(8,128)(2,1)S(1)}, u32[]{:S(2)}, u32[]{:S(2)}) collective-permute-start(bf16[2,64,256]{2,1,0:T(8,128)(2,1)S(1)} %pad_add_fusion.refs_0_), channel_id=1, source_target_pairs={{0,2},{1,3},{2,0},{3,1},{4,6},{5,7},{6,4},{7,5},{8,10},{9,11},{10,... | collective-permute-start | bytes 196616 | tf_op jit(solution)/shard_map/ppermute | solution.py:41
  5.3 4.2 %collective-permute-start = (bf16[2,64,256]{2,1,0:T(8,128)(2,1)S(1)}, bf16[2,64,256]{2,1,0:T(8,128)(2,1)S(1)}, u32[]{:S(2)}, u32[]{:S(2)}) collective-permute-start(bf16[2,64,256]{2,1,0:T(8,128)(2,1)S(1)} %pad_add_fusion.refs_0_), channel_id=1, source_target_pairs={{0,1},{1,0},{2,3},{3,2},{4,5},{5,4},{6,7},{7,6},{8,9},{9,8},{10,11... | collective-permute-start | bytes 196616 | tf_op jit(solution)/shard_map/ppermute | solution.py:41
  6.9 2.5 %collective-permute-start.6 = (bf16[2,64,256]{2,1,0:T(8,128)(2,1)S(1)}, bf16[2,64,256]{2,1,0:T(8,128)(2,1)S(1)}, u32[]{:S(2)}, u32[]{:S(2)}) collective-permute-start(bf16[2,64,256]{2,1,0:T(8,128)(2,1)S(1)} %collective-permute-done.5.refs_6_), channel_id=1, source_target_pairs={{0,1},{1,0},{2,3},{3,2},{4,5},{5,4},{6,7},{7,6},{8,9},{9,8},{10,11... | collective-permute-start | bytes 196616 | tf_op jit(solution)/shard_map/ppermute | solution.py:41
  8.9 1.3 %collective-permute-start.4 = (bf16[2,64,256]{2,1,0:T(8,128)(2,1)S(1)}, bf16[2,64,256]{2,1,0:T(8,128)(2,1)S(1)}, u32[]{:S(2)}, u32[]{:S(2)}) collective-permute-start(bf16[2,64,256]{2,1,0:T(8,128)(2,1)S(1)} %collective-permute-done.3.refs_4_), channel_id=1, source_target_pairs={{0,1},{1,0},{2,3},{3,2},{4,5},{5,4},{6,7},{7,6},{8,9},{9,8},{10,11... | collective-permute-start | bytes 196616 | tf_op jit(solution)/shard_map/ppermute | solution.py:41
  9.4 1.3 %collective-permute-start.2 = (bf16[2,64,256]{2,1,0:T(8,128)(2,1)S(1)}, bf16[2,64,256]{2,1,0:T(8,128)(2,1)S(1)}, u32[]{:S(2)}, u32[]{:S(2)}) collective-permute-start(bf16[2,64,256]{2,1,0:T(8,128)(2,1)S(1)} %collective-permute-done.1.refs_2_), channel_id=1, source_target_pairs={{0,1},{1,0},{2,3},{3,2},{4,5},{5,4},{6,7},{7,6},{8,9},{9,8},{10,11... | collective-permute-start | bytes 196616 | tf_op jit(solution)/shard_map/ppermute | solution.py:41
  9.5 7.6 %copy-start = (bf16[2,32,256,256]{3,2,1,0:T(8,128)(2,1)S(1)}, bf16[2,32,256,256]{3,2,1,0:T(8,128)(2,1)}, u32[]{:S(2)}) copy-start(bf16[2,32,256,256]{3,2,1,0:T(8,128)(2,1)} %refs_8_.7) | copy-start | bytes 25165828
  15.2 25.3 %collective-permute-start.14 = (bf16[2,32,32,256]{3,2,1,0:T(8,128)(2,1)S(1)}, bf16[2,32,32,256]{3,2,1,0:T(8,128)(2,1)S(1)}, u32[]{:S(2)}, u32[]{:S(2)}) collective-permute-start(bf16[2,32,32,256]{3,2,1,0:T(8,128)(2,1)S(1)} %get-tuple-element.20), channel_id=1, source_target_pairs={{0,5},{1,4},{2,7},{3,6},{4,1},{5,0},{6,3},{7,2},{8,13},{9,12},{10,... | collective-permute-start | bytes 3145736 | tf_op jit(solution)/shard_map/ppermute | solution.py:41
  16.4 24.8 %collective-permute-start.10 = (bf16[2,32,32,256]{3,2,1,0:T(8,128)(2,1)S(1)}, bf16[2,32,32,256]{3,2,1,0:T(8,128)(2,1)S(1)}, u32[]{:S(2)}, u32[]{:S(2)}) collective-permute-start(bf16[2,32,32,256]{3,2,1,0:T(8,128)(2,1)S(1)} %get-tuple-element.14.refs_9_), channel_id=1, source_target_pairs={{0,3},{1,2},{2,1},{3,0},{4,7},{5,6},{6,5},{7,4},{8,11},{9,10},{10,... | collective-permute-start | bytes 3145736 | tf_op jit(solution)/shard_map/ppermute | solution.py:41
  22.8 40.4 %collective-permute-start.13 = (bf16[2,32,8192]{2,1,0:T(8,128)(2,1)S(1)}, bf16[2,32,8192]{2,1,0:T(8,128)(2,1)S(1)}, u32[]{:S(2)}, u32[]{:S(2)}) collective-permute-start(bf16[2,32,8192]{2,1,0:T(8,128)(2,1)S(1)} %get-tuple-element.19), channel_id=1, source_target_pairs={{0,4},{1,5},{2,6},{3,7},{4,0},{5,1},{6,2},{7,3},{8,12},{9,13},{10,... | collective-permute-start | bytes 3145736 | tf_op jit(solution)/shard_map/ppermute | solution.py:41
  23.3 41.4 %slice-start = ((s8[8388608]{0:T(1024)(128)(4,1)}), s8[4194304]{0:T(1024)(128)(4,1)S(1)}, s32[]{:S(2)}) async-start(s8[8388608]{0:T(1024)(128)(4,1)} %bitcast.1), calls=%async_computation | async-start | bytes 8388608
  23.3 44.5 %collective-permute-start.9 = (bf16[2,32,8192]{2,1,0:T(8,128)(2,1)S(1)}, bf16[2,32,8192]{2,1,0:T(8,128)(2,1)S(1)}, u32[]{:S(2)}, u32[]{:S(2)}) collective-permute-start(bf16[2,32,8192]{2,1,0:T(8,128)(2,1)S(1)} %get-tuple-element.15.refs_9_), channel_id=1, source_target_pairs={{0,2},{1,3},{2,0},{3,1},{4,6},{5,7},{6,4},{7,5},{8,10},{9,11},{10,... | collective-permute-start | bytes 3145736 | tf_op jit(solution)/shard_map/ppermute | solution.py:41
  31.0 33.7 %slice-start.1 = ((s8[8388608]{0:T(1024)(128)(4,1)}), s8[4194304]{0:T(1024)(128)(4,1)S(1)}, s32[]{:S(2)}) async-start(s8[8388608]{0:T(1024)(128)(4,1)} %bitcast.1), calls=%async_computation.1 | async-start | bytes 8388608
  31.0 55.1 %collective-permute-start.18 = (bf16[2,32,8192]{2,1,0:T(8,128)(2,1)S(1)}, bf16[2,32,8192]{2,1,0:T(8,128)(2,1)S(1)}, u32[]{:S(2)}, u32[]{:S(2)}) collective-permute-start(bf16[2,32,8192]{2,1,0:T(8,128)(2,1)S(1)} %get-tuple-element.16.refs_9_), channel_id=1, source_target_pairs={{0,7},{1,6},{2,5},{3,4},{4,3},{5,2},{6,1},{7,0},{8,15},{9,14},{10,... | collective-permute-start | bytes 3145736 | tf_op jit(solution)/shard_map/ppermute | solution.py:41
  40.5 48.2 %collective-permute-start.7 = (bf16[2,32,8192]{2,1,0:T(8,128)(2,1)S(1)}, bf16[2,32,8192]{2,1,0:T(8,128)(2,1)S(1)}, u32[]{:S(2)}, u32[]{:S(2)}) collective-permute-start(bf16[2,32,8192]{2,1,0:T(8,128)(2,1)S(1)} %get-tuple-element.18), channel_id=1, source_target_pairs={{0,1},{1,0},{2,3},{3,2},{4,5},{5,4},{6,7},{7,6},{8,9},{9,8},{10,11... | collective-permute-start | bytes 3145736 | tf_op jit(solution)/shard_map/ppermute | solution.py:41
  41.2 57.5 %collective-permute-start.17 = (bf16[1,32,8192]{2,1,0:T(8,128)(2,1)S(1)}, bf16[1,32,8192]{2,1,0:T(8,128)(2,1)S(1)}, u32[]{:S(2)}, u32[]{:S(2)}) collective-permute-start(bf16[1,32,8192]{2,1,0:T(8,128)(2,1)S(1)} %get-tuple-element.21), channel_id=1, source_target_pairs={{0,6},{1,7},{2,4},{3,5},{4,2},{5,3},{6,0},{7,1},{8,14},{9,15},{10,... | collective-permute-start | bytes 1572872 | tf_op jit(solution)/shard_map/ppermute | solution.py:41
  63.2 46.7 %collective-permute-start.21 = (bf16[1,32,8192]{2,1,0:T(8,128)(2,1)S(1)}, bf16[1,32,8192]{2,1,0:T(8,128)(2,1)S(1)}, u32[]{:S(2)}, u32[]{:S(2)}) collective-permute-start(bf16[1,32,8192]{2,1,0:T(8,128)(2,1)S(1)} %get-tuple-element.22), channel_id=1, source_target_pairs={{0,6},{1,7},{2,4},{3,5},{4,2},{5,3},{6,0},{7,1},{8,14},{9,15},{10,... | collective-permute-start | bytes 1572872 | tf_op jit(solution)/shard_map/ppermute | solution.py:41
  67.8 22.6 %collective-permute-start.15 = (f32[2,32,256]{2,1,0:T(8,128)S(1)}, f32[2,32,256]{2,1,0:T(8,128)S(1)}, u32[]{:S(2)}, u32[]{:S(2)}) collective-permute-start(f32[2,32,256]{2,1,0:T(8,128)S(1)} %last.13), channel_id=1, source_target_pairs={{0,1},{1,0},{2,3},{3,2},{4,5},{5,4},{6,7},{7,6},{8,9},{9,8},{10,11... | collective-permute-start | bytes 196616 | tf_op jit(solution)/shard_map/ppermute | solution.py:41
  86.1 6.3 %collective-permute-start.11 = (f32[2,32,256]{2,1,0:T(8,128)S(1)}, f32[2,32,256]{2,1,0:T(8,128)S(1)}, u32[]{:S(2)}, u32[]{:S(2)}) collective-permute-start(f32[2,32,256]{2,1,0:T(8,128)S(1)} %last.11), channel_id=1, source_target_pairs={{0,1},{1,0},{2,3},{3,2},{4,5},{5,4},{6,7},{7,6},{8,9},{9,8},{10,11... | collective-permute-start | bytes 196616 | tf_op jit(solution)/shard_map/ppermute | solution.py:41
  88.7 10.4 %collective-permute-start.19 = (f32[2,32,256]{2,1,0:T(8,128)S(1)}, f32[2,32,256]{2,1,0:T(8,128)S(1)}, u32[]{:S(2)}, u32[]{:S(2)}) collective-permute-start(f32[2,32,256]{2,1,0:T(8,128)S(1)} %last.15), channel_id=1, source_target_pairs={{0,1},{1,0},{2,3},{3,2},{4,5},{5,4},{6,7},{7,6},{8,9},{9,8},{10,11... | collective-permute-start | bytes 196616 | tf_op jit(solution)/shard_map/ppermute | solution.py:41
  90.4 21.9 %collective-permute-start.8 = (f32[2,32,256]{2,1,0:T(8,128)S(1)}, f32[2,32,256]{2,1,0:T(8,128)S(1)}, u32[]{:S(2)}, u32[]{:S(2)}) collective-permute-start(f32[2,32,256]{2,1,0:T(8,128)S(1)} %last.9), channel_id=1, source_target_pairs={{0,1},{1,0},{2,3},{3,2},{4,5},{5,4},{6,7},{7,6},{8,9},{9,8},{10,11... | collective-permute-start | bytes 196616 | tf_op jit(solution)/shard_map/ppermute | solution.py:41
  92.5 23.1 %collective-permute-start.16 = (f32[2,32,256]{2,1,0:T(8,128)S(1)}, f32[2,32,256]{2,1,0:T(8,128)S(1)}, u32[]{:S(2)}, u32[]{:S(2)}) collective-permute-start(f32[2,32,256]{2,1,0:T(8,128)S(1)} %last.14), channel_id=1, source_target_pairs={{0,4},{1,5},{2,6},{3,7},{4,0},{5,1},{6,2},{7,3},{8,12},{9,13},{10,... | collective-permute-start | bytes 196616 | tf_op jit(solution)/shard_map/ppermute | solution.py:41
  98.7 16.9 %collective-permute-start.12 = (f32[2,32,256]{2,1,0:T(8,128)S(1)}, f32[2,32,256]{2,1,0:T(8,128)S(1)}, u32[]{:S(2)}, u32[]{:S(2)}) collective-permute-start(f32[2,32,256]{2,1,0:T(8,128)S(1)} %last.12), channel_id=1, source_target_pairs={{0,2},{1,3},{2,0},{3,1},{4,6},{5,7},{6,4},{7,5},{8,10},{9,11},{10,... | collective-permute-start | bytes 196616 | tf_op jit(solution)/shard_map/ppermute | solution.py:41
  100.0 13.8 %collective-permute-start.20 = (f32[1,32,256]{2,1,0:T(8,128)S(1)}, f32[1,32,256]{2,1,0:T(8,128)S(1)}, u32[]{:S(2)}, u32[]{:S(2)}) collective-permute-start(f32[1,32,256]{2,1,0:T(8,128)S(1)} %last.16), channel_id=1, source_target_pairs={{0,6},{1,7},{2,4},{3,5},{4,2},{5,3},{6,0},{7,1},{8,14},{9,15},{10,... | collective-permute-start | bytes 98312 | tf_op jit(solution)/shard_map/ppermute | solution.py:41
  110.7 4.9 %collective-permute-start.22 = (f32[1,32,256]{2,1,0:T(8,128)S(1)}, f32[1,32,256]{2,1,0:T(8,128)S(1)}, u32[]{:S(2)}, u32[]{:S(2)}) collective-permute-start(f32[1,32,256]{2,1,0:T(8,128)S(1)} %last.17), channel_id=1, source_target_pairs={{0,6},{1,7},{2,4},{3,5},{4,2},{5,3},{6,0},{7,1},{8,14},{9,15},{10,... | collective-permute-start | bytes 98312 | tf_op jit(solution)/shard_map/ppermute | solution.py:41
